TPU v7x, 32 devices: a whole 2x2x4 slice. The times are simulated.
32 devices in a mesh: groups: 2 (over y), seq: 4 (over z), head: 2 (over x), sub: 2 (over core).
Axes of the slice: x: 2, y: 2, z: 4, core: 2. Of those that a mesh axis runs over, the one named last changes fastest.
Arguments:
- tokens: int32 [3, 4096], P(None, ('groups', 'seq')), parts along dimension 1, may hold values from 0 to 1023
- masked: int32 [4096], P(('groups', 'seq')), parts along dimension 0, may hold values 0 or 1
- used_frames: int32 [2], P('groups'), parts along dimension 0, may hold values from 1024 to 2048
- tables: bfloat16 [3, 1024, 1024], P(None, None, ('head', 'sub')), may hold values from -6 to 6
- mask_vec: bfloat16 [1024], P(('head', 'sub')), may hold values from -6 to 6
- attn_in: bfloat16 [3, 1024, 512], P(None, None, ('head', 'sub')), may hold values from -0.1875 to 0.1875
- head_temp: float32 [8], P(('head', 'sub')), may hold values from 12 to 28
- attn_out: bfloat16 [512, 1024], P(('head', 'sub')), may hold values from -0.25 to 0.25
- conv_in: bfloat16 [2, 1024, 1024], P(None, None, ('head', 'sub')), may hold values from -0.1875 to 0.1875
- conv_kernel: float32 [31, 1024], P(None, ('head', 'sub')), may hold values from -1 to 1
- conv_out: bfloat16 [1024, 1024], P(('head', 'sub')), may hold values from -0.1875 to 0.1875
- voc_in: bfloat16 [1024, 512], P(('head', 'sub')), may hold values from -0.1875 to 0.1875
- voc_kernel: float32 [7, 512], replicated, may hold values from -2 to 2
- voc_up: bfloat16 [512, 1536], P(('head', 'sub')), may hold values from -0.25 to 0.25
- voc_down: bfloat16 [1536, 512], P(('head', 'sub')), may hold values from -0.15625 to 0.15625
- voc_head: bfloat16 [512, 1282], P(('head', 'sub')), may hold values from -0.25 to 0.25
- head_bias: float32 [1282], replicated, may hold values from 0.5 to 2.5
Outputs:
- features: bfloat16 [4096, 1024], P(('groups', 'seq', 'head', 'sub')), parts along dimension 0
- waveform: float32 [1310720], P(('groups', 'seq', 'head', 'sub')), parts along dimension 0
There are 2 independent parts, one for each index of `groups`. A program takes and returns all parts, laid end to end along the dimension named above; an argument that names none is the same for every part. Nothing has to cross between parts.
All inputs are finite; a program needn't handle non-finite values. No bound on the sum of `masked` on one device may be relied on, other than what follows from the above.
Results may differ from a plain program's by a relative error of at most 0.02.
Values may be sent and summed in bfloat16 or wider, within the bound.
No kernel may reach another device: no remote copies, remote signals or barrier semaphores. Data moves between devices by JAX's collectives and lax.ppermute only.
A program may use at most 64 MiB of HBM per device.

v0:
```python
import math

import jax
import jax.numpy as jnp
from jax import lax
from jax.sharding import PartitionSpec as P

HOP = 320


def with_halo(x, sides, width):
    for axis, dim in sides:
        size, length = (lax.axis_size(axis), x.shape[dim])
        up = [(i, (i + 1) % size) for i in range(size - 1)]
        down = [(j, i) for i, j in up]
        last = lax.slice_in_dim(x, length - width, length, axis=dim)
        initial = lax.slice_in_dim(x, 0, width, axis=dim)
        before = lax.ppermute(last, axis, up)
        after = lax.ppermute(initial, axis, down)
        x = jnp.concatenate([before, x, after], axis=dim)
    return x


def layer_norm(values):
    average = jnp.mean(values, axis=-1, keepdims=True)
    centered = values - average
    return centered * lax.rsqrt(jnp.mean(centered * centered, axis=-1, keepdims=True) + 1e-05)


def unit_heads(projected, head_count):
    row_count = projected.shape[0]
    split_heads = projected.reshape(row_count, head_count, projected.shape[1] // head_count)
    scaled = split_heads * lax.rsqrt(
        jnp.sum(split_heads * split_heads, axis=-1, keepdims=True) + 1e-06
    )
    return scaled.astype(jnp.bfloat16)


def depthwise(kernel, padded_rows):
    tap_count = kernel.shape[0]
    out_rows = padded_rows.shape[0] - tap_count + 1
    result = jnp.zeros((out_rows, padded_rows.shape[1]), jnp.float32)
    for offset in range(tap_count):
        result = result + kernel[offset] * padded_rows[offset : offset + out_rows].astype(
            jnp.float32
        )
    return result


def attend_block(
    paired_sums,
    key_tile_rows,
    value_tile_rows,
    leading_row,
    query_normalized,
    similarity_sharpness,
    frame_ceiling,
):
    weighted, normalizer = paired_sums
    row_count = key_tile_rows.shape[0]
    angular_similarity = jnp.einsum(
        "qhd,khd->hqk", query_normalized, key_tile_rows, preferred_element_type=jnp.float32
    )
    token_position = leading_row + lax.broadcasted_iota(jnp.int32, (1, 1, row_count), 2)
    attention_probabilities = jnp.where(
        token_position < frame_ceiling,
        jnp.exp(similarity_sharpness[:, None, None] * (angular_similarity - 1.0)),
        0.0,
    )
    normalizer = normalizer + jnp.sum(attention_probabilities, axis=2).T
    weighted = weighted + jnp.einsum(
        "hqk,khd->qhd",
        attention_probabilities.astype(jnp.bfloat16),
        value_tile_rows,
        preferred_element_type=jnp.float32,
    )
    return (weighted, normalizer)


def synthesis_tables(bin_count, fft_size):
    bin_ids = lax.broadcasted_iota(jnp.int32, (bin_count, fft_size), 0)
    sample_ids = lax.broadcasted_iota(jnp.int32, (bin_count, fft_size), 1)
    phase_angle = 2.0 * math.pi / fft_size * (bin_ids * sample_ids % fft_size).astype(jnp.float32)
    edge_bin = (bin_ids == 0) | (bin_ids == bin_count - 1)
    factor = jnp.where(edge_bin, 1.0, 2.0) / fft_size
    cos_table = factor * jnp.cos(phase_angle)
    sin_table = jnp.where(edge_bin, 0.0, -factor * jnp.sin(phase_angle))
    return jnp.concatenate([cos_table, sin_table], axis=0)


def local(
    tokens,
    masked,
    used_frames,
    tables,
    mask_vec,
    attn_in,
    head_temp,
    attn_out,
    conv_in,
    conv_kernel,
    conv_out,
    voc_in,
    voc_kernel,
    voc_up,
    voc_down,
    voc_head,
    head_bias,
):
    frame_count = tokens.shape[1]
    group_count = lax.axis_size(("head", "sub"))
    group_index = lax.axis_index(("head", "sub"))
    seq_index = lax.axis_index("seq")
    slab_rows = frame_count // group_count
    frame_ceiling = used_frames[0]
    total_frames = frame_count * lax.axis_size("seq")
    code_ids = lax.broadcasted_iota(jnp.int32, (frame_count, tables.shape[1]), 1)
    masked_rows = masked == 1
    embedded = masked_rows.astype(jnp.float32)[:, None] * mask_vec.astype(jnp.float32)[None, :]
    for rvq_level in range(3):
        matches = tokens[rvq_level][:, None] == code_ids
        if rvq_level == 2:
            matches = matches & jnp.logical_not(masked_rows)[:, None]
        embedded = embedded + jnp.dot(
            matches.astype(jnp.bfloat16), tables[rvq_level], preferred_element_type=jnp.float32
        )
    embedded = embedded.astype(jnp.bfloat16)
    inputs, voc_in_full, voc_up_full, voc_down_full, voc_head_full = (
        lax.all_gather(embedded, ("head", "sub"), axis=1, tiled=True),
        lax.all_gather(voc_in, ("head", "sub"), axis=0, tiled=True),
        lax.all_gather(voc_up, ("head", "sub"), axis=0, tiled=True),
        lax.all_gather(voc_down, ("head", "sub"), axis=0, tiled=True),
        lax.all_gather(voc_head, ("head", "sub"), axis=0, tiled=True),
    )
    normed = layer_norm(inputs.astype(jnp.float32)).astype(jnp.bfloat16)
    local_heads = head_temp.shape[0]
    query_normalized = unit_heads(
        jnp.dot(normed, attn_in[0], preferred_element_type=jnp.float32), local_heads
    )
    key_unit = unit_heads(
        jnp.dot(normed, attn_in[1], preferred_element_type=jnp.float32), local_heads
    ).reshape(frame_count, -1)
    value_rows = jnp.dot(normed, attn_in[2], preferred_element_type=jnp.float32).astype(
        jnp.bfloat16
    )
    head_size = value_rows.shape[1] // local_heads
    start_pair = (
        jnp.zeros((frame_count, local_heads, head_size), jnp.float32),
        jnp.zeros((frame_count, local_heads), jnp.float32),
    )
    paired_sums = start_pair
    key_piece = lax.all_gather(key_unit, "seq", axis=0, tiled=True)
    value_piece = lax.all_gather(value_rows, "seq", axis=0, tiled=True)
    row_count = key_piece.shape[0]
    key_heads = key_piece.reshape(row_count, local_heads, head_size)
    value_heads = value_piece.reshape(row_count, local_heads, head_size)
    block_count = row_count // 512

    def scan_step(inner_pair, block_item):
        key_tile_rows, value_tile_rows, block_index = block_item
        return (
            attend_block(
                inner_pair,
                key_tile_rows,
                value_tile_rows,
                block_index * 512,
                query_normalized,
                head_temp,
                frame_ceiling,
            ),
            None,
        )

    block_items = (
        key_heads.reshape(block_count, 512, local_heads, head_size),
        value_heads.reshape(block_count, 512, local_heads, head_size),
        jnp.arange(block_count, dtype=jnp.int32),
    )
    paired_sums, _unused = lax.scan(scan_step, paired_sums, block_items)
    weighted, normalizer = paired_sums
    attended = (weighted / normalizer[:, :, None]).reshape(frame_count, -1).astype(jnp.bfloat16)
    head_part = jnp.dot(attended, attn_out, preferred_element_type=jnp.float32)
    fft_size = 2 * (head_bias.shape[0] // 2 - 1)
    intersection = fft_size // HOP
    half_voc = voc_kernel.shape[0] // 2
    vocoder_rim = half_voc + intersection // 2
    conv_reach = conv_kernel.shape[0] // 2 + vocoder_rim
    window_rows = slab_rows + 2 * vocoder_rim
    stream = inputs.astype(jnp.float32) + lax.psum(
        head_part.astype(jnp.bfloat16), ("head", "sub")
    ).astype(jnp.float32)
    stream_rims = with_halo(stream.astype(jnp.bfloat16), (("seq", 0),), conv_reach).astype(
        stream.dtype
    )
    conv_normed = layer_norm(stream_rims).astype(jnp.bfloat16)
    residual_window = lax.dynamic_slice_in_dim(
        stream_rims, group_index * slab_rows + conv_reach - vocoder_rim, window_rows, 0
    )
    gate_value = jnp.dot(conv_normed, conv_in[0], preferred_element_type=jnp.float32)
    gate_signal = jnp.dot(conv_normed, conv_in[1], preferred_element_type=jnp.float32)
    gated_rows = (gate_value * jax.nn.sigmoid(gate_signal)).astype(jnp.bfloat16)
    depth_rows = depthwise(conv_kernel, gated_rows)
    activated = (depth_rows * jax.nn.sigmoid(depth_rows)).astype(jnp.bfloat16)
    windows = jnp.stack(
        [
            activated[member * slab_rows : member * slab_rows + window_rows]
            for member in range(group_count)
        ]
    )
    partial_out = jnp.einsum("gsc,cd->gsd", windows, conv_out, preferred_element_type=jnp.float32)
    conv_sum = lax.psum_scatter(
        partial_out.astype(jnp.bfloat16), ("head", "sub"), scatter_dimension=0, tiled=True
    ).astype(jnp.float32)[0]
    block_norm = layer_norm(residual_window + conv_sum).astype(jnp.bfloat16)
    feature_out = block_norm[vocoder_rim : vocoder_rim + slab_rows]
    first_frame = seq_index * frame_count + group_index * slab_rows - vocoder_rim
    frame_ids = first_frame + lax.broadcasted_iota(jnp.int32, (window_rows, 1), 0)
    live_rows = (frame_ids >= 0) & (frame_ids < frame_ceiling)
    base_rows = layer_norm(
        jnp.where(
            live_rows, jnp.dot(block_norm, voc_in_full, preferred_element_type=jnp.float32), 0.0
        )
    )
    vdepth = depthwise(voc_kernel, base_rows)
    voc_rows = vdepth.shape[0]
    inner_rows = layer_norm(vdepth).astype(jnp.bfloat16)
    hidden = jax.nn.gelu(
        jnp.dot(inner_rows, voc_up_full, preferred_element_type=jnp.float32), approximate=False
    ).astype(jnp.bfloat16)
    refined = base_rows[half_voc : half_voc + voc_rows] + jnp.dot(
        hidden, voc_down_full, preferred_element_type=jnp.float32
    )
    head_input = layer_norm(refined).astype(jnp.bfloat16)
    spectrum = jnp.dot(head_input, voc_head_full, preferred_element_type=jnp.float32) + head_bias
    bin_count = spectrum.shape[1] // 2
    magnitude = jnp.minimum(jnp.exp(spectrum[:, :bin_count]), 100.0)
    phase_rows = spectrum[:, bin_count:]
    coefficients = jnp.concatenate(
        [magnitude * jnp.cos(phase_rows), magnitude * jnp.sin(phase_rows)], axis=1
    )
    wave_rows = jnp.dot(
        coefficients, synthesis_tables(bin_count, fft_size), precision=lax.Precision.HIGHEST
    )
    sample_ids = lax.broadcasted_iota(jnp.int32, (fft_size,), 0).astype(jnp.float32)
    hann_window = 0.5 - 0.5 * jnp.cos(2.0 * math.pi / fft_size * sample_ids)
    wave_ids = first_frame + half_voc + lax.broadcasted_iota(jnp.int32, (voc_rows, 1), 0)
    exists = ((wave_ids >= 0) & (wave_ids < total_frames)).astype(jnp.float32)
    framed = (wave_rows * hann_window[None, :] * exists).reshape(voc_rows, intersection, HOP)
    env_rows = (exists * (hann_window * hann_window)[None, :]).reshape(voc_rows, intersection, HOP)
    audio_sum = jnp.zeros((slab_rows, HOP), jnp.float32)
    energy = jnp.zeros((slab_rows, HOP), jnp.float32)
    for quarter in range(intersection):
        begin = intersection - quarter
        audio_sum = audio_sum + framed[begin : begin + slab_rows, quarter]
        energy = energy + env_rows[begin : begin + slab_rows, quarter]
    waveform = (audio_sum / energy).reshape(slab_rows * HOP)
    return (feature_out, waveform)


def solution(mesh):
    in_specs = (
        P(None, ("groups", "seq")),
        P(("groups", "seq")),
        P("groups"),
        P(None, None, ("head", "sub")),
        P(("head", "sub")),
        P(None, None, ("head", "sub")),
        P(("head", "sub")),
        P(("head", "sub"), None),
        P(None, None, ("head", "sub")),
        P(None, ("head", "sub")),
        P(("head", "sub"), None),
        P(("head", "sub"), None),
        P(),
        P(("head", "sub"), None),
        P(("head", "sub"), None),
        P(("head", "sub"), None),
        P(),
    )
    out_specs = (P(("groups", "seq", "head", "sub"), None), P(("groups", "seq", "head", "sub")))
    return jax.shard_map(local, mesh=mesh, in_specs=in_specs, out_specs=out_specs, check_vma=False)
```

profile of v0, /device:TPU:0, one launch (start us, length us, event | category | flops | bytes accessed | tf_op | source)
XLA Modules:
  0.0 276.0 jit_solution(7080855097597714248)
XLA Ops:
  12.6 2.3 fusion.41
  16.1 18.6 %all-gather.6.cloned.1.call-done = bf16[512,1024]{1,0:T(8,128)(2,1)} async-done(((bf16[512,256]{1,0:T(8,128)(2,1)}), bf16[512,1024]{1,0:T(8,128)(2,1)}) %all-gather.6.cloned.1.call-update) | async-done | bytes 1048592 | tf_op jit(solution)/shard_map/all_gather | solution.py:129
  40.1 16.1 %all_gather.23 = bf16[2048,128]{0,1:T(8,128)(2,1)S(1)} all-gather(bf16[512,128]{0,1:T(8,128)(2,1)S(1)} %bitcast.157), channel_id=1, replica_groups=mesh['groups'=2,'seq'=4,'head'=2,'sub'=2] {'seq'}, dimensions={0}, use_global_device_ids=true | all-gather | bytes 655360 | tf_op jit(solution)/shard_map/all_gather | solution.py:152
  57.3 1.9 copy.28
  59.3 2.1 multiply_reduce_fusion.5
  61.4 16.0 %all_gather.22 = bf16[2048,128]{1,0:T(8,128)(2,1)S(1)} all-gather(bf16[512,128]{1,0:T(8,128)(2,1)S(1)} %convolution_convert_fusion.2), channel_id=1, replica_groups=mesh['groups'=2,'seq'=4,'head'=2,'sub'=2] {'seq'}, dimensions={0}, use_global_device_ids=true | all-gather | bytes 655360 | tf_op jit(solution)/shard_map/all_gather | solution.py:153
  79.6 15.6 %while.15 = (s32[]{:T(128)}, f32[512,2,64]{0,2,1:T(8,128)S(1)}, f32[512,2]{0,1:T(2,128)S(1)}, bf16[4,512,2,64]{1,3,2,0:T(8,128)(2,1)S(1)}, s32[4]{0:T(128)S(1)},...) while((s32[]{:T(128)}, f32[512,2,64]{0,2,1:T(8,128)S(1)}, ...), condition=%wide.region_6.7_spmd.clone, body=%wide.region_4.6_spmd.clone.sunk | while | flops 136972288 | bytes 3032748 | solution.py:179
  95.3 2.4 convolution_convert_fusion.1
  97.9 35.7 %all-reduce.2.cloned.1.call-done = bf16[512,1024]{1,0:T(8,128)(2,1)} async-done(((bf16[512,1024]{1,0:T(8,128)(2,1)}), bf16[512,1024]{1,0:T(8,128)(2,1)}) %all-reduce.2.cloned.1.call-update) | async-done | bytes 1048592 | tf_op jit(solution)/shard_map/psum | solution.py:189
  133.6 1.7 fusion.26
  135.3 3.4 %collective-permute-start = (bf16[20,1024]{1,0:T(8,128)(2,1)S(1)}, bf16[20,1024]{1,0:T(8,128)(2,1)S(1)}, u32[]{:S(2)}, u32[]{:S(2)}) collective-permute-start(bf16[20,1024]{1,0:T(8,128)(2,1)S(1)} %get-tuple-element.190), channel_id=1, source_target_pairs={{0,4},{4,8},{8,12},{1,5},{5,9},{9,13},{2,6},{6,10},{10,14},{3,7},{... | collective-permute-start | bytes 122888 | tf_op jit(solution)/shard_map/ppermute | solution.py:18
  140.5 4.3 %collective-permute-done.1 = bf16[20,1024]{1,0:T(8,128)(2,1)S(1)} collective-permute-done((bf16[20,1024]{1,0:T(8,128)(2,1)S(1)}, bf16[20,1024]{1,0:T(8,128)(2,1)S(1)}, u32[]{:S(2)}, u32[]{:S(2)}) %collective-permute-start.1) | collective-permute-done | bytes 40992 | tf_op jit(solution)/shard_map/ppermute | solution.py:19
  147.2 2.3 multiply_convert_fusion.2
  154.7 15.1 %multiply_select_fusion = (f32[641,1280]{1,0:T(8,128)}, f32[641,1280]{1,0:T(8,128)}) fusion(f32[641]{0:T(1024)S(1)} %fusion.133, pred[641]{0:T(1024)(128)(4,1)S(1)} %fusion.132, f32[641]{0:T(1024)S(1)} %select_multiply_fusion), kind=kLoop, calls=%fused_computation.20 | loop fusion | flops 9845760 | bytes 6569609 | tf_op jit(solution)/shard_map/jit(_where)/select_n | solution.py:87
  169.8 1.8 fusion.166
  171.6 4.9 %reduce-scatter.2.cloned.1.call-done = bf16[1,138,1024]{2,1,0:T(8,128)(2,1)} async-done(((bf16[4,138,1024]{2,1,0:T(8,128)(2,1)}), bf16[1,138,1024]{2,1,0:T(8,128)(2,1)}) %reduce-scatter.2.cloned.1.call-update) | async-done | bytes 282640 | tf_op jit(solution)/shard_map/reduce_scatter | solution.py:211
  180.6 14.1 %all-gather.8.cloned.1.call-done = bf16[1024,512]{1,0:T(8,128)(2,1)} async-done(((bf16[256,512]{1,0:T(8,128)(2,1)}), bf16[1024,512]{1,0:T(8,128)(2,1)}) %all-gather.8.cloned.1.call-update) | async-done | bytes 1048592 | tf_op jit(solution)/shard_map/all_gather | solution.py:130
  198.0 17.8 %all-gather.10.cloned.1.call-done = bf16[512,1536]{1,0:T(8,128)(2,1)} async-done(((bf16[128,1536]{1,0:T(8,128)(2,1)}), bf16[512,1536]{1,0:T(8,128)(2,1)}) %all-gather.10.cloned.1.call-update) | async-done | bytes 1572880 | tf_op jit(solution)/shard_map/all_gather | solution.py:131
  215.8 21.1 %all-gather.12.cloned.1.call-done = bf16[1536,512]{1,0:T(8,128)(2,1)} async-done(((bf16[384,512]{1,0:T(8,128)(2,1)}), bf16[1536,512]{1,0:T(8,128)(2,1)}) %all-gather.12.cloned.1.call-update) | async-done | bytes 1572880 | tf_op jit(solution)/shard_map/all_gather | solution.py:132
  236.9 4.3 %fusion.178 = (f32[132]{0:T(256)S(1)}, f32[132,512]{1,0:T(8,128)S(1)}) fusion(bf16[1536,512]{1,0:T(8,128)(2,1)} %all-gather.12.cloned.1.call-done, bf16[512,1536]{1,0:T(8,128)(2,1)} %all-gather.10.cloned.1.call-done, f32[132,512]{1,0:T(8,128)S(1)} %get-tuple-element.185, f32[132]{0:T(256)S(1)} %add_rsqrt_fusion.5, f32[132]{0:T(256)S(1)} %broadcast_multiply_fusion.4, ...), kind=kOutput, calls=%fused_computation.260 | convolution fusion | flops 428752768 | bytes 3958320 | tf_op jit(solution)/shard_map/dot_general | solution.py:230
  241.4 15.5 %all-gather.14.cloned.1.call-done = bf16[512,1282]{0,1:T(8,128)(2,1)} async-done(((bf16[128,1282]{0,1:T(8,128)(2,1)}), bf16[512,1282]{0,1:T(8,128)(2,1)}) %all-gather.14.cloned.1.call-update) | async-done | bytes 1312784 | tf_op jit(solution)/shard_map/all_gather | solution.py:133
  256.9 2.1 convolution_add_fusion
  259.0 1.9 cosine_multiply_fusion.1
  260.9 6.2 %fusion.19 = f32[132,1280]{1,0:T(8,128)S(1)} fusion(f32[641,1280]{1,0:T(8,128)S(1)} %copy-done.2, f32[641,1280]{1,0:T(8,128)} %get-tuple-element.254, f32[132,641]{1,0:T(8,128)S(1)} %get-tuple-element.199, f32[132,641]{1,0:T(8,128)S(1)} %get-tuple-element.198, f32[132]{0:T(256)S(1)} %and_convert_fusion, f32[1280]{0:T(1024)S(1)} %multiply_subtract_fusion), kind=kOutput, calls=%fused_computation.31 | convolution fusion | flops 2601428736 | bytes 7922224 | tf_op jit(solution)/shard_map/dot_general | solution.py:241
  (123 shorter events, 46.3 us)
Async XLA Ops:
  7.2 142.5 %copy-start = (bf16[256,1024]{1,0:T(8,128)(2,1)S(1)}, bf16[256,1024]{1,0:T(8,128)(2,1)}, u32[]{:S(2)}) copy-start(bf16[256,1024]{1,0:T(8,128)(2,1)} %param.29) | copy-start | bytes 1572868
  7.2 27.5 %all-gather.6.cloned.1.call-start = ((), (), s32[]{:S(2)}) async-start(), calls=%async_computation.1 | async-start | bytes 1310720 | tf_op jit(solution)/shard_map/all_gather | solution.py:129
  10.9 4.1 %copy-start.3 = (bf16[3,1024,128]{2,1,0:T(8,128)(2,1)S(1)}, bf16[3,1024,128]{2,1,0:T(8,128)(2,1)}, u32[]{:S(2)}) copy-start(bf16[3,1024,128]{2,1,0:T(8,128)(2,1)} %param.24) | copy-start | bytes 2359300
  14.9 118.6 %all-reduce.2.cloned.1.call-start = ((), (), s32[]{:S(2)}) async-start(), calls=%async_computation.2 | async-start | bytes 2097152 | tf_op jit(solution)/shard_map/psum | solution.py:189
  34.6 3.2 %copy-start.1 = (bf16[512,1024]{1,0:T(8,128)(2,1)S(1)}, bf16[512,1024]{1,0:T(8,128)(2,1)}, u32[]{:S(2)}) copy-start(bf16[512,1024]{1,0:T(8,128)(2,1)} %all-gather.6.cloned.1.call-done) | copy-start | bytes 3145732
  61.4 18.2 %copy-start.8 = (f32[2]{0:T(128)S(1)}, f32[2]{0:T(128)}, u32[]{:S(2)}) copy-start(f32[2]{0:T(128)} %param.25) | copy-start | bytes 28
  95.3 2.6 copy-start.4
  97.8 78.7 %reduce-scatter.2.cloned.1.call-start = ((), (), s32[]{:S(2)}) async-start(), calls=%async_computation.3 | async-start | bytes 1474560 | tf_op jit(solution)/shard_map/reduce_scatter | solution.py:211
  133.6 12.1 %copy-start.7 = (bf16[2,1024,256]{2,1,0:T(8,128)(2,1)S(1)}, bf16[2,1024,256]{2,1,0:T(8,128)(2,1)}, u32[]{:S(2)}) copy-start(bf16[2,1024,256]{2,1,0:T(8,128)(2,1)} %param.27) | copy-start | bytes 3145732
  135.3 5.1 %collective-permute-start = (bf16[20,1024]{1,0:T(8,128)(2,1)S(1)}, bf16[20,1024]{1,0:T(8,128)(2,1)S(1)}, u32[]{:S(2)}, u32[]{:S(2)}) collective-permute-start(bf16[20,1024]{1,0:T(8,128)(2,1)S(1)} %get-tuple-element.190), channel_id=1, source_target_pairs={{0,4},{4,8},{8,12},{1,5},{5,9},{9,13},{2,6},{6,10},{10,14},{3,7},{... | collective-permute-start | bytes 122888 | tf_op jit(solution)/shard_map/ppermute | solution.py:18
  138.7 6.0 %collective-permute-start.1 = (bf16[20,1024]{1,0:T(8,128)(2,1)S(1)}, bf16[20,1024]{1,0:T(8,128)(2,1)S(1)}, u32[]{:S(2)}, u32[]{:S(2)}) collective-permute-start(bf16[20,1024]{1,0:T(8,128)(2,1)S(1)} %get-tuple-element.191), channel_id=1, source_target_pairs={{4,0},{8,4},{12,8},{5,1},{9,5},{13,9},{6,2},{10,6},{14,10},{7,3},{... | collective-permute-start | bytes 122888 | tf_op jit(solution)/shard_map/ppermute | solution.py:19
  149.6 4.8 %copy-start.5 = (f32[7,512]{1,0:T(8,128)S(1)}, f32[7,512]{1,0:T(8,128)}, u32[]{:S(2)}) copy-start(f32[7,512]{1,0:T(8,128)} %param.31) | copy-start | bytes 43012
  151.2 43.5 %all-gather.8.cloned.1.call-start = ((), (), s32[]{:S(2)}) async-start(), calls=%async_computation.4 | async-start | bytes 1310720 | tf_op jit(solution)/shard_map/all_gather | solution.py:130
  151.7 64.1 %all-gather.10.cloned.1.call-start = ((), (), s32[]{:S(2)}) async-start(), calls=%async_computation.5 | async-start | bytes 1966080 | tf_op jit(solution)/shard_map/all_gather | solution.py:131
  152.3 84.6 %all-gather.12.cloned.1.call-start = ((), (), s32[]{:S(2)}) async-start(), calls=%async_computation.6 | async-start | bytes 1966080 | tf_op jit(solution)/shard_map/all_gather | solution.py:132
  152.9 104.0 %all-gather.14.cloned.1.call-start = ((), (), s32[]{:S(2)}) async-start(), calls=%async_computation.7 | async-start | bytes 1648640 | tf_op jit(solution)/shard_map/all_gather | solution.py:133
  198.0 58.9 %copy-start.6 = (f32[1282]{0:T(1024)S(1)}, f32[1282]{0:T(1024)}, u32[]{:S(2)}) copy-start(f32[1282]{0:T(1024)} %param.35) | copy-start | bytes 15388
  256.9 4.0 %copy-start.2 = (f32[641,1280]{1,0:T(8,128)S(1)}, f32[641,1280]{1,0:T(8,128)}, u32[]{:S(2)}) copy-start(f32[641,1280]{1,0:T(8,128)} %get-tuple-element.253) | copy-start | bytes 9845764
Sparse Core Ops, SparseCore 0:
  15.1 19.5 all-gather.5
  97.9 35.6 all-reduce.1
  151.3 25.1 reduce-scatter.1
  177.9 16.7 all-gather.7
  196.1 19.6 all-gather.9
  217.2 19.6 all-gather.11
  238.4 18.3 all-gather.13
where the time goes:
time: 277 us; the launch traced here: 276 us
  waiting for transfers between devices  134 us (48%)
  other arithmetic  38 us (14%)
  matrix products  37 us (13%)
  blocking collectives  32.1 us (12%)
  between operations  15.2 us (5%)
  local copies, waits for them, and re-layouts  11.3 us (4%)
  starting transfers between devices  5.14 us (2%)
  loops' own time  2.77 us (1%)
    psum x1, waiting for transfers between devices, local(): lax.psum(head_part.astype(jnp.bfloat16), ('head', 'sub'))  35.7 us
    all_gather x1, waiting for transfers between devices, local(): lax.all_gather(voc_down, ('head', 'sub'), axis=0, tiled=True)  21.1 us
    all_gather x1, waiting for transfers between devices, local(): lax.all_gather(embedded, ('head', 'sub'), axis=1, tiled=True)  18.6 us
    all_gather x1, waiting for transfers between devices, local(): lax.all_gather(voc_up, ('head', 'sub'), axis=0, tiled=True)  17.8 us
    all_gather x1, blocking collectives, local(): key_piece = lax.all_gather(key_unit, 'seq', axis=0, tiled=True)  16.1 us
    all_gather x1, blocking collectives, local(): value_piece = lax.all_gather(value_rows, 'seq', axis=0, tiled=True)  16 us
    all_gather x1, waiting for transfers between devices, local(): lax.all_gather(voc_head, ('head', 'sub'), axis=0, tiled=True)  15.5 us
    select_n x1, other arithmetic, synthesis_tables(): sin_table = jnp.where(edge_bin, 0.0, -factor * jnp.sin(phase_angle))  15.1 us
  transfers between devices with their start and end apart: 9, of which 9 were waited for; matrix products, arithmetic and copies ran while one was open for 11% of the time, Pallas kernels for 0%

commit v1 on v0

v1 whole, which is shorter than its diff:
```python
import math

import jax
import jax.numpy as jnp
import ml_dtypes
import numpy as np
from jax import lax
from jax.experimental import pallas as pl
from jax.experimental.pallas import tpu as pltpu
from jax.sharding import PartitionSpec as P

HOP = 320
LANES = 128
KEY_TILE = 256
EDGE = 32
VMEM_BYTES = 56 * 2**20
F32 = jnp.float32
BF16 = jnp.bfloat16
HBM = pl.BlockSpec(memory_space=pl.ANY)
VMEM = pl.BlockSpec(memory_space=pltpu.VMEM)
SMEM = pl.BlockSpec(memory_space=pltpu.SMEM)


def round_up(value, multiple):
    return -(-value // multiple) * multiple


def row_tile(rows, most):
    return max(t for t in range(16, most + 1, 16) if rows % t == 0)


def shifts():
    heads, subs = lax.axis_size("head"), lax.axis_size("sub")
    return [(dh, ds) for dh in range(heads) for ds in range(subs)]


def member(shift, sign):
    heads, subs = lax.axis_size("head"), lax.axis_size("sub")
    head = lax.rem(lax.axis_index("head") + (sign * shift[0] + heads), heads)
    sub = lax.rem(lax.axis_index("sub") + (sign * shift[1] + subs), subs)
    return head * subs + sub


def rotate(x, axis, by):
    size = lax.axis_size(axis)
    return lax.ppermute(x, axis, [(i, (i + by) % size) for i in range(size)])


def gather_members(x):
    pieces = []
    for dh in range(lax.axis_size("head")):
        base = x if dh == 0 else rotate(x, "head", dh)
        for ds in range(lax.axis_size("sub")):
            pieces.append(base if ds == 0 else rotate(base, "sub", ds))
    return pieces


def send_members(pieces):
    heads, subs = lax.axis_size("head"), lax.axis_size("sub")
    out = []
    for (dh, ds), piece in zip(shifts(), pieces):
        if dh or ds:
            perm = [
                (h * subs + s, (h + dh) % heads * subs + (s + ds) % subs)
                for h in range(heads)
                for s in range(subs)
            ]
            piece = lax.ppermute(piece, ("head", "sub"), perm)
        out.append(piece)
    return out


def ring_block(place):
    size = lax.axis_size("seq")
    place = lax.rem(place + size, size)
    return jnp.where(2 * place < size, 2 * place, 2 * (size - 1 - place) + 1)


def ring_place(block):
    size = lax.axis_size("seq")
    return jnp.where(lax.rem(block, 2) == 0, lax.div(block, 2), size - 1 - lax.div(block, 2))


def ring_send(x, by):
    size = lax.axis_size("seq")
    order = list(range(0, size, 2)) + list(range(1, size, 2))[::-1]
    return lax.ppermute(x, "seq", [(order[i], order[(i + by) % size]) for i in range(size)])


def ring_gather(first, second, stages):
    size = lax.axis_size("seq")
    blocks, sources = [first, second], [(0, 0), (0, 1)]
    ahead, behind = [first, second], [first, second]
    for hop in range(1, size // 2 + 1):
        if 2 * hop == size:
            ahead, behind = [ring_send(ahead[0], 1), None], [None, ring_send(behind[1], -1)]
        else:
            new = [ring_send(ahead[0], 1), ring_send(behind[1], -1)]
            new += [ring_send(ahead[1], 1), ring_send(behind[0], -1)]
            ahead, behind = [new[0], new[2]], [new[3], new[1]]
        done = stages[hop]([p for p in ahead + behind if p is not None])
        ahead = [None if p is None else done.pop(0) for p in ahead]
        behind = [None if p is None else done.pop(0) for p in behind]
        for pieces, way in ((ahead, -1), (behind, 1)):
            for half, piece in enumerate(pieces):
                if piece is not None:
                    blocks.append(piece)
                    sources.append((way * hop, half))
    return blocks, sources


def together(*groups):
    flat = lax.optimization_barrier(tuple(x for g in groups for x in g))
    out, at = [], 0
    for g in groups:
        out.append(list(flat[at : at + len(g)]))
        at += len(g)
    return out


def dot(a, b):
    return jnp.dot(a, b, preferred_element_type=F32)


def normalize(parts, width):
    mean = sum(jnp.sum(p, axis=-1, keepdims=True) for p in parts) * (1.0 / width)
    parts = [p - mean for p in parts]
    var = sum(jnp.sum(p * p, axis=-1, keepdims=True) for p in parts) * (1.0 / width)
    scale = lax.rsqrt(var + 1e-05)
    return [p * scale for p in parts]


def layer_norm(values):
    return normalize([values], values.shape[-1])[0]


def call(kernel, out_shape, in_specs, out_specs, scratch, cost, name):
    return pl.pallas_call(
        kernel,
        out_shape=out_shape,
        in_specs=in_specs,
        out_specs=out_specs,
        scratch_shapes=scratch,
        compiler_params=pltpu.CompilerParams(vmem_limit_bytes=VMEM_BYTES),
        cost_estimate=pl.CostEstimate(flops=0, bytes_accessed=int(cost * 2**20), transcendentals=0),
        name=name,
    )


def embed_kernel(tokens_ref, masked_ref, tables_ref, mask_ref, out_ref):
    rows, codes = out_ref.shape[0], tables_ref.shape[1]
    tile = LANES
    lane = lax.broadcasted_iota(jnp.int32, (tile, LANES), 1)
    mask_row = mask_ref[...].astype(F32)[None, :]

    def column(row):
        return jnp.transpose(jnp.broadcast_to(row, (LANES, tile)))

    for start in range(0, rows, tile):
        masked = column(masked_ref[:, start : start + tile]) == 1
        total = jnp.where(masked[:, :1], mask_row, 0.0)
        for level in range(3):
            ids = column(tokens_ref[level : level + 1, start : start + tile])
            if level == 2:
                ids = jnp.where(masked, -1, ids)
            hot = jnp.concatenate(
                [
                    jnp.where(ids == lane + at, 1.0, 0.0).astype(BF16)
                    for at in range(0, codes, LANES)
                ],
                axis=1,
            )
            total = total + dot(hot, tables_ref[level])
        out_ref[start : start + tile, :] = total.astype(BF16)


def unit_heads(projected, head_size):
    width = projected.shape[1]
    lane = lax.broadcasted_iota(jnp.int32, (1, width), 1)
    squares = projected * projected
    scale = jnp.zeros_like(projected)
    for at in range(0, width, head_size):
        own = (lane >= at) & (lane < at + head_size)
        total = jnp.sum(jnp.where(own, squares, 0.0), axis=-1, keepdims=True)
        scale = jnp.where(own, lax.rsqrt(total + 1e-06), scale)
    return projected * scale


def project_kernel(count, head_size, *refs):
    pieces, (w_ref,) = refs[:count], refs[count : count + 1]
    q_ref, kv_refs, emb_ref, first_ref, last_ref = (
        refs[count + 1],
        refs[count + 2 : count + 4],
        *refs[count + 4 : count + 7],
    )
    w_scr = refs[count + 7]
    rows, piece_cols = pieces[0].shape
    cols = w_ref.shape[2]
    width = q_ref.shape[1]
    model = emb_ref.shape[1]
    owners = [pl.multiple_of(member(s, -1) * piece_cols, piece_cols) for s in shifts()]
    if width != cols:
        w_scr[...] = jnp.zeros_like(w_scr)
    for r in range(count):
        for p in range(3):
            w_scr[r * piece_cols : (r + 1) * piece_cols, p * width : p * width + cols] = w_ref[
                p, pl.ds(owners[r], piece_cols), :
            ]
    half = rows // 2
    tile = row_tile(half, 128)
    for start in range(0, rows, tile):
        at = slice(start, start + tile)
        raw = [piece[at, :] for piece in pieces]
        normed = jnp.concatenate(
            [p.astype(BF16) for p in normalize([p.astype(F32) for p in raw], model)], axis=1
        )
        proj = dot(normed, w_scr[...])
        query = unit_heads(proj[:, :width], head_size).astype(BF16)
        q_ref[at, :] = query
        kv = jnp.concatenate(
            [unit_heads(proj[:, width : 2 * width], head_size), proj[:, 2 * width :]], axis=1
        ).astype(BF16)
        kv_refs[start // half][start % half : start % half + tile, :] = kv
        for r in range(count):
            emb_ref[at, pl.ds(owners[r], piece_cols)] = raw[r]
        for edge_ref, here in (
            (first_ref, slice(0, EDGE) if start == 0 else None),
            (last_ref, slice(tile - EDGE, tile) if start + tile == rows else None),
        ):
            if here is not None:
                for r in range(count):
                    edge_ref[:, pl.ds(owners[r], piece_cols)] = raw[r][here]
                edge_ref[:, model:] = query[here]


def attend_kernel(head_size, sources, seq_size, out_count, slab, *refs):
    used_ref, temp_ref, q_ref = refs[:3]
    kv_refs = refs[3 : 3 + len(sources)]
    out_refs = refs[3 + len(sources) : 3 + len(sources) + out_count]
    kv_scr, acc_scr, att_scr, sems = refs[3 + len(sources) + out_count :]
    me = lax.axis_index("seq")
    used = used_ref[0]
    rows, width = q_ref.shape
    heads = temp_ref.shape[0]
    total = kv_scr.shape[0]
    frame_count = total // seq_size

    place = ring_place(me)

    def transfers(act):
        for at, (ref, (hop, half)) in enumerate(zip(kv_refs, sources)):
            part = ref.shape[0]
            start = pl.multiple_of(ring_block(place + hop) * frame_count + half * part, part)
            copy = pltpu.make_async_copy(ref, kv_scr.at[pl.ds(start, part), :], sems.at[at])
            getattr(copy, act)()

    transfers("start")
    acc_scr[...] = jnp.zeros_like(acc_scr)
    lane = lax.broadcasted_iota(jnp.int32, (1, width), 1)
    own = [(lane >= h * head_size) & (lane < (h + 1) * head_size) for h in range(heads)]
    sharp = [temp_ref[h] * math.log2(math.e) for h in range(heads)]
    transfers("wait")
    tile = row_tile(rows, 128)

    def step(block, carry):
        start = pl.multiple_of(block * KEY_TILE, KEY_TILE)
        key = kv_scr[pl.ds(start, KEY_TILE), :width]
        live = start + lax.broadcasted_iota(jnp.int32, (KEY_TILE, 1), 0) < used
        value = jnp.concatenate(
            [
                jnp.where(live, kv_scr[pl.ds(start, KEY_TILE), width:].astype(F32), 0.0),
                jnp.broadcast_to(jnp.where(live, 1.0, 0.0), (KEY_TILE, width)),
            ],
            axis=1,
        ).astype(BF16)
        for h in range(heads):
            for at in range(0, rows, tile):
                query = q_ref[at : at + tile, :]
                query = jnp.where(own[h], query, jnp.zeros_like(query))
                score = lax.dot_general(
                    query, key, (((1,), (1,)), ((), ())), preferred_element_type=F32
                )
                weight = jnp.exp2(score * sharp[h] - sharp[h]).astype(BF16)
                acc_scr[h, at : at + tile, :] += dot(weight, value)
        return carry

    lax.fori_loop(0, lax.div(used + (KEY_TILE - 1), KEY_TILE), step, 0)
    for at in range(0, rows, tile):
        result = jnp.zeros((tile, width), F32)
        for h in range(heads):
            summed = acc_scr[h, at : at + tile, :]
            result = jnp.where(own[h], summed[:, :width] / summed[:, width:], result)
        att_scr[at : at + tile, :] = result.astype(BF16)
    for shift, out_ref in zip(shifts(), out_refs):
        start = pl.multiple_of(member(shift, 1) * slab, slab)
        out_ref[...] = att_scr[pl.ds(start, out_ref.shape[0]), : out_ref.shape[1]]


def sine_cosine(x):
    turns = jnp.floor(x * (1.0 / math.pi) + 0.5)
    r = x - turns * 3.140625
    r = r - turns * 9.67502593994140625e-4
    r = r - turns * 1.509957990978376432e-7
    sign = 1.0 - 2.0 * (turns - 2.0 * jnp.floor(turns * 0.5))
    z = r * r
    s = -2.5052108385e-08
    for c in (2.7557319224e-06, -1.9841269841e-04, 8.3333333333e-03, -1.6666666667e-01):
        s = s * z + c
    c_ = 2.0876756988e-09
    for c in (-2.7557319224e-07, 2.4801587302e-05, -1.3888888889e-03, 4.1666666667e-02, -0.5):
        c_ = c_ * z + c
    return sign * (r + r * z * s), sign * (1.0 + z * c_)


def pack_kernel(*refs):
    attn_out, conv_in, conv_out, voc_in, voc_up, voc_down, conv_kernel, head = refs[:8]
    own, mine = refs[8:12], refs[12:16]
    k_scr, head_scr, sems = refs[16:]
    group = lax.axis_index("groups") % 2
    taps, split = conv_kernel.shape
    kernel = conv_kernel[...]
    upper = kernel.astype(BF16)
    lower = (kernel - upper.astype(F32)).astype(BF16)
    blank = jnp.zeros((k_scr.shape[0] - taps, split), BF16)
    k_scr[...] = jnp.concatenate(
        [
            jnp.concatenate([upper, blank], axis=0),
            jnp.concatenate([lower, blank], axis=0),
            jnp.zeros((k_scr.shape[0], k_scr.shape[1] - 2 * split), BF16),
        ],
        axis=1,
    )
    bins, rows = head.shape[0] // 2, head.shape[1]
    padded = head_scr.shape[1] // 2
    blank = jnp.zeros((padded - bins, rows), F32)
    values = head[...].astype(F32)
    values = jnp.concatenate([values[:bins], blank, values[bins:], blank], axis=0)
    head_scr[...] = jnp.transpose(values).astype(BF16)
    chunks = (
        (attn_out, conv_out, k_scr),
        (conv_in,),
        (voc_in, voc_down),
        (voc_up, head_scr),
    )
    copies = []
    for at, chunk in enumerate(chunks):
        for side in range(2):
            half = lax.rem(group + side, 2)
            start = 0
            for src in chunk:
                if len(src.shape) == 3:
                    src, part = src.at[half], src.shape[1]
                else:
                    part = src.shape[0] // 2
                    src = src.at[pl.ds(pl.multiple_of(half * part, part), part), :]
                for dst in (own[at].at[side], mine[at])[: 2 - side]:
                    copies.append((src, dst.at[pl.ds(start, part), :]))
                start += part
    copies = [pltpu.make_async_copy(a, b, sems.at[i]) for i, (a, b) in enumerate(copies)]
    for copy in copies:
        copy.start()
    for copy in copies:
        copy.wait()


def fetcher(chunks, sems):
    group = lax.axis_index("groups") % 2
    copies = {}

    def fetch(kind, r, chunk, start, part, dst, base):
        copies[kind, r] = []
        for side in range(2):
            pair = chunks[chunk][r]
            src = pair[side] if len(pair) == 2 else pair[0].at[side]
            half = lax.rem(group + side, 2)
            to = pl.ds(pl.multiple_of(base + half * part, part), part)
            copy = pltpu.make_async_copy(
                src.at[pl.ds(start, part), :], dst.at[to, :], sems.at[len(copies) * 2 - 1 - side]
            )
            copy.start()
            copies[kind, r].append(copy)

    def ready(kind, r):
        for copy in copies[kind, r]:
            copy.wait()

    return fetch, ready


def weight_pairs(refs, chunk_count):
    chunks, at = [], 0
    for _ in range(chunk_count):
        pairs = []
        for dh in range(lax.axis_size("head")):
            for ds in range(lax.axis_size("sub")):
                taken = 1 if dh == 0 else 2
                pairs.append(refs[at : at + taken])
                at += taken
        chunks.append(pairs)
    return chunks, refs[at:]


def first_frame(slab):
    count = lax.axis_size("head") * lax.axis_size("sub")
    return (lax.axis_index("seq") * count + member((0, 0), 1)) * slab


def conv_kernel_body(geo, *refs):
    count, halo, rim, taps = geo
    emb_ref = refs[0]
    att_refs = refs[1 : 1 + count]
    chunks, refs = weight_pairs(refs[1 + count :], 2)
    feat_ref, window_ref, emb_scr, w_out, w_conv, k_conv, w_mix, stream_scr, gate_scr, sems = refs
    win, model = emb_scr.shape
    slab = feat_ref.shape[0]
    first = first_frame(slab)
    total_frames = lax.axis_size("seq") * count * slab
    emb_copy = pltpu.make_async_copy(
        emb_ref.at[pl.ds(pl.multiple_of(member((0, 0), 1) * slab, slab), win), :],
        emb_scr,
        sems.at[8 * count],
    )
    emb_copy.start()
    fetch, ready = fetcher(chunks, sems)
    out_half = w_out.shape[0] // count // 2
    mix_half = w_mix.shape[1] // 2
    tap_half = k_conv.shape[1] // 2
    deep = w_conv.shape[1] // 2
    for r in range(count):
        fetch("out", r, 0, 0, out_half, w_out, r * 2 * out_half)
    for r in range(count):
        fetch("conv", r, 1, 0, deep, w_conv.at[r], 0)
        fetch("taps", r, 0, out_half + mix_half, tap_half, k_conv.at[r], 0)
        fetch("mix", r, 0, out_half, mix_half, w_mix.at[r], 0)

    attended = jnp.concatenate([ref[...] for ref in att_refs], axis=1)
    emb_copy.wait()
    for r in range(count):
        ready("out", r)
    frames = first - halo + lax.broadcasted_iota(jnp.int32, (win, 1), 0)
    inside = (frames >= 0) & (frames < total_frames)
    stream = jnp.where(inside, emb_scr[...].astype(F32) + dot(attended, w_out[...]), 0.0)
    stream_scr[...] = stream
    conv_normed = layer_norm(stream).astype(BF16)

    mid = slab + 2 * rim
    group_cols = w_conv.shape[2]
    lead = halo - rim - taps // 2
    conv_sum = jnp.zeros((mid, model), F32)
    for r in range(count):
        ready("conv", r)
        signal = dot(conv_normed, w_conv[r, deep:, :])
        gated = dot(conv_normed, w_conv[r, :deep, :]) * jax.nn.sigmoid(signal)
        gated = gated.astype(BF16).astype(F32)
        ready("taps", r)
        kernel = k_conv[r, :, : 2 * group_cols].astype(F32)
        kernel = kernel[:, :group_cols] + kernel[:, group_cols:]
        active = []
        for c in range(group_cols // LANES):
            lanes = slice(c * LANES, (c + 1) * LANES)
            gate_scr[c] = gated[:, lanes]
            depth = jnp.zeros((mid, LANES), F32)
            for k in range(taps):
                depth = depth + kernel[k : k + 1, lanes] * gate_scr[c, lead + k : lead + k + mid, :]
            active.append((depth * jax.nn.sigmoid(depth)).astype(BF16))
        ready("mix", r)
        part = dot(jnp.concatenate(active, axis=1), w_mix[r])
        conv_sum = conv_sum + part.astype(BF16).astype(F32)
    features = layer_norm(stream_scr[halo - rim : halo - rim + mid, :] + conv_sum).astype(BF16)
    feat_ref[...] = features[rim : rim + slab]
    window_ref[...] = features


def voc_kernel_body(geo, *refs):
    count, rim, half_voc = geo
    used_ref, window_ref, voc_kernel_ref, bias_ref, table_ref, hann_ref = refs[:6]
    chunks, refs = weight_pairs(refs[6:], 2)
    wave_ref, w_vin, w_up, w_down, w_head, w_table, base_scr, wave_scr, sems = refs
    slab = wave_ref.shape[0]
    first = first_frame(slab)
    total_frames = lax.axis_size("seq") * count * slab
    used = used_ref[0]
    owners = [member(s, -1) for s in shifts()]
    fetch, ready = fetcher(chunks, sems)
    vin_half = w_vin.shape[0] // count // 2
    down_half = w_down.shape[0] // count // 2
    up_half = w_up.shape[0] // count // 2
    head_half = w_head.shape[0] // count // 2
    for r in range(count):
        fetch("vin", r, 0, 0, vin_half, w_vin, owners[r] * 2 * vin_half)
    for r in range(count):
        fetch("up", r, 1, 0, up_half, w_up, owners[r] * 2 * up_half)
    for r in range(count):
        fetch("down", r, 0, vin_half, down_half, w_down, owners[r] * 2 * down_half)
    for r in range(count):
        fetch("head", r, 1, up_half, head_half, w_head, owners[r] * 2 * head_half)
    table_copy = pltpu.make_async_copy(table_ref, w_table, sems.at[8 * count])
    table_copy.start()
    features = window_ref[...]
    mid = features.shape[0]

    for r in range(count):
        ready("vin", r)
    ids = first - rim + lax.broadcasted_iota(jnp.int32, (mid, 1), 0)
    live = (ids >= 0) & (ids < used)
    base = layer_norm(jnp.where(live, dot(features, w_vin[...]), 0.0))
    voc = base.shape[1]
    trim = half_voc + 1
    rows = mid - 2 * trim
    depth = []
    for c in range(voc // LANES):
        lanes = slice(c * LANES, (c + 1) * LANES)
        base_scr[c] = base[:, lanes]
        total = jnp.zeros((rows, LANES), F32)
        for k in range(2 * half_voc + 1):
            total = total + voc_kernel_ref[k : k + 1, lanes] * base_scr[c, 1 + k : 1 + k + rows, :]
        depth.append(total)
    inner = jnp.concatenate(
        [p.astype(BF16) for p in normalize(depth, voc)], axis=1
    )
    for r in range(count):
        ready("up", r)
    up = dot(inner, w_up[...])
    hidden = (0.5 * up * (1.0 + lax.erf(up * math.sqrt(0.5)))).astype(BF16)
    for r in range(count):
        ready("down", r)
    center = jnp.concatenate(
        [base_scr[c, trim : trim + rows, :] for c in range(voc // LANES)], axis=1
    )
    head_input = layer_norm(center + dot(hidden, w_down[...])).astype(BF16)
    for r in range(count):
        ready("head", r)
    spectrum = dot(head_input, w_head[...]) + bias_ref[...]
    bins = spectrum.shape[1] // 2
    magnitude = jnp.minimum(jnp.exp(spectrum[:, :bins]), 100.0)
    sine, cosine = sine_cosine(spectrum[:, bins:])
    coefficients = jnp.concatenate([magnitude * cosine, magnitude * sine], axis=1).astype(BF16)
    table_copy.wait()
    ids = first - rim + trim + lax.broadcasted_iota(jnp.int32, (rows, 1), 0)
    exists = jnp.where((ids >= 0) & (ids < total_frames), 1.0, 0.0)
    parts = wave_scr.shape[0]
    span = wave_scr.shape[2]
    for q in range(parts):
        wave_scr[q] = exists * dot(coefficients, w_table[:, q * span : (q + 1) * span])
    audio = jnp.zeros((slab, span), F32)
    energy = jnp.zeros((slab, span), F32)
    for q in range(parts):
        begin = rim - trim + parts // 2 - q
        audio = audio + wave_scr[q, begin : begin + slab, :]
        energy = energy + exists[begin : begin + slab] * hann_ref[q : q + 1, :]
    wave_ref[...] = audio[:, :HOP] / energy[:, :HOP]


def synthesis(bins, padded, span):
    size = 2 * (bins - 1)
    parts = size // HOP
    k = np.arange(bins)[:, None]
    n = np.arange(size)[None, :]
    angle = 2.0 * np.pi / size * (k * n % size)
    hann = 0.5 - 0.5 * np.cos(2.0 * np.pi / size * np.arange(size))
    edge = (k == 0) | (k == bins - 1)
    factor = np.where(edge, 1.0, 2.0) / size * hann[None, :]
    both = (factor * np.cos(angle), np.where(edge, 0.0, -factor * np.sin(angle)))
    table = np.zeros((2, padded, parts, span), np.float32)
    for at, values in enumerate(both):
        table[at, :bins, :, :HOP] = values.reshape(bins, parts, HOP)
    squares = np.zeros((parts, span), np.float32)
    squares[:, :HOP] = (hann * hann).reshape(parts, HOP)
    return table.reshape(2 * padded, parts * span).astype(ml_dtypes.bfloat16), squares


def local(
    tokens,
    masked,
    used_frames,
    tables,
    mask_vec,
    attn_in,
    head_temp,
    attn_out,
    conv_in,
    conv_kernel,
    conv_out,
    voc_in,
    voc_kernel,
    voc_up,
    voc_down,
    voc_head,
    head_bias,
):
    frame_count = tokens.shape[1]
    count = lax.axis_size("head") * lax.axis_size("sub")
    seq_size = lax.axis_size("seq")
    model = attn_in.shape[1]
    piece_cols = tables.shape[2]
    cols = attn_in.shape[2]
    width = round_up(cols, LANES)
    head_size = cols // head_temp.shape[0]
    slab = frame_count // count
    bins = head_bias.shape[0] // 2
    half_voc = voc_kernel.shape[0] // 2
    parts = 2 * (bins - 1) // HOP
    rim = round_up(half_voc + parts // 2, 8)
    halo = round_up(half_voc + parts // 2 + conv_kernel.shape[0] // 2, 8)
    win = slab + 2 * halo
    mid = slab + 2 * rim
    taps = conv_kernel.shape[0]

    embedded = call(
        embed_kernel,
        jax.ShapeDtypeStruct((frame_count, piece_cols), BF16),
        [VMEM] * 4,
        VMEM,
        [],
        9,
        "embed",
    )(tokens, masked[None, :], tables, mask_vec)
    heads_out = lax.axis_size("head")
    crossed = [rotate(embedded, "head", dh) for dh in range(1, heads_out)]
    beside = rotate(embedded, "sub", 1)
    conv_kernel, embedded = lax.optimization_barrier((conv_kernel, embedded))

    padded = round_up(bins, LANES)
    gap = ((0, 0), (0, padded - bins))
    bias = jnp.pad(head_bias.reshape(2, bins), gap).reshape(1, 2 * padded)
    deep = conv_in.shape[1]
    tap_rows = round_up(taps, 32)
    voc = voc_in.shape[1]
    hidden = voc_up.shape[1]
    shapes = (
        ((attn_out.shape[0] + conv_out.shape[0] + tap_rows) // 2, model),
        (deep, conv_in.shape[2]),
        ((voc_in.shape[0] + voc_down.shape[0]) // 2, voc),
        ((voc_up.shape[0] + voc_head.shape[0]) // 2, hidden),
    )
    packed = call(
        pack_kernel,
        [jax.ShapeDtypeStruct((2,) + shape, BF16) for shape in shapes]
        + [jax.ShapeDtypeStruct(shape, BF16) for shape in shapes],
        [HBM] * 6 + [VMEM] * 2,
        [VMEM] * 8,
        [
            pltpu.VMEM((tap_rows, model), BF16),
            pltpu.VMEM((voc_head.shape[0], 2 * padded), BF16),
            pltpu.SemaphoreType.DMA((24,)),
        ],
        15,
        "pack",
    )(attn_out, conv_in, conv_out, voc_in, voc_up, voc_down, conv_kernel, voc_head.T)
    crossed, packed = together(crossed, packed)
    own, mine = packed[:4], packed[4:]
    pieces = [embedded, beside]
    for piece in crossed:
        pieces += [piece, rotate(piece, "sub", 1)]
    others = range(1, heads_out)
    near, far, near_sub, far_sub, own_sub = [[None] * 4 for _ in range(5)]

    def cross(at):
        near[at] = [rotate(mine[at], "head", dh) for dh in others]

    def spread(at):
        far[at] = [rotate(x, "groups", 1) for x in near[at]]

    def share(at):
        near_sub[at] = [rotate(x, "sub", 1) for x in near[at]]
        far_sub[at] = [rotate(x, "sub", 1) for x in far[at]]

    cross(0)
    cross(1)

    half = frame_count // 2
    q_own, kv_first, kv_second, emb_own, edge_first, edge_last = call(
        lambda *refs: project_kernel(count, head_size, *refs),
        (
            jax.ShapeDtypeStruct((frame_count, width), BF16),
            jax.ShapeDtypeStruct((half, 2 * width), BF16),
            jax.ShapeDtypeStruct((half, 2 * width), BF16),
            jax.ShapeDtypeStruct((frame_count, model), BF16),
            jax.ShapeDtypeStruct((EDGE, model + width), BF16),
            jax.ShapeDtypeStruct((EDGE, model + width), BF16),
        ),
        [VMEM] * (count + 1),
        (VMEM,) * 6,
        [pltpu.VMEM((model, 3 * width), BF16)],
        10,
        "project",
    )(*pieces, attn_in)

    def first_stage(results):
        results, near[0], edges[:], mine[2:], own[:2] = together(
            results, near[0], edges, mine[2:], own[:2]
        )
        spread(0)
        cross(2)
        edges[:] = [rotate(edges[0], "seq", -1), rotate(edges[1], "seq", 1)]
        return results

    def second_stage(results):
        results, near[1], edges[:], mine[3:], own[2:] = together(
            results, near[1], edges, mine[3:], own[2:]
        )
        spread(1)
        cross(3)
        return results

    edges = [edge_first, edge_last]
    stages = {hop: lambda results: results for hop in range(1, seq_size // 2 + 1)}
    stages[1] = first_stage
    stages[max(2, seq_size // 2)] = second_stage
    blocks, sources = ring_gather(kv_first, kv_second, stages)
    after, before = edges[0][:halo], edges[1][EDGE - halo :]
    query = jnp.concatenate([before[:, model:], q_own, after[:, model:]], axis=0)
    emb = jnp.concatenate([before[:, :model], emb_own, after[:, :model]], axis=0)

    rows = frame_count + 2 * halo
    total_frames = seq_size * frame_count
    heads = head_temp.shape[0]
    windows = call(
        lambda *refs: attend_kernel(head_size, sources, seq_size, count, slab, *refs),
        (jax.ShapeDtypeStruct((win, cols), BF16),) * count,
        [SMEM, SMEM, VMEM] + [HBM] * len(blocks),
        (VMEM,) * count,
        [
            pltpu.VMEM((total_frames, 2 * width), BF16),
            pltpu.VMEM((heads, rows, 2 * width), F32),
            pltpu.VMEM((rows, width), BF16),
            pltpu.SemaphoreType.DMA((len(blocks),)),
        ],
        24,
        "attend",
    )(used_frames, head_temp, query, *blocks)
    windows, near[0], far[0], near[2] = together(windows, near[0], far[0], near[2])
    attended = send_members(windows)
    spread(2)
    share(0)
    own_sub[:] = [rotate(x, "sub", 1) for x in own]
    share(1)
    attended, near[3] = together(attended, near[3])
    spread(3)
    share(2)
    share(3)
    weights = []
    for at in range(4):
        weights.append([own[at], own_sub[at]])
        for dh in range(heads_out - 1):
            weights[at] += [near[at][dh], far[at][dh], near_sub[at][dh], far_sub[at][dh]]

    span = round_up(HOP, LANES)
    table, squares = synthesis(bins, padded, span)
    features, window = call(
        lambda *refs: conv_kernel_body((count, halo, rim, taps), *refs),
        (
            jax.ShapeDtypeStruct((slab, model), BF16),
            jax.ShapeDtypeStruct((mid, model), BF16),
        ),
        [HBM] + [VMEM] * count + [HBM] * (len(weights[0]) + len(weights[1])),
        (VMEM, VMEM),
        [
            pltpu.VMEM((win, model), BF16),
            pltpu.VMEM((count * cols, model), BF16),
            pltpu.VMEM((count, 2 * deep, conv_in.shape[2]), BF16),
            pltpu.VMEM((count, tap_rows, model), BF16),
            pltpu.VMEM((count,) + conv_out.shape, BF16),
            pltpu.VMEM((win, model), F32),
            pltpu.VMEM((conv_in.shape[2] // LANES, win, LANES), F32),
            pltpu.SemaphoreType.DMA((8 * count + 1,)),
        ],
        18,
        "conv",
    )(emb, *attended, *weights[0], *weights[1])
    wave = call(
        lambda *refs: voc_kernel_body((count, rim, half_voc), *refs),
        jax.ShapeDtypeStruct((slab, HOP), F32),
        [SMEM] + [VMEM] * 3 + [HBM, VMEM] + [HBM] * (len(weights[2]) + len(weights[3])),
        VMEM,
        [
            pltpu.VMEM((count * voc_in.shape[0], voc), BF16),
            pltpu.VMEM((count * voc_up.shape[0], voc_up.shape[1]), BF16),
            pltpu.VMEM((count * voc_down.shape[0], voc), BF16),
            pltpu.VMEM((count * voc_head.shape[0], 2 * padded), BF16),
            pltpu.VMEM(table.shape, BF16),
            pltpu.VMEM((voc // LANES, mid, LANES), F32),
            pltpu.VMEM((parts, mid - 2 * (half_voc + 1), span), F32),
            pltpu.SemaphoreType.DMA((8 * count + 1,)),
        ],
        18,
        "vocoder",
    )(
        used_frames,
        window,
        voc_kernel,
        bias,
        jnp.asarray(table),
        jnp.asarray(squares),
        *weights[2],
        *weights[3],
    )
    return features, wave.reshape(slab * HOP)


def solution(mesh):
    in_specs = (
        P(None, ("groups", "seq")),
        P(("groups", "seq")),
        P("groups"),
        P(None, None, ("head", "sub")),
        P(("head", "sub")),
        P(None, None, ("head", "sub")),
        P(("head", "sub")),
        P(("head", "sub"), None),
        P(None, None, ("head", "sub")),
        P(None, ("head", "sub")),
        P(("head", "sub"), None),
        P(("head", "sub"), None),
        P(),
        P(("head", "sub"), None),
        P(("head", "sub"), None),
        P(("head", "sub"), None),
        P(),
    )
    out_specs = (P(("groups", "seq", "head", "sub"), None), P(("groups", "seq", "head", "sub")))
    return jax.shard_map(local, mesh=mesh, in_specs=in_specs, out_specs=out_specs, check_vma=False)
```

time: 277 us -> 116 us (0.42)
  waiting for transfers between devices: 134 us -> 38.1 us
  matrix products: 37 us -> 0 us
  other arithmetic: 38 us -> 2.7 us
  Pallas kernels: 0 us -> 34.3 us
  blocking collectives: 32.1 us -> 0 us
  starting transfers between devices: 5.14 us -> 29 us
  between operations: 15.2 us -> 1.63 us
  loops' own time: 2.77 us -> 0 us
    all_gather x5 -> x0, waiting for transfers between devices: 87 us -> none  [the longest x1 21.1 us: local(): lax.all_gather(voc_down, ('head', 'sub'), axis=0, tiled=True)]
    dot_general x22 -> x0, matrix products: 37 us -> none  [the longest x4 6.58 us: attend_block(): jnp.einsum('qhd,khd->hqk', query_normalized, key_tile_rows, preferred_ele...]
    psum x1 -> x0, waiting for transfers between devices: 35.7 us -> none  [local(): lax.psum(head_part.astype(jnp.bfloat16), ('head', 'sub'))]
    pallas_call x0 -> x6, Pallas kernels: none -> 34.3 us  [the longest x1 7.95 us: local(): call(lambda *refs: conv_kernel_body((count, halo, rim, taps), *refs), (ja...]
    ppermute x2 -> x34, waiting for transfers between devices: 4.66 us -> 38.1 us  [the longest x25 25.5 us: rotate(): return lax.ppermute(x, axis, [(i, (i + by) % size) for i in range(size)])]
    all_gather x2 -> x0, blocking collectives: 32.1 us -> none  [the longest x1 16.1 us: local(): key_piece = lax.all_gather(key_unit, 'seq', axis=0, tiled=True)]
    ppermute x2 -> x34, starting transfers between devices: 4.69 us -> 29 us  [the longest x25 18.2 us: rotate(): return lax.ppermute(x, axis, [(i, (i + by) % size) for i in range(size)])]
    select_n x1 -> x0, other arithmetic: 15.1 us -> none  [synthesis_tables(): sin_table = jnp.where(edge_bin, 0.0, -factor * jnp.sin(phase_angle))]
  transfers between devices with their start and end apart: 9 -> 34, of which waited for: 9 -> 14; matrix products, arithmetic and copies ran while one was open for 11% -> 6% of each run, Pallas kernels for 0% -> 21%
where the time goes in v1:
time: 116 us; the launch traced here: 114 us
  waiting for transfers between devices  38.1 us (33%)
  Pallas kernels  34.3 us (30%)
  starting transfers between devices  29 us (25%)
  local copies, waits for them, and re-layouts  8.59 us (7%)
  other arithmetic  2.7 us (2%)
  between operations  1.63 us (1%)
    ppermute x25, waiting for transfers between devices, rotate(): return lax.ppermute(x, axis, [(i, (i + by) % size) for i in range(size)])  25.5 us
    ppermute x25, starting transfers between devices, rotate(): return lax.ppermute(x, axis, [(i, (i + by) % size) for i in range(size)])  18.2 us
    ppermute x6, starting transfers between devices, ring_send(): lax.ppermute(x, 'seq', [(order[i], order[(i + by) % size]) for i in range...  9.26 us
    ppermute x6, waiting for transfers between devices, ring_send(): lax.ppermute(x, 'seq', [(order[i], order[(i + by) % size]) for i in range...  8.89 us
    pallas_call x1, Pallas kernels, local(): call(lambda *refs: conv_kernel_body((count, halo, rim, taps), *refs), (ja...  7.95 us
    pallas_call x1, Pallas kernels, local(): call(lambda *refs: voc_kernel_body((count, rim, half_voc), *refs), jax.Sh...  7.36 us
    pallas_call x1, Pallas kernels, local(): call(lambda *refs: attend_kernel(head_size, sources, seq_size, count, sla...  6.3 us
    pallas_call x1, Pallas kernels, local(): call(pack_kernel, [jax.ShapeDtypeStruct((2,) + shape, BF16) for shape in...  5.86 us
  transfers between devices with their start and end apart: 34, of which 14 were waited for; matrix products, arithmetic and copies ran while one was open for 6% of the time, Pallas kernels for 21%

profile of v1, /device:TPU:0, one launch (start us, length us, event | category | flops | bytes accessed | tf_op | source)
XLA Modules:
  0.0 114.3 jit_solution(1338158225232853635)
XLA Ops:
  0.6 3.4 %embed.1.refs_0_ = bf16[512,256]{1,0:T(8,128)(2,1)} custom-call(s32[3,512]{1,0:T(4,128)} %tokens_ref.1, s32[1,512]{1,0:T(1,128)} %bitcast.8, bf16[3,1024,256]{2,1,0:T(8,128)(2,1)} %tables_ref.1, bf16[256]{0:T(256)(128)(2,1)} %mask_ref.1), custom_call_target="tpu_custom_call" | custom-call | bytes 9437184 | tf_op jit(solution)/shard_map/embed/pallas_call | solution.py:609
  4.0 2.9 %collective-permute-start.1 = (bf16[512,256]{1,0:T(8,128)(2,1)}, bf16[512,256]{1,0:T(8,128)(2,1)S(1)}, u32[]{:S(2)}, u32[]{:S(2)}) collective-permute-start(bf16[512,256]{1,0:T(8,128)(2,1)} %embed.1.refs_0_), channel_id=1, source_target_pairs={{0,2},{2,0},{1,3},{3,1},{4,6},{6,4},{5,7},{7,5},{8,10},{10,8},{9,1... | collective-permute-start | bytes 786440 | tf_op jit(solution)/shard_map/ppermute | solution.py:46
  6.9 5.9 %pack.1 = (bf16[2,208,1024]{2,1,0:T(8,128)(2,1)}, bf16[2,1024,256]{2,1,0:T(8,128)(2,1)}, bf16[2,320,512]{2,1,0:T(8,128)(2,1)}, bf16[2,128,1536]{2,1,0:T(8,128)(2...) custom-call(bf16[128,1024]{1,0:T(8,128)(2,1)} %refs_0_.3, ...), custom_call_target="tpu_custom_call" | custom-call | bytes 15728640 | tf_op jit(solution)/shard_map/pack/pallas_call | solution.py:636
  13.4 1.7 %collective-permute-start.7 = (bf16[208,1024]{1,0:T(8,128)(2,1)}, bf16[208,1024]{1,0:T(8,128)(2,1)S(1)}, u32[]{:S(2)}, u32[]{:S(2)}) collective-permute-start(bf16[208,1024]{1,0:T(8,128)(2,1)} %get-tuple-element.77), channel_id=1, source_target_pairs={{0,2},{2,0},{1,3},{3,1},{4,6},{6,4},{5,7},{7,5},{8,10},{10,8},{9,1... | collective-permute-start | bytes 1277960 | tf_op jit(solution)/shard_map/ppermute | solution.py:46
  16.9 3.4 %project.1 = (bf16[512,128]{1,0:T(8,128)(2,1)}, bf16[256,256]{1,0:T(8,128)(2,1)}, bf16[256,256]{1,0:T(8,128)(2,1)}, bf16[512,1024]{1,0:T(8,128)(2,1)}, bf16[32,1...) custom-call(bf16[512,256]{1,0:T(8,128)(2,1)} %embed.1.refs_0_, bf16[512,256]{1,0:T(8,128)(2,1)} %copy-done.19, ...), custom_call_target="tpu_custom_call" | custom-call | bytes 10485760 | tf_op jit(solution)/shard_map/project/pallas_call | solution.py:672
  20.3 2.9 %collective-permute-start.3 = (bf16[256,256]{1,0:T(8,128)(2,1)}, bf16[256,256]{1,0:T(8,128)(2,1)S(1)}, u32[]{:S(2)}, u32[]{:S(2)}) collective-permute-start(bf16[256,256]{1,0:T(8,128)(2,1)} %get-tuple-element.75.refs_3_), channel_id=1, source_target_pairs={{0,8},{8,12},{12,4},{4,0},{1,9},{9,13},{13,5},{5,1},{2,10},{10,14}... | collective-permute-start | bytes 393224 | tf_op jit(solution)/shard_map/ppermute | solution.py:87
  23.2 2.9 %collective-permute-start.4 = (bf16[256,256]{1,0:T(8,128)(2,1)}, bf16[256,256]{1,0:T(8,128)(2,1)S(1)}, u32[]{:S(2)}, u32[]{:S(2)}) collective-permute-start(bf16[256,256]{1,0:T(8,128)(2,1)} %get-tuple-element.76.refs_4_), channel_id=1, source_target_pairs={{0,8},{8,12},{12,4},{4,0},{1,9},{9,13},{13,5},{5,1},{2,10},{10,14}... | collective-permute-start | bytes 393224 | tf_op jit(solution)/shard_map/ppermute | solution.py:87
  27.4 2.2 %collective-permute-start.6 = (bf16[256,256]{1,0:T(8,128)(2,1)}, bf16[256,256]{1,0:T(8,128)(2,1)S(1)}, u32[]{:S(2)}, u32[]{:S(2)}) collective-permute-start(bf16[256,256]{1,0:T(8,128)(2,1)} %get-tuple-element.76.refs_4_), channel_id=1, source_target_pairs={{0,4},{8,0},{12,8},{4,12},{1,5},{9,1},{13,9},{5,13},{2,6},{10,2},{... | collective-permute-start | bytes 393224 | tf_op jit(solution)/shard_map/ppermute | solution.py:87
  29.6 3.4 %collective-permute-done.4.refs_6_ = bf16[256,256]{1,0:T(8,128)(2,1)S(1)} collective-permute-done((bf16[256,256]{1,0:T(8,128)(2,1)}, bf16[256,256]{1,0:T(8,128)(2,1)S(1)}, u32[]{:S(2)}, u32[]{:S(2)}) %collective-permute-start.4) | collective-permute-done | bytes 131104 | tf_op jit(solution)/shard_map/ppermute | solution.py:87
  33.6 2.9 %collective-permute-done.6.refs_8_ = bf16[256,256]{1,0:T(8,128)(2,1)S(1)} collective-permute-done((bf16[256,256]{1,0:T(8,128)(2,1)}, bf16[256,256]{1,0:T(8,128)(2,1)S(1)}, u32[]{:S(2)}, u32[]{:S(2)}) %collective-permute-start.6) | collective-permute-done | bytes 131104 | tf_op jit(solution)/shard_map/ppermute | solution.py:87
  36.5 2.5 %collective-permute-start.11 = (bf16[32,1152]{1,0:T(8,128)(2,1)}, bf16[32,1152]{1,0:T(8,128)(2,1)}, u32[]{:S(2)}, u32[]{:S(2)}) collective-permute-start(bf16[32,1152]{1,0:T(8,128)(2,1)} %get-tuple-element.87), channel_id=1, source_target_pairs={{0,12},{4,0},{8,4},{12,8},{1,13},{5,1},{9,5},{13,9},{2,14},{6,2},{... | collective-permute-start | bytes 221192 | tf_op jit(solution)/shard_map/ppermute | solution.py:46
  39.0 1.5 %collective-permute-start.13 = (bf16[208,1024]{1,0:T(8,128)(2,1)S(1)}, bf16[208,1024]{1,0:T(8,128)(2,1)S(1)}, u32[]{:S(2)}, u32[]{:S(2)}) collective-permute-start(bf16[208,1024]{1,0:T(8,128)(2,1)S(1)} %collective-permute-done.7.refs_7_), channel_id=1, source_target_pairs={{0,16},{16,0},{1,17},{17,1},{2,18},{18,2},{3,19},{19,3},{4,20},{20... | collective-permute-start | bytes 1277960 | tf_op jit(solution)/shard_map/ppermute | solution.py:46
  42.6 5.0 %collective-permute-done.12 = bf16[32,1152]{1,0:T(8,128)(2,1)} collective-permute-done((bf16[32,1152]{1,0:T(8,128)(2,1)}, bf16[32,1152]{1,0:T(8,128)(2,1)}, u32[]{:S(2)}, u32[]{:S(2)}) %collective-permute-start.12) | collective-permute-done | bytes 73760 | tf_op jit(solution)/shard_map/ppermute | solution.py:46
  47.6 1.9 %collective-permute-start.14 = (bf16[320,512]{1,0:T(8,128)(2,1)}, bf16[320,512]{1,0:T(8,128)(2,1)S(1)}, u32[]{:S(2)}, u32[]{:S(2)}) collective-permute-start(bf16[320,512]{1,0:T(8,128)(2,1)} %get-tuple-element.105), channel_id=1, source_target_pairs={{0,2},{2,0},{1,3},{3,1},{4,6},{6,4},{5,7},{7,5},{8,10},{10,8},{9,1... | collective-permute-start | bytes 983048 | tf_op jit(solution)/shard_map/ppermute | solution.py:46
  50.2 1.8 %collective-permute-start.18 = (bf16[128,1536]{1,0:T(8,128)(2,1)}, bf16[128,1536]{1,0:T(8,128)(2,1)S(1)}, u32[]{:S(2)}, u32[]{:S(2)}) collective-permute-start(bf16[128,1536]{1,0:T(8,128)(2,1)} %get-tuple-element.110), channel_id=1, source_target_pairs={{0,2},{2,0},{1,3},{3,1},{4,6},{6,4},{5,7},{7,5},{8,10},{10,8},{9,1... | collective-permute-start | bytes 1179656 | tf_op jit(solution)/shard_map/ppermute | solution.py:46
  54.6 1.6 %pad_maximum_fusion.1.refs_2_ = bf16[560,128]{1,0:T(8,128)(2,1)} fusion(bf16[24,128]{1,0:T(8,128)(2,1)S(1)} %slice.21, bf16[512,128]{1,0:T(8,128)(2,1)} %get-tuple-element.95, bf16[24,128]{1,0:T(8,128)(2,1)S(1)} %slice.20), kind=kLoop, calls=%fused_computation.1 | loop fusion | flops 430080 | bytes 286720 | tf_op jit(solution)/shard_map/concatenate | solution.py:712
  56.2 6.3 %attend.1 = (bf16[176,128]{1,0:T(8,128)(2,1)}, bf16[176,128]{1,0:T(8,128)(2,1)}, bf16[176,128]{1,0:T(8,128)(2,1)}, bf16[176,128]{1,0:T(8,128)(2,1)}) custom-call(s32[1]{0:T(128)S(6)} %copy.22.refs_0_, f32[2]{0:T(128)} %refs_1_.3, bf16[560,128]{1,0:T(8,128)(2,1)} %pad_maximum_fusion.1.refs_2_, bf16[256,256]{1,0:T(8,128)(2,1)} %get-tuple-element.75.refs_3_, ...), custom_call_target="tpu_custom_call" | custom-call | bytes 25165824 | tf_op jit(solution)/shard_map/attend/pallas_call | solution.py:718
  64.7 2.7 %collective-permute-done.16.refs_3_ = bf16[176,128]{1,0:T(8,128)(2,1)S(1)} collective-permute-done((bf16[176,128]{1,0:T(8,128)(2,1)}, bf16[176,128]{1,0:T(8,128)(2,1)S(1)}, u32[]{:S(2)}, u32[]{:S(2)}) %collective-permute-start.16) | collective-permute-done | bytes 45088 | tf_op jit(solution)/shard_map/ppermute | solution.py:68
  70.1 7.9 %collective-permute-done.27.refs_9_ = bf16[320,512]{1,0:T(8,128)(2,1)} collective-permute-done((bf16[320,512]{1,0:T(8,128)(2,1)S(1)}, bf16[320,512]{1,0:T(8,128)(2,1)}, u32[]{:S(2)}, u32[]{:S(2)}) %collective-permute-start.27) | collective-permute-done | bytes 327712 | tf_op jit(solution)/shard_map/ppermute | solution.py:46
  78.0 1.6 %collective-permute-done.28.refs_10_ = bf16[320,512]{1,0:T(8,128)(2,1)S(1)} collective-permute-done((bf16[320,512]{1,0:T(8,128)(2,1)S(1)}, bf16[320,512]{1,0:T(8,128)(2,1)S(1)}, u32[]{:S(2)}, u32[]{:S(2)}) %collective-permute-start.28) | collective-permute-done | bytes 327712 | tf_op jit(solution)/shard_map/ppermute | solution.py:46
  81.8 9.5 %collective-permute-done.31.refs_15_ = bf16[128,1536]{1,0:T(8,128)(2,1)} collective-permute-done((bf16[128,1536]{1,0:T(8,128)(2,1)S(1)}, bf16[128,1536]{1,0:T(8,128)(2,1)}, u32[]{:S(2)}, u32[]{:S(2)}) %collective-permute-start.31) | collective-permute-done | bytes 393248 | tf_op jit(solution)/shard_map/ppermute | solution.py:46
  96.3 7.9 %conv.1 = (bf16[128,1024]{1,0:T(8,128)(2,1)}, bf16[144,1024]{1,0:T(8,128)(2,1)}) custom-call(bf16[560,1024]{1,0:T(8,128)(2,1)} %pad_maximum_fusion.refs_0_, bf16[176,128]{1,0:T(8,128)(2,1)} %get-tuple-element.111.refs_1_, bf16[176,128]{1,0:T(8,128)(2,1)} %copy-done.27, bf16[176,128]{1,0:T(8,128)(2,1)} %copy-done.28, bf16[176,128]{1,0:T(8,128)(2,1)} %copy-done.29, ...), custom_call_target="tpu_custom_call" | custom-call | bytes 18874368 | tf_op jit(solution)/shard_map/conv/pallas_call | solution.py:750
  105.2 7.4 %vocoder.1 = f32[128,320]{1,0:T(8,128)} custom-call(s32[1]{0:T(128)S(6)} %copy.22.refs_0_, bf16[144,1024]{1,0:T(8,128)(2,1)} %get-tuple-element.121.refs_1_, f32[7,512]{1,0:T(8,128)} %refs_2_.3, f32[1,1536]{1,0:T(1,128)} %bitcast.7, bf16[1536,1536]{1,0:T(8,128)(2,1)} %constant.7.clone.refs_4_, f32[4,384]{1,0:T(4,128)} %constant.8.clone.refs_5_, ...), custom_call_target="tpu_custom_call" | custom-call | bytes 18874368 | tf_op jit(solution)/shard_map/vocoder/pallas_call | solution.py:771
  112.6 1.7 %reshape.15 = f32[40960]{0:T(1024)} reshape(f32[128,320]{1,0:T(8,128)} %vocoder.1) | data formatting | bytes 327680 | tf_op jit(solution)/shard_map/reshape | solution.py:798
  (122 shorter events, 21.7 us)
Async XLA Ops:
  4.0 9.4 %collective-permute-start.1 = (bf16[512,256]{1,0:T(8,128)(2,1)}, bf16[512,256]{1,0:T(8,128)(2,1)S(1)}, u32[]{:S(2)}, u32[]{:S(2)}) collective-permute-start(bf16[512,256]{1,0:T(8,128)(2,1)} %embed.1.refs_0_), channel_id=1, source_target_pairs={{0,2},{2,0},{1,3},{3,1},{4,6},{6,4},{5,7},{7,5},{8,10},{10,8},{9,1... | collective-permute-start | bytes 786440 | tf_op jit(solution)/shard_map/ppermute | solution.py:46
  13.4 23.1 %collective-permute-start.7 = (bf16[208,1024]{1,0:T(8,128)(2,1)}, bf16[208,1024]{1,0:T(8,128)(2,1)S(1)}, u32[]{:S(2)}, u32[]{:S(2)}) collective-permute-start(bf16[208,1024]{1,0:T(8,128)(2,1)} %get-tuple-element.77), channel_id=1, source_target_pairs={{0,2},{2,0},{1,3},{3,1},{4,6},{6,4},{5,7},{7,5},{8,10},{10,8},{9,1... | collective-permute-start | bytes 1277960 | tf_op jit(solution)/shard_map/ppermute | solution.py:46
  15.2 34.3 %collective-permute-start.10 = (bf16[1024,256]{1,0:T(8,128)(2,1)}, bf16[1024,256]{1,0:T(8,128)(2,1)S(1)}, u32[]{:S(2)}, u32[]{:S(2)}) collective-permute-start(bf16[1024,256]{1,0:T(8,128)(2,1)} %get-tuple-element.86), channel_id=1, source_target_pairs={{0,2},{2,0},{1,3},{3,1},{4,6},{6,4},{5,7},{7,5},{8,10},{10,8},{9,1... | collective-permute-start | bytes 1572872 | tf_op jit(solution)/shard_map/ppermute | solution.py:46
  23.2 10.4 %collective-permute-start.5 = (bf16[256,256]{1,0:T(8,128)(2,1)}, bf16[256,256]{1,0:T(8,128)(2,1)S(1)}, u32[]{:S(2)}, u32[]{:S(2)}) collective-permute-start(bf16[256,256]{1,0:T(8,128)(2,1)} %get-tuple-element.75.refs_3_), channel_id=1, source_target_pairs={{0,4},{8,0},{12,8},{4,12},{1,5},{9,1},{13,9},{5,13},{2,6},{10,2},{... | collective-permute-start | bytes 393224 | tf_op jit(solution)/shard_map/ppermute | solution.py:87
  23.2 9.8 %collective-permute-start.4 = (bf16[256,256]{1,0:T(8,128)(2,1)}, bf16[256,256]{1,0:T(8,128)(2,1)S(1)}, u32[]{:S(2)}, u32[]{:S(2)}) collective-permute-start(bf16[256,256]{1,0:T(8,128)(2,1)} %get-tuple-element.76.refs_4_), channel_id=1, source_target_pairs={{0,8},{8,12},{12,4},{4,0},{1,9},{9,13},{13,5},{5,1},{2,10},{10,14}... | collective-permute-start | bytes 393224 | tf_op jit(solution)/shard_map/ppermute | solution.py:87
  27.4 9.1 %collective-permute-start.6 = (bf16[256,256]{1,0:T(8,128)(2,1)}, bf16[256,256]{1,0:T(8,128)(2,1)S(1)}, u32[]{:S(2)}, u32[]{:S(2)}) collective-permute-start(bf16[256,256]{1,0:T(8,128)(2,1)} %get-tuple-element.76.refs_4_), channel_id=1, source_target_pairs={{0,4},{8,0},{12,8},{4,12},{1,5},{9,1},{13,9},{5,13},{2,6},{10,2},{... | collective-permute-start | bytes 393224 | tf_op jit(solution)/shard_map/ppermute | solution.py:87
  39.0 23.5 %collective-permute-start.13 = (bf16[208,1024]{1,0:T(8,128)(2,1)S(1)}, bf16[208,1024]{1,0:T(8,128)(2,1)S(1)}, u32[]{:S(2)}, u32[]{:S(2)}) collective-permute-start(bf16[208,1024]{1,0:T(8,128)(2,1)S(1)} %collective-permute-done.7.refs_7_), channel_id=1, source_target_pairs={{0,16},{16,0},{1,17},{17,1},{2,18},{18,2},{3,19},{19,3},{4,20},{20... | collective-permute-start | bytes 1277960 | tf_op jit(solution)/shard_map/ppermute | solution.py:46
  40.5 8.9 %collective-permute-start.8 = (bf16[256,256]{1,0:T(8,128)(2,1)S(1)}, bf16[256,256]{1,0:T(8,128)(2,1)S(1)}, u32[]{:S(2)}, u32[]{:S(2)}) collective-permute-start(bf16[256,256]{1,0:T(8,128)(2,1)S(1)} %collective-permute-done.3.refs_5_), channel_id=1, source_target_pairs={{0,8},{8,12},{12,4},{4,0},{1,9},{9,13},{13,5},{5,1},{2,10},{10,14}... | collective-permute-start | bytes 393224 | tf_op jit(solution)/shard_map/ppermute | solution.py:87
  47.6 14.9 %collective-permute-start.14 = (bf16[320,512]{1,0:T(8,128)(2,1)}, bf16[320,512]{1,0:T(8,128)(2,1)S(1)}, u32[]{:S(2)}, u32[]{:S(2)}) collective-permute-start(bf16[320,512]{1,0:T(8,128)(2,1)} %get-tuple-element.105), channel_id=1, source_target_pairs={{0,2},{2,0},{1,3},{3,1},{4,6},{6,4},{5,7},{7,5},{8,10},{10,8},{9,1... | collective-permute-start | bytes 983048 | tf_op jit(solution)/shard_map/ppermute | solution.py:46
  50.2 19.2 %collective-permute-start.18 = (bf16[128,1536]{1,0:T(8,128)(2,1)}, bf16[128,1536]{1,0:T(8,128)(2,1)S(1)}, u32[]{:S(2)}, u32[]{:S(2)}) collective-permute-start(bf16[128,1536]{1,0:T(8,128)(2,1)} %get-tuple-element.110), channel_id=1, source_target_pairs={{0,2},{2,0},{1,3},{3,1},{4,6},{6,4},{5,7},{7,5},{8,10},{10,8},{9,1... | collective-permute-start | bytes 1179656 | tf_op jit(solution)/shard_map/ppermute | solution.py:46
  52.0 17.5 %collective-permute-start.23 = (bf16[1024,256]{1,0:T(8,128)(2,1)S(1)}, bf16[1024,256]{1,0:T(8,128)(2,1)S(1)}, u32[]{:S(2)}, u32[]{:S(2)}) collective-permute-start(bf16[1024,256]{1,0:T(8,128)(2,1)S(1)} %collective-permute-done.10.refs_13_), channel_id=1, source_target_pairs={{0,16},{16,0},{1,17},{17,1},{2,18},{18,2},{3,19},{19,3},{4,20},{20... | collective-permute-start | bytes 1572872 | tf_op jit(solution)/shard_map/ppermute | solution.py:46
  52.6 17.4 %collective-permute-start.24 = (bf16[1024,256]{1,0:T(8,128)(2,1)S(1)}, bf16[1024,256]{1,0:T(8,128)(2,1)S(1)}, u32[]{:S(2)}, u32[]{:S(2)}) collective-permute-start(bf16[1024,256]{1,0:T(8,128)(2,1)S(1)} %collective-permute-done.10.refs_13_), channel_id=1, source_target_pairs={{0,1},{1,0},{2,3},{3,2},{4,5},{5,4},{6,7},{7,6},{8,9},{9,8},{10,11... | collective-permute-start | bytes 1572872 | tf_op jit(solution)/shard_map/ppermute | solution.py:46
  67.4 13.9 %collective-permute-start.19 = (bf16[2,208,1024]{2,1,0:T(8,128)(2,1)S(1)}, bf16[2,208,1024]{2,1,0:T(8,128)(2,1)S(1)}, u32[]{:S(2)}, u32[]{:S(2)}) collective-permute-start(bf16[2,208,1024]{2,1,0:T(8,128)(2,1)S(1)} %copy-done.3), channel_id=1, source_target_pairs={{0,1},{1,0},{2,3},{3,2},{4,5},{5,4},{6,7},{7,6},{8,9},{9,8},{10,11... | collective-permute-start | bytes 2555912 | tf_op jit(solution)/shard_map/ppermute | solution.py:46
  67.9 10.1 %collective-permute-start.27 = (bf16[320,512]{1,0:T(8,128)(2,1)S(1)}, bf16[320,512]{1,0:T(8,128)(2,1)}, u32[]{:S(2)}, u32[]{:S(2)}) collective-permute-start(bf16[320,512]{1,0:T(8,128)(2,1)S(1)} %collective-permute-done.14.refs_8_), channel_id=1, source_target_pairs={{0,16},{16,0},{1,17},{17,1},{2,18},{18,2},{3,19},{19,3},{4,20},{20... | collective-permute-start | bytes 983048 | tf_op jit(solution)/shard_map/ppermute | solution.py:46
  69.4 21.9 %collective-permute-start.22 = (bf16[2,1024,256]{2,1,0:T(8,128)(2,1)S(1)}, bf16[2,1024,256]{2,1,0:T(8,128)(2,1)S(1)}, u32[]{:S(2)}, u32[]{:S(2)}) collective-permute-start(bf16[2,1024,256]{2,1,0:T(8,128)(2,1)S(1)} %copy-done), channel_id=1, source_target_pairs={{0,1},{1,0},{2,3},{3,2},{4,5},{5,4},{6,7},{7,6},{8,9},{9,8},{10,11... | collective-permute-start | bytes 3145736 | tf_op jit(solution)/shard_map/ppermute | solution.py:46
  69.5 10.2 %collective-permute-start.20 = (bf16[208,1024]{1,0:T(8,128)(2,1)S(1)}, bf16[208,1024]{1,0:T(8,128)(2,1)S(1)}, u32[]{:S(2)}, u32[]{:S(2)}) collective-permute-start(bf16[208,1024]{1,0:T(8,128)(2,1)S(1)} %collective-permute-done.7.refs_7_), channel_id=1, source_target_pairs={{0,1},{1,0},{2,3},{3,2},{4,5},{5,4},{6,7},{7,6},{8,9},{9,8},{10,11... | collective-permute-start | bytes 1277960 | tf_op jit(solution)/shard_map/ppermute | solution.py:46
  70.0 11.3 %collective-permute-start.21 = (bf16[208,1024]{1,0:T(8,128)(2,1)S(1)}, bf16[208,1024]{1,0:T(8,128)(2,1)S(1)}, u32[]{:S(2)}, u32[]{:S(2)}) collective-permute-start(bf16[208,1024]{1,0:T(8,128)(2,1)S(1)} %collective-permute-done.13.refs_8_), channel_id=1, source_target_pairs={{0,1},{1,0},{2,3},{3,2},{4,5},{5,4},{6,7},{7,6},{8,9},{9,8},{10,11... | collective-permute-start | bytes 1277960 | tf_op jit(solution)/shard_map/ppermute | solution.py:46
  79.6 12.2 %collective-permute-start.25 = (bf16[1024,256]{1,0:T(8,128)(2,1)S(1)}, bf16[1024,256]{1,0:T(8,128)(2,1)S(1)}, u32[]{:S(2)}, u32[]{:S(2)}) collective-permute-start(bf16[1024,256]{1,0:T(8,128)(2,1)S(1)} %collective-permute-done.23.refs_14_), channel_id=1, source_target_pairs={{0,1},{1,0},{2,3},{3,2},{4,5},{5,4},{6,7},{7,6},{8,9},{9,8},{10,11... | collective-permute-start | bytes 1572872 | tf_op jit(solution)/shard_map/ppermute | solution.py:46
  79.8 11.5 %collective-permute-start.31 = (bf16[128,1536]{1,0:T(8,128)(2,1)S(1)}, bf16[128,1536]{1,0:T(8,128)(2,1)}, u32[]{:S(2)}, u32[]{:S(2)}) collective-permute-start(bf16[128,1536]{1,0:T(8,128)(2,1)S(1)} %collective-permute-done.18.refs_14_), channel_id=1, source_target_pairs={{0,16},{16,0},{1,17},{17,1},{2,18},{18,2},{3,19},{19,3},{4,20},{20... | collective-permute-start | bytes 1179656 | tf_op jit(solution)/shard_map/ppermute | solution.py:46
  81.3 23.0 %collective-permute-start.30 = (bf16[2,128,1536]{2,1,0:T(8,128)(2,1)}, bf16[2,128,1536]{2,1,0:T(8,128)(2,1)}, u32[]{:S(2)}, u32[]{:S(2)}) collective-permute-start(bf16[2,128,1536]{2,1,0:T(8,128)(2,1)} %get-tuple-element.124.refs_12_), channel_id=1, source_target_pairs={{0,1},{1,0},{2,3},{3,2},{4,5},{5,4},{6,7},{7,6},{8,9},{9,8},{10,11... | collective-permute-start | bytes 2359304 | tf_op jit(solution)/shard_map/ppermute | solution.py:46
  81.3 22.9 %collective-permute-start.26 = (bf16[2,320,512]{2,1,0:T(8,128)(2,1)}, bf16[2,320,512]{2,1,0:T(8,128)(2,1)}, u32[]{:S(2)}, u32[]{:S(2)}) collective-permute-start(bf16[2,320,512]{2,1,0:T(8,128)(2,1)} %get-tuple-element.122.refs_6_), channel_id=1, source_target_pairs={{0,1},{1,0},{2,3},{3,2},{4,5},{5,4},{6,7},{7,6},{8,9},{9,8},{10,11... | collective-permute-start | bytes 1966088 | tf_op jit(solution)/shard_map/ppermute | solution.py:46
  91.3 13.0 %collective-permute-start.32 = (bf16[128,1536]{1,0:T(8,128)(2,1)S(1)}, bf16[128,1536]{1,0:T(8,128)(2,1)}, u32[]{:S(2)}, u32[]{:S(2)}) collective-permute-start(bf16[128,1536]{1,0:T(8,128)(2,1)S(1)} %collective-permute-done.18.refs_14_), channel_id=1, source_target_pairs={{0,1},{1,0},{2,3},{3,2},{4,5},{5,4},{6,7},{7,6},{8,9},{9,8},{10,11... | collective-permute-start | bytes 1179656 | tf_op jit(solution)/shard_map/ppermute | solution.py:46
  91.3 13.1 %collective-permute-start.33 = (bf16[128,1536]{1,0:T(8,128)(2,1)}, bf16[128,1536]{1,0:T(8,128)(2,1)S(1)}, u32[]{:S(2)}, u32[]{:S(2)}) collective-permute-start(bf16[128,1536]{1,0:T(8,128)(2,1)} %collective-permute-done.31.refs_15_), channel_id=1, source_target_pairs={{0,1},{1,0},{2,3},{3,2},{4,5},{5,4},{6,7},{7,6},{8,9},{9,8},{10,11... | collective-permute-start | bytes 1179656 | tf_op jit(solution)/shard_map/ppermute | solution.py:46
  92.7 11.6 %collective-permute-start.29 = (bf16[320,512]{1,0:T(8,128)(2,1)}, bf16[320,512]{1,0:T(8,128)(2,1)S(1)}, u32[]{:S(2)}, u32[]{:S(2)}) collective-permute-start(bf16[320,512]{1,0:T(8,128)(2,1)} %collective-permute-done.27.refs_9_), channel_id=1, source_target_pairs={{0,1},{1,0},{2,3},{3,2},{4,5},{5,4},{6,7},{7,6},{8,9},{9,8},{10,11... | collective-permute-start | bytes 983048 | tf_op jit(solution)/shard_map/ppermute | solution.py:46
  (41 other events, 734.8 us)

commit v2 on v1

v2 whole, which is shorter than its diff:
```python
import math

import jax
import jax.numpy as jnp
import ml_dtypes
import numpy as np
from jax import lax
from jax.experimental import pallas as pl
from jax.experimental.pallas import tpu as pltpu
from jax.sharding import PartitionSpec as P

HOP = 320
LANES = 128
ROWS = 128
COST = 2**36
EDGE = 32
VMEM_BYTES = 56 * 2**20
F32 = jnp.float32
BF16 = jnp.bfloat16
HBM = pl.BlockSpec(memory_space=pl.ANY)
VMEM = pl.BlockSpec(memory_space=pltpu.VMEM)
SMEM = pl.BlockSpec(memory_space=pltpu.SMEM)


def round_up(value, multiple):
    return -(-value // multiple) * multiple


def row_tile(rows, most):
    return max(t for t in range(16, most + 1, 16) if rows % t == 0)


def shifts():
    heads, subs = lax.axis_size("head"), lax.axis_size("sub")
    return [(dh, ds) for dh in range(heads) for ds in range(subs)]


def member(shift, sign):
    heads, subs = lax.axis_size("head"), lax.axis_size("sub")
    head = lax.rem(lax.axis_index("head") + (sign * shift[0] + heads), heads)
    sub = lax.rem(lax.axis_index("sub") + (sign * shift[1] + subs), subs)
    return head * subs + sub


def rotate(x, axis, by):
    size = lax.axis_size(axis)
    return lax.ppermute(x, axis, [(i, (i + by) % size) for i in range(size)])


def send_members(pieces):
    heads, subs = lax.axis_size("head"), lax.axis_size("sub")
    out = []
    for (dh, ds), piece in zip(shifts(), pieces):
        if dh or ds:
            perm = [
                (h * subs + s, (h + dh) % heads * subs + (s + ds) % subs)
                for h in range(heads)
                for s in range(subs)
            ]
            piece = lax.ppermute(piece, ("head", "sub"), perm)
        out.append(piece)
    return out


def together(*groups):
    flat = lax.optimization_barrier(tuple(x for g in groups for x in g))
    out, at = [], 0
    for g in groups:
        out.append(list(flat[at : at + len(g)]))
        at += len(g)
    return out


def dot(a, b):
    return jnp.dot(a, b, preferred_element_type=F32)


def normalize(parts, width):
    mean = sum(jnp.sum(p, axis=-1, keepdims=True) for p in parts) * (1.0 / width)
    parts = [p - mean for p in parts]
    var = sum(jnp.sum(p * p, axis=-1, keepdims=True) for p in parts) * (1.0 / width)
    scale = lax.rsqrt(var + 1e-05)
    return [p * scale for p in parts]


def layer_norm(values):
    return normalize([values], values.shape[-1])[0]


def call(kernel, out_shape, in_specs, out_specs, scratch, cost, name):
    return pl.pallas_call(
        kernel,
        out_shape=out_shape,
        in_specs=in_specs,
        out_specs=out_specs,
        scratch_shapes=scratch,
        compiler_params=pltpu.CompilerParams(vmem_limit_bytes=VMEM_BYTES),
        cost_estimate=pl.CostEstimate(flops=COST, bytes_accessed=0, transcendentals=0),
        name=name,
    )


def embed_kernel(tokens_ref, masked_ref, tables_ref, mask_ref, out_ref):
    rows, codes = out_ref.shape[0], tables_ref.shape[1]
    tile = LANES
    lane = lax.broadcasted_iota(jnp.int32, (tile, LANES), 1)
    mask_row = mask_ref[...].astype(F32)[None, :]

    def column(row):
        return jnp.transpose(jnp.broadcast_to(row, (LANES, tile)))

    for start in range(0, rows, tile):
        masked = column(masked_ref[:, start : start + tile]) == 1
        total = jnp.where(masked[:, :1], mask_row, 0.0)
        for level in range(3):
            ids = column(tokens_ref[level : level + 1, start : start + tile])
            if level == 2:
                ids = jnp.where(masked, -1, ids)
            hot = jnp.concatenate(
                [
                    jnp.where(ids == lane + at, 1.0, 0.0).astype(BF16)
                    for at in range(0, codes, LANES)
                ],
                axis=1,
            )
            total = total + dot(hot, tables_ref[level])
        out_ref[start : start + tile, :] = total.astype(BF16)


def unit_heads(projected, head_size):
    width = projected.shape[1]
    lane = lax.broadcasted_iota(jnp.int32, (1, width), 1)
    squares = projected * projected
    scale = jnp.zeros_like(projected)
    for at in range(0, width, head_size):
        own = (lane >= at) & (lane < at + head_size)
        total = jnp.sum(jnp.where(own, squares, 0.0), axis=-1, keepdims=True)
        scale = jnp.where(own, lax.rsqrt(total + 1e-06), scale)
    return projected * scale


def project_kernel(count, head_size, *refs):
    pieces, w_ref = refs[:count], refs[count]
    rows, piece_cols = pieces[0].shape
    cols = w_ref.shape[2]
    owners = [pl.multiple_of(member(s, -1) * piece_cols, piece_cols) for s in shifts()]
    kinds = (0, 1, 2)
    w_scr = refs[-1]
    width = w_scr.shape[1] // len(kinds)
    if width != cols:
        w_scr[...] = jnp.zeros_like(w_scr)
    for r in range(count):
        for p, kind in enumerate(kinds):
            w_scr[r * piece_cols : (r + 1) * piece_cols, p * width : p * width + cols] = w_ref[
                kind, pl.ds(owners[r], piece_cols), :
            ]
    model = count * piece_cols
    tile = row_tile(rows, 128)
    for start in range(0, rows, tile):
        at = slice(start, start + tile)
        raw = [piece[at, :] for piece in pieces]
        normed = jnp.concatenate(
            [p.astype(BF16) for p in normalize([p.astype(F32) for p in raw], model)], axis=1
        )
        proj = dot(normed, w_scr[...])
        kv = jnp.concatenate(
            [unit_heads(proj[:, -2 * width : -width], head_size), proj[:, -width:]], axis=1
        ).astype(BF16)
        q_ref, emb_ref, up_ref, down_ref = refs[count + 1 : count + 5]
        query = unit_heads(proj[:, :width], head_size).astype(BF16)
        q_ref[at, :] = query
        for r in range(count):
            emb_ref[at, pl.ds(owners[r], piece_cols)] = raw[r]
        for ref in (up_ref, down_ref):
            ref[at, :] = kv
        halo = (up_ref.shape[0] - rows) // (model // (2 * width) + 1)
        for ref, here in (
            (down_ref, slice(0, halo) if start == 0 else None),
            (up_ref, slice(tile - halo, tile) if start + tile == rows else None),
        ):
            if here is not None:
                ref[up_ref.shape[0] - halo :, :] = jnp.concatenate(
                    [query[here], jnp.zeros((halo, width), BF16)], axis=1
                )
                for c in range(model // (2 * width)):
                    lanes = slice(c * 2 * width, (c + 1) * 2 * width)
                    to = rows + c * halo
                    ref[to : to + halo, :] = emb_ref[start + here.start : start + here.stop, lanes]


def value_rows(kv, block, used, width):
    rows = kv.shape[0]
    live = block * rows + lax.broadcasted_iota(jnp.int32, (rows, 1), 0) < used
    return jnp.concatenate(
        [
            jnp.where(live, kv[:, width:].astype(F32), 0.0),
            jnp.broadcast_to(jnp.where(live, 1.0, 0.0), (rows, width)),
        ],
        axis=1,
    ).astype(BF16)


def head_lanes(width, head_size, heads):
    lane = lax.broadcasted_iota(jnp.int32, (1, width), 1)
    return [(lane >= h * head_size) & (lane < (h + 1) * head_size) for h in range(heads)]


def weigh(query, own, sharp, key, value):
    query = jnp.where(own, query, jnp.zeros_like(query))
    score = lax.dot_general(query, key, (((1,), (1,)), ((), ())), preferred_element_type=F32)
    return dot(jnp.exp2(score * sharp - sharp).astype(BF16), value)


def seq_block(hop):
    size = lax.axis_size("seq")
    return lax.rem(lax.axis_index("seq") + (hop + size), size)


def attend_part_kernel(head_size, hops, *refs):
    used_ref, temp_ref, q_ref = refs[:3]
    kv_refs = refs[3 : 3 + len(hops)]
    sums_ref = refs[3 + len(hops)] if len(refs) > 5 + len(hops) else None
    acc_ref, v_scr = refs[-2:]
    rows, width = q_ref.shape
    heads = temp_ref.shape[0]
    own = head_lanes(width, head_size, heads)
    for i, (ref, hop) in enumerate(zip(kv_refs, hops)):
        v_scr[i] = value_rows(ref[:rows, :], seq_block(hop), used_ref[0], width)
    tile = row_tile(rows, ROWS)
    for at in range(0, rows, tile):
        for h in range(heads):
            sharp = temp_ref[h] * math.log2(math.e)
            total = 0.0 if sums_ref is None else sums_ref[h, at : at + tile, :]
            for i, ref in enumerate(kv_refs):
                query = q_ref[at : at + tile, :]
                total = total + weigh(query, own[h], sharp, ref[:rows, :width], v_scr[i])
            acc_ref[h, at : at + tile, :] = total


def attend_last_kernel(head_size, halo, hops, done, out_count, slab, *refs):
    used_ref, temp_ref, q_ref, acc_ref, before_ref, after_ref = refs[:6]
    kv_refs = refs[6 : 6 + len(hops)]
    out_refs = refs[6 + len(hops) : 6 + len(hops) + out_count]
    v_scr, att_scr = refs[6 + len(hops) + out_count :]
    rows, width = q_ref.shape
    heads = temp_ref.shape[0]
    own = head_lanes(width, head_size, heads)
    for i, (ref, hop) in enumerate(zip(kv_refs, hops)):
        v_scr[i] = value_rows(ref[:rows, :], seq_block(hop), used_ref[0], width)
    tile = row_tile(rows, ROWS)
    tiles = [(at, None) for at in range(0, rows, tile)] + [(rows, (before_ref, after_ref))]
    for at, edges in tiles:
        if edges is None:
            query = q_ref[at : at + tile, :]
            blocks = range(done, len(hops))
        else:
            query = jnp.concatenate([r[r.shape[0] - halo :, :width] for r in edges], axis=0)
            blocks = range(len(hops))
        result = jnp.zeros(query.shape, F32)
        for h in range(heads):
            sharp = temp_ref[h] * math.log2(math.e)
            total = acc_ref[h, at : at + tile, :] if edges is None else 0.0
            for i in blocks:
                total = total + weigh(query, own[h], sharp, kv_refs[i][:rows, :width], v_scr[i])
            result = jnp.where(own[h], total[:, :width] / total[:, width:], result)
        result = result.astype(BF16)
        if edges is None:
            att_scr[halo + at : halo + at + tile, :] = result
        else:
            att_scr[:halo, :] = result[:halo]
            att_scr[halo + rows :, :] = result[halo:]
    for shift, out_ref in zip(shifts(), out_refs):
        start = pl.multiple_of(member(shift, 1) * slab, slab)
        out_ref[...] = att_scr[pl.ds(start, out_ref.shape[0]), : out_ref.shape[1]]


def sine_cosine(x):
    turns = jnp.floor(x * (1.0 / math.pi) + 0.5)
    r = x - turns * 3.140625
    r = r - turns * 9.67502593994140625e-4
    r = r - turns * 1.509957990978376432e-7
    sign = 1.0 - 2.0 * (turns - 2.0 * jnp.floor(turns * 0.5))
    z = r * r
    s = -2.5052108385e-08
    for c in (2.7557319224e-06, -1.9841269841e-04, 8.3333333333e-03, -1.6666666667e-01):
        s = s * z + c
    c_ = 2.0876756988e-09
    for c in (-2.7557319224e-07, 2.4801587302e-05, -1.3888888889e-03, 4.1666666667e-02, -0.5):
        c_ = c_ * z + c
    return sign * (r + r * z * s), sign * (1.0 + z * c_)


def pack_kernel(*refs):
    attn_out, conv_in, conv_out, voc_in, voc_up, voc_down, conv_kernel, head = refs[:8]
    own_first, own_rest, mine_first, mine_rest = refs[8:12]
    k_scr, head_scr, sems = refs[12:]
    group = lax.axis_index("groups") % 2
    taps, split = conv_kernel.shape
    kernel = conv_kernel[...]
    upper = kernel.astype(BF16)
    lower = (kernel - upper.astype(F32)).astype(BF16)
    blank = jnp.zeros((k_scr.shape[0] - taps, split), BF16)
    k_scr[...] = jnp.concatenate(
        [
            jnp.concatenate([upper, blank], axis=0),
            jnp.concatenate([lower, blank], axis=0),
            jnp.zeros((k_scr.shape[0], k_scr.shape[1] - 2 * split), BF16),
        ],
        axis=1,
    )
    bins, rows = head.shape[0] // 2, head.shape[1]
    padded = head_scr.shape[1] // 2
    blank = jnp.zeros((padded - bins, rows), F32)
    values = head[...].astype(F32)
    values = jnp.concatenate([values[:bins], blank, values[bins:], blank], axis=0)
    head_scr[...] = jnp.transpose(values).astype(BF16)
    chunks = (
        ((attn_out, conv_out, k_scr), own_first, 0, mine_first),
        ((voc_in, voc_down, voc_up, head_scr), own_rest, 0, mine_rest),
    )
    copies = []
    for sources, own, base, mine in chunks:
        for side in range(2):
            half = lax.rem(group + side, 2)
            start = 0
            for src in sources:
                part = src.shape[0] // 2
                cols = mine.shape[1]
                for c in range(src.shape[1] // cols):
                    piece = src.at[
                        pl.ds(pl.multiple_of(half * part, part), part), pl.ds(c * cols, cols)
                    ]
                    copies.append((piece, own.at[side, pl.ds(base + start, part), :]))
                    if side == 0:
                        copies.append((piece, mine.at[pl.ds(start, part), :]))
                    start += part
    start = own_first.shape[1]
    deep, cols = conv_in.shape[1:]
    part = mine_first.shape[0] - start
    for c in range(mine_first.shape[1] // cols):
        copies.append(
            (
                conv_in.at[group, pl.ds(deep // 2 + c * part, part), :],
                mine_first.at[pl.ds(start, part), pl.ds(c * cols, cols)],
            )
        )
    copies = [pltpu.make_async_copy(a, b, sems.at[i]) for i, (a, b) in enumerate(copies)]
    for copy in copies:
        copy.start()
    for copy in copies:
        copy.wait()


def fetcher(chunks, sems):
    group = lax.axis_index("groups") % 2
    subs = lax.axis_size("sub")
    copies = {}
    used = [0]

    def fetch(
        kind, r, chunk, start, part, dst, base, stride=None, cols=None, lanes=None
    ):
        copies[kind, r] = []
        pieces = chunks[chunk][r]
        here = r < subs
        for side in range(2):
            half = lax.rem(group + side, 2)
            if len(pieces) == 2:
                src = pieces[side]
            else:
                src = pieces[0]
                src = src.at[half if here and stride else side]
            to = pl.ds(pl.multiple_of(base + half * (stride or part), part), part)
            for c in range(dst.shape[1] // cols if cols else 1):
                target = dst.at[to, pl.ds(c * cols, cols)] if cols else dst.at[to, :]
                source = src.at[pl.ds(start + c * part, part), pl.ds(*lanes) if lanes else slice(None)]
                copy = pltpu.make_async_copy(source, target, sems.at[used[0]])
                used[0] += 1
                copy.start()
                copies[kind, r].append(copy)

    def ready(kind, r):
        for copy in copies[kind, r]:
            copy.wait()

    return fetch, ready


def weight_pairs(refs, chunk_count):
    chunks, at = [], 0
    for _ in range(chunk_count):
        pairs = []
        for dh in range(lax.axis_size("head")):
            for ds in range(lax.axis_size("sub")):
                taken = 2 if dh and not ds else 1
                pairs.append(refs[at : at + taken])
                at += taken
        chunks.append(pairs)
    return chunks, refs[at:]


def first_frame(slab):
    count = lax.axis_size("head") * lax.axis_size("sub")
    return (lax.axis_index("seq") * count + member((0, 0), 1)) * slab


def conv_kernel_body(geo, *refs):
    count, halo, rim, taps = geo
    emb_ref, before_ref, after_ref = refs[:3]
    att_refs = refs[3 : 3 + count]
    chunks, refs = weight_pairs(refs[3 + count :], 2)
    feat_ref, window_ref, emb_scr, w_out, w_conv, k_conv, w_mix, stream_scr, gate_scr, sems = refs
    win, model = emb_scr.shape
    slab = feat_ref.shape[0]
    first = first_frame(slab)
    total_frames = lax.axis_size("seq") * count * slab
    me = member((0, 0), 1)
    rows = emb_ref.shape[0]
    own = win - halo
    cols = before_ref.shape[1]
    window = []
    for c in range(model // cols):
        piece, lanes = pl.ds(rows + c * halo, halo), pl.ds(c * cols, cols)
        window += [
            (me == 0, before_ref.at[piece, :], emb_scr.at[pl.ds(0, halo), lanes]),
            (me == count - 1, after_ref.at[piece, :], emb_scr.at[pl.ds(own, halo), lanes]),
        ]
    window += [
        (me == 0, emb_ref.at[pl.ds(0, own), :], emb_scr.at[pl.ds(halo, own), :]),
        (me == count - 1, emb_ref.at[pl.ds(rows - own, own), :], emb_scr.at[pl.ds(0, own), :]),
        (
            (me > 0) & (me < count - 1),
            emb_ref.at[pl.ds(pl.multiple_of(jnp.clip(me * slab - halo, 0, rows - win), halo), win), :],
            emb_scr,
        ),
    ]

    def window_copies(act):
        for at, (here, src, dst) in enumerate(window):
            copy = pltpu.make_async_copy(src, dst, sems.at[18 * count + at])
            pl.when(here)(lambda copy=copy: getattr(copy, act)())

    window_copies("start")
    fetch, ready = fetcher(chunks, sems)
    out_half = w_out.shape[0] // count // 2
    mix_half = w_mix.shape[1] // 2
    tap_half = k_conv.shape[1] // 2
    deep = w_conv.shape[1] // 2
    step = deep // 2
    low_rows = step // (model // w_conv.shape[2])

    def fetch_low(r):
        at = out_half + mix_half + tap_half
        for c in range(step // low_rows):
            lanes = (c * w_conv.shape[2], w_conv.shape[2])
            fetch(
                ("low", c), r, 0, at, low_rows, w_conv.at[r], step + c * low_rows, deep, lanes=lanes
            )

    def ready_low(r):
        if r < lax.axis_size("sub"):
            ready("low", r)
        else:
            for c in range(step // low_rows):
                ready(("low", c), r)

    for r in range(count):
        fetch("out", r, 0, 0, out_half, w_out, r * 2 * out_half)
    for r in range(count):
        fetch("top", r, 1, 0, step, w_conv.at[r], 0, deep)
        if r < lax.axis_size("sub"):
            fetch("low", r, 1, step, step, w_conv.at[r], step, deep)
        else:
            fetch_low(r)
        fetch("taps", r, 0, out_half + mix_half, tap_half, k_conv.at[r], 0)
        fetch("mix", r, 0, out_half, mix_half, w_mix.at[r], 0)

    attended = jnp.concatenate([ref[...] for ref in att_refs], axis=1)
    window_copies("wait")
    for r in range(count):
        ready("out", r)
    frames = first - halo + lax.broadcasted_iota(jnp.int32, (win, 1), 0)
    inside = (frames >= 0) & (frames < total_frames)
    stream = jnp.where(inside, emb_scr[...].astype(F32) + dot(attended, w_out[...]), 0.0)
    stream_scr[...] = stream
    conv_normed = layer_norm(stream).astype(BF16)

    mid = slab + 2 * rim
    group_cols = w_conv.shape[2]
    lead = halo - rim - taps // 2
    conv_sum = jnp.zeros((mid, model), F32)
    for r in range(count):
        ready("top", r)
        ready_low(r)
        signal = dot(conv_normed, w_conv[r, deep:, :])
        gated = dot(conv_normed, w_conv[r, :deep, :]) * jax.nn.sigmoid(signal)
        gated = gated.astype(BF16).astype(F32)
        ready("taps", r)
        kernel = k_conv[r, :, : 2 * group_cols].astype(F32)
        kernel = kernel[:, :group_cols] + kernel[:, group_cols:]
        active = []
        for c in range(group_cols // LANES):
            lanes = slice(c * LANES, (c + 1) * LANES)
            gate_scr[c] = gated[:, lanes]
            depth = jnp.zeros((mid, LANES), F32)
            for k in range(taps):
                depth = depth + kernel[k : k + 1, lanes] * gate_scr[c, lead + k : lead + k + mid, :]
            active.append((depth * jax.nn.sigmoid(depth)).astype(BF16))
        ready("mix", r)
        part = dot(jnp.concatenate(active, axis=1), w_mix[r])
        conv_sum = conv_sum + part.astype(BF16).astype(F32)
    features = layer_norm(stream_scr[halo - rim : halo - rim + mid, :] + conv_sum).astype(BF16)
    feat_ref[...] = features[rim : rim + slab]
    window_ref[...] = features


def voc_kernel_body(geo, *refs):
    count, rim, half_voc = geo
    used_ref, window_ref, voc_kernel_ref, bias_ref, table_ref, hann_ref = refs[:6]
    chunks, refs = weight_pairs(refs[6:], 1)
    wave_ref, w_vin, w_up, w_down, w_head, w_table, base_scr, wave_scr, out_scr, sems = refs
    slab = out_scr.shape[1]
    first = first_frame(slab)
    total_frames = lax.axis_size("seq") * count * slab
    used = used_ref[0]
    owners = [member(s, -1) for s in shifts()]
    fetch, ready = fetcher(chunks, sems)
    vin_half = w_vin.shape[0] // count // 2
    down_half = w_down.shape[0] // count // 2
    up_half = w_up.shape[0] // count // 2
    head_half = w_head.shape[0] // count // 2
    voc = w_vin.shape[1]
    rest = vin_half + down_half
    for r in range(count):
        fetch("vin", r, 0, 0, vin_half, w_vin, owners[r] * 2 * vin_half)
    for r in range(count):
        fetch(
            "up", r, 0, rest, up_half, w_up, owners[r] * 2 * up_half, cols=voc
        )
    for r in range(count):
        fetch("down", r, 0, vin_half, down_half, w_down, owners[r] * 2 * down_half)
    for r in range(count):
        at = up_half * (w_up.shape[1] // voc)
        fetch(
            "head",
            r,
            0,
            rest + at,
            head_half,
            w_head,
            owners[r] * 2 * head_half,
            cols=voc,
        )
    table_copy = pltpu.make_async_copy(table_ref, w_table, sems.at[sems.shape[0] - 1])
    table_copy.start()
    features = window_ref[...]
    mid = features.shape[0]

    for r in range(count):
        ready("vin", r)
    ids = first - rim + lax.broadcasted_iota(jnp.int32, (mid, 1), 0)
    live = (ids >= 0) & (ids < used)
    base = layer_norm(jnp.where(live, dot(features, w_vin[...]), 0.0))
    voc = base.shape[1]
    trim = half_voc + 1
    rows = mid - 2 * trim
    depth = []
    for c in range(voc // LANES):
        lanes = slice(c * LANES, (c + 1) * LANES)
        base_scr[c] = base[:, lanes]
        total = jnp.zeros((rows, LANES), F32)
        for k in range(2 * half_voc + 1):
            total = total + voc_kernel_ref[k : k + 1, lanes] * base_scr[c, 1 + k : 1 + k + rows, :]
        depth.append(total)
    inner = jnp.concatenate(
        [p.astype(BF16) for p in normalize(depth, voc)], axis=1
    )
    for r in range(count):
        ready("up", r)
    up = dot(inner, w_up[...])
    hidden = (0.5 * up * (1.0 + lax.erf(up * math.sqrt(0.5)))).astype(BF16)
    for r in range(count):
        ready("down", r)
    center = jnp.concatenate(
        [base_scr[c, trim : trim + rows, :] for c in range(voc // LANES)], axis=1
    )
    head_input = layer_norm(center + dot(hidden, w_down[...])).astype(BF16)
    for r in range(count):
        ready("head", r)
    spectrum = dot(head_input, w_head[...]) + bias_ref[...]
    bins = spectrum.shape[1] // 2
    magnitude = jnp.minimum(jnp.exp(spectrum[:, :bins]), 100.0)
    sine, cosine = sine_cosine(spectrum[:, bins:])
    coefficients = jnp.concatenate([magnitude * cosine, magnitude * sine], axis=1).astype(BF16)
    table_copy.wait()
    ids = first - rim + trim + lax.broadcasted_iota(jnp.int32, (rows, 1), 0)
    exists = jnp.where((ids >= 0) & (ids < total_frames), 1.0, 0.0)
    parts = wave_scr.shape[0]
    span = wave_scr.shape[2]
    for q in range(parts):
        wave_scr[q] = exists * dot(coefficients, w_table[:, q * span : (q + 1) * span])
    audio = jnp.zeros((slab, span), F32)
    energy = jnp.zeros((slab, span), F32)
    for q in range(parts):
        begin = rim - trim + parts // 2 - q
        audio = audio + wave_scr[q, begin : begin + slab, :]
        energy = energy + exists[begin : begin + slab] * hann_ref[q : q + 1, :]
    audio = audio / energy
    tiles = range(span // LANES)
    for c in tiles:
        out_scr[c] = audio[:, c * LANES : (c + 1) * LANES]
    even, odd = (
        jnp.concatenate([out_scr[c, pl.ds(at, slab // 2, stride=2), :] for c in tiles], axis=1)
        for at in range(2)
    )
    samples = jnp.concatenate([even[:, :HOP], odd[:, :HOP]], axis=1)
    count = 2 * HOP // LANES
    for c in range(count):
        wave_ref[pl.ds(c, slab // 2, stride=count), :] = samples[:, c * LANES : (c + 1) * LANES]


def synthesis(bins, padded, span):
    size = 2 * (bins - 1)
    parts = size // HOP
    k = np.arange(bins)[:, None]
    n = np.arange(size)[None, :]
    angle = 2.0 * np.pi / size * (k * n % size)
    hann = 0.5 - 0.5 * np.cos(2.0 * np.pi / size * np.arange(size))
    edge = (k == 0) | (k == bins - 1)
    factor = np.where(edge, 1.0, 2.0) / size * hann[None, :]
    both = (factor * np.cos(angle), np.where(edge, 0.0, -factor * np.sin(angle)))
    table = np.zeros((2, padded, parts, span), np.float32)
    for at, values in enumerate(both):
        table[at, :bins, :, :HOP] = values.reshape(bins, parts, HOP)
    squares = np.ones((parts, span), np.float32)
    squares[:, :HOP] = (hann * hann).reshape(parts, HOP)
    return table.reshape(2 * padded, parts * span).astype(ml_dtypes.bfloat16), squares


def local(
    tokens,
    masked,
    used_frames,
    tables,
    mask_vec,
    attn_in,
    head_temp,
    attn_out,
    conv_in,
    conv_kernel,
    conv_out,
    voc_in,
    voc_kernel,
    voc_up,
    voc_down,
    voc_head,
    head_bias,
):
    frame_count = tokens.shape[1]
    count = lax.axis_size("head") * lax.axis_size("sub")
    seq_size = lax.axis_size("seq")
    model = attn_in.shape[1]
    piece_cols = tables.shape[2]
    cols = attn_in.shape[2]
    width = round_up(cols, LANES)
    head_size = cols // head_temp.shape[0]
    slab = frame_count // count
    bins = head_bias.shape[0] // 2
    half_voc = voc_kernel.shape[0] // 2
    parts = 2 * (bins - 1) // HOP
    rim = round_up(half_voc + parts // 2, 8)
    halo = round_up(half_voc + parts // 2 + conv_kernel.shape[0] // 2, EDGE)
    win = slab + 2 * halo
    mid = slab + 2 * rim
    taps = conv_kernel.shape[0]

    others = range(1, lax.axis_size("head"))
    group = lax.rem(lax.axis_index("groups"), 2)
    deep = conv_in.shape[1]

    def cross(x):
        return [rotate(x, "head", dh) for dh in others]

    def spread(xs):
        return [rotate(x, "groups", 1) for x in xs]

    def share(xs):
        return [rotate(x, "sub", 1) for x in xs]

    def share_both(kind):
        return share([jnp.stack(pair) for pair in zip(near[kind], far[kind])])

    near, far, both, own, own_sub, mine = {}, {}, {}, {}, {}, {}
    mine["top"] = lax.dynamic_slice(
        conv_in, (group, 0, 0), (1, deep // 2, conv_in.shape[2])
    ).reshape(deep // 2, conv_in.shape[2])
    own["b"] = conv_in
    near["top"] = cross(mine["top"])
    own_sub["b"] = share([own["b"]])

    embedded = call(
        embed_kernel,
        jax.ShapeDtypeStruct((frame_count, piece_cols), BF16),
        [VMEM] * 4,
        VMEM,
        [],
        9,
        "embed",
    )(tokens, masked[None, :], tables, mask_vec)
    crossed = cross(embedded)
    beside = share([embedded])
    [conv_kernel], [embedded], near["top"] = together([conv_kernel], [embedded], near["top"])

    padded = round_up(bins, LANES)
    gap = ((0, 0), (0, padded - bins))
    bias = jnp.pad(head_bias.reshape(2, bins), gap).reshape(1, 2 * padded)
    tap_rows = round_up(taps, 32)
    voc = voc_in.shape[1]
    first_rows = (attn_out.shape[0] + conv_out.shape[0] + tap_rows) // 2
    low_rows = deep // 2 * conv_in.shape[2] // model
    conv_rows = (voc_in.shape[0] + voc_down.shape[0]) // 2
    head_rows = (voc_up.shape[0] * voc_up.shape[1] + voc_head.shape[0] * 2 * padded) // voc // 2
    packed = call(
        pack_kernel,
        [
            jax.ShapeDtypeStruct((2, first_rows, model), BF16),
            jax.ShapeDtypeStruct((2, conv_rows + head_rows, voc), BF16),
            jax.ShapeDtypeStruct((first_rows + low_rows, model), BF16),
            jax.ShapeDtypeStruct((conv_rows + head_rows, voc), BF16),
        ],
        [HBM] * 6 + [VMEM] * 2,
        [VMEM] * 4,
        [
            pltpu.VMEM((tap_rows, model), BF16),
            pltpu.VMEM((voc_head.shape[0], 2 * padded), BF16),
            pltpu.SemaphoreType.DMA((48,)),
        ],
        15,
        "pack",
    )(attn_out, conv_in, conv_out, voc_in, voc_up, voc_down, conv_kernel, voc_head.T)

    crossed, beside, own_sub["b"], packed = together(crossed, beside, own_sub["b"], packed)
    own["a"], own["c"], mine["a"], mine["c"] = packed

    def members(own_piece, beside_piece, others_pieces):
        pieces = [own_piece] + beside_piece
        for piece in others_pieces:
            pieces += [piece] + share([piece])
        return pieces

    pieces = members(embedded, beside, crossed)
    far["top"] = spread(near["top"])
    near["a"] = cross(mine["a"])
    chunk = 2 * width
    message = (frame_count + (model // chunk + 1) * halo, chunk)
    q_own, emb, upward, downward = call(
        lambda *refs: project_kernel(count, head_size, *refs),
        (
            jax.ShapeDtypeStruct((frame_count, width), BF16),
            jax.ShapeDtypeStruct((frame_count, model), BF16),
            jax.ShapeDtypeStruct(message, BF16),
            jax.ShapeDtypeStruct(message, BF16),
        ),
        [VMEM] * (count + 1),
        (VMEM,) * 4,
        [pltpu.VMEM((model, 3 * width), BF16)],
        10,
        "project",
    )(*pieces, attn_in)

    below, above = rotate(upward, "seq", 1), rotate(downward, "seq", -1)
    heads = head_temp.shape[0]

    def attend(hops, blocks, sums):
        return call(
            lambda *refs: attend_part_kernel(head_size, hops, *refs),
            jax.ShapeDtypeStruct((heads, frame_count, chunk), F32),
            [SMEM, SMEM] + [VMEM] * (1 + len(blocks) + len(sums)),
            VMEM,
            [pltpu.VMEM((len(blocks), frame_count, chunk), BF16)],
            10,
            "attend",
        )(used_frames, head_temp, q_own, *blocks, *sums)

    sums = attend([0], [upward], [])
    [below, sums, mine["c"]], near["a"], far["top"] = together(
        [below, sums, mine["c"]], near["a"], far["top"]
    )
    blocks, hops = [upward, below, above], [0, -1, 1]
    ahead, behind = below[:frame_count], above[:frame_count]
    for hop in range(2, seq_size // 2 + 1):
        ahead = rotate(ahead, "seq", 1)
        blocks.append(ahead)
        hops.append(-hop)
        if 2 * hop < seq_size:
            behind = rotate(behind, "seq", -1)
            blocks.append(behind)
            hops.append(hop)
    far["a"], near["c"] = spread(near["a"]), cross(mine["c"])
    sums = attend([-1], [below], [sums])

    sums = attend([1], [above], [sums])
    last, [sums, own["a"], own["c"]], near["top"], far["top"] = together(
        blocks[3:], [sums, own["a"], own["c"]], near["top"], far["top"]
    )
    blocks[3:] = last
    own_sub["a"], own_sub["c"] = share([own["a"]]), share([own["c"]])
    both["top"] = share_both("top")
    windows = call(
        lambda *refs: attend_last_kernel(head_size, halo, hops, 3, count, slab, *refs),
        (jax.ShapeDtypeStruct((win, cols), BF16),) * count,
        [SMEM, SMEM] + [VMEM] * (4 + len(blocks)),
        (VMEM,) * count,
        [
            pltpu.VMEM((len(blocks), frame_count, chunk), BF16),
            pltpu.VMEM((frame_count + 2 * halo, width), BF16),
        ],
        10,
        "attend_last",
    )(used_frames, head_temp, q_own, sums, below, above, *blocks)

    windows, far["a"], near["c"], both["top"], own_sub["a"], own_sub["c"] = together(
        windows, far["a"], near["c"], both["top"], own_sub["a"], own_sub["c"]
    )
    attended = send_members(windows)
    both["a"] = share_both("a")
    far["c"] = spread(near["c"])
    own["top"], own_sub["top"] = own["b"], own_sub["b"]

    def weights(kind):
        found = [own[kind], *own_sub[kind]]
        for dh in range(len(others)):
            found += [t[kind][dh] for t in (near, far, both)]
        return found

    conv_weights = [w for kind in ("a", "top") for w in weights(kind)]
    span = round_up(HOP, LANES)
    table, squares = synthesis(bins, padded, span)
    features, window = call(
        lambda *refs: conv_kernel_body((count, halo, rim, taps), *refs),
        (
            jax.ShapeDtypeStruct((slab, model), BF16),
            jax.ShapeDtypeStruct((mid, model), BF16),
        ),
        [HBM] * 3 + [VMEM] * count + [HBM] * len(conv_weights),
        (VMEM, VMEM),
        [
            pltpu.VMEM((win, model), BF16),
            pltpu.VMEM((count * cols, model), BF16),
            pltpu.VMEM((count, 2 * deep, conv_in.shape[2]), BF16),
            pltpu.VMEM((count, tap_rows, model), BF16),
            pltpu.VMEM((count,) + conv_out.shape, BF16),
            pltpu.VMEM((win, model), F32),
            pltpu.VMEM((conv_in.shape[2] // LANES, win, LANES), F32),
            pltpu.SemaphoreType.DMA((10 * count + 3 + 2 * model // (2 * width) + 8 * count,)),
        ],
        18,
        "conv",
    )(emb, below, above, *attended, *conv_weights)
    [window], far["c"] = together([window], far["c"])
    both["c"] = share_both("c")
    voc_weights = weights("c")
    wave = call(
        lambda *refs: voc_kernel_body((count, rim, half_voc), *refs),
        jax.ShapeDtypeStruct((slab * HOP // LANES, LANES), F32),
        [SMEM] + [VMEM] * 3 + [HBM, VMEM] + [HBM] * len(voc_weights),
        VMEM,
        [
            pltpu.VMEM((count * voc_in.shape[0], voc), BF16),
            pltpu.VMEM((count * voc_up.shape[0], voc_up.shape[1]), BF16),
            pltpu.VMEM((count * voc_down.shape[0], voc), BF16),
            pltpu.VMEM((count * voc_head.shape[0], 2 * padded), BF16),
            pltpu.VMEM(table.shape, BF16),
            pltpu.VMEM((voc // LANES, mid, LANES), F32),
            pltpu.VMEM((parts, mid - 2 * (half_voc + 1), span), F32),
            pltpu.VMEM((span // LANES, slab, LANES), F32),
            pltpu.SemaphoreType.DMA((4 * count + 4 * count * (voc_up.shape[1] // voc) + 1,)),
        ],
        18,
        "vocoder",
    )(
        used_frames,
        window,
        voc_kernel,
        bias,
        jnp.asarray(table),
        jnp.asarray(squares),
        *voc_weights,
    )
    return features, wave.reshape(slab * HOP)


def solution(mesh):
    in_specs = (
        P(None, ("groups", "seq")),
        P(("groups", "seq")),
        P("groups"),
        P(None, None, ("head", "sub")),
        P(("head", "sub")),
        P(None, None, ("head", "sub")),
        P(("head", "sub")),
        P(("head", "sub"), None),
        P(None, None, ("head", "sub")),
        P(None, ("head", "sub")),
        P(("head", "sub"), None),
        P(("head", "sub"), None),
        P(),
        P(("head", "sub"), None),
        P(("head", "sub"), None),
        P(("head", "sub"), None),
        P(),
    )
    out_specs = (P(("groups", "seq", "head", "sub"), None), P(("groups", "seq", "head", "sub")))
    return jax.shard_map(local, mesh=mesh, in_specs=in_specs, out_specs=out_specs, check_vma=False)
```

time: 116 us -> 93 us (0.80); the launches traced: 114 us -> 92.5 us
  waiting for transfers between devices: 38.1 us -> 24.8 us
  starting transfers between devices: 29 us -> 17.1 us
  Pallas kernels: 34.3 us -> 42.2 us
  other arithmetic: 2.7 us -> 0.31 us
  local copies, waits for them, and re-layouts: 8.59 us -> 6.41 us
    ppermute x6 -> x0, starting transfers between devices: 9.26 us -> none  [ring_send(): lax.ppermute(x, 'seq', [(order[i], order[(i + by) % size]) for i in range...]
    ppermute x6 -> x0, waiting for transfers between devices: 8.89 us -> none  [ring_send(): lax.ppermute(x, 'seq', [(order[i], order[(i + by) % size]) for i in range...]
    pallas_call x2 -> x5, Pallas kernels: 12.2 us -> 18.8 us  [the longest x3 9.29 us: attend(): call(lambda *refs: attend_part_kernel(head_size, hops, *refs), jax.ShapeD...]
    ppermute x25 -> x18, starting transfers between devices: 18.2 us -> 15 us  [rotate(): return lax.ppermute(x, axis, [(i, (i + by) % size) for i in range(size)])]
    ppermute x25 -> x18, waiting for transfers between devices: 25.5 us -> 22.4 us  [rotate(): return lax.ppermute(x, axis, [(i, (i + by) % size) for i in range(size)])]
    slice x4 -> x1, local copies, waits for them, and re-layouts: 2.99 us -> 0.02 us  [local(): ahead, behind = (below[:frame_count], above[:frame_count])]
    concatenate x2 -> x0, other arithmetic: 2.7 us -> none  [the longest x1 1.57 us: local(): jnp.concatenate([before[:, model:], q_own, after[:, model:]], axis=0)]
    unnamed x64 -> x58, local copies, waits for them, and re-layouts: 3.81 us -> 5.34 us
  transfers between devices with their start and end apart: 34 -> 21, of which waited for: 14 -> 10; matrix products, arithmetic and copies ran while one was open for 6% -> 1% of each run, Pallas kernels for 21% -> 37%
where the time goes in v2:
time: 93 us; the launch traced here: 92.5 us
  Pallas kernels  42.2 us (45%)
  waiting for transfers between devices  24.8 us (27%)
  starting transfers between devices  17.1 us (18%)
  local copies, waits for them, and re-layouts  6.41 us (7%)
  between operations  1.73 us (2%)
    ppermute x18, waiting for transfers between devices, rotate(): return lax.ppermute(x, axis, [(i, (i + by) % size) for i in range(size)])  22.4 us
    ppermute x18, starting transfers between devices, rotate(): return lax.ppermute(x, axis, [(i, (i + by) % size) for i in range(size)])  15 us
    pallas_call x3, Pallas kernels, attend(): call(lambda *refs: attend_part_kernel(head_size, hops, *refs), jax.ShapeD...  9.29 us
    pallas_call x1, Pallas kernels, local(): call(lambda *refs: conv_kernel_body((count, halo, rim, taps), *refs), (ja...  8.56 us
    pallas_call x1, Pallas kernels, local(): call(lambda *refs: voc_kernel_body((count, rim, half_voc), *refs), jax.Sh...  7.72 us
    unnamed x58, local copies, waits for them, and re-layouts  5.34 us
    pallas_call x1, Pallas kernels, local(): call(pack_kernel, [jax.ShapeDtypeStruct((2, first_rows, model), BF16), ja...  5.31 us
    pallas_call x1, Pallas kernels, local(): call(lambda *refs: attend_last_kernel(head_size, halo, hops, 3, count, sl...  4.18 us
  transfers between devices with their start and end apart: 21, of which 10 were waited for; matrix products, arithmetic and copies ran while one was open for 1% of the time, Pallas kernels for 37%

profile of v2, /device:TPU:0, one launch (start us, length us, event | category | flops | bytes accessed | tf_op | source)
XLA Modules:
  0.0 92.5 jit_solution(2694324562791614610)
XLA Ops:
  1.6 3.0 %collective-permute-start = (bf16[512,256]{1,0:T(8,128)(2,1)S(1)}, bf16[512,256]{1,0:T(8,128)(2,1)S(1)}, u32[]{:S(2)}, u32[]{:S(2)}) collective-permute-start(bf16[512,256]{1,0:T(8,128)(2,1)S(1)} %dynamic-slice_bitcast_fusion), channel_id=1, source_target_pairs={{0,2},{2,0},{1,3},{3,1},{4,6},{6,4},{5,7},{7,5},{8,10},{10,8},{9,1... | collective-permute-start | bytes 786440 | tf_op jit(solution)/shard_map/ppermute | solution.py:47
  4.6 3.4 %embed.1.refs_0_ = bf16[512,256]{1,0:T(8,128)(2,1)} custom-call(s32[3,512]{1,0:T(4,128)} %tokens_ref.1, s32[1,512]{1,0:T(1,128)} %bitcast.23, bf16[3,1024,256]{2,1,0:T(8,128)(2,1)} %tables_ref.1, bf16[256]{0:T(256)(128)(2,1)} %mask_ref.1), custom_call_target="tpu_custom_call" | custom-call | flops 68719476736 | tf_op jit(solution)/shard_map/embed/pallas_call | solution.py:701
  8.6 2.8 %collective-permute-done.refs_14_ = bf16[512,256]{1,0:T(8,128)(2,1)S(1)} collective-permute-done((bf16[512,256]{1,0:T(8,128)(2,1)S(1)}, bf16[512,256]{1,0:T(8,128)(2,1)S(1)}, u32[]{:S(2)}, u32[]{:S(2)}) %collective-permute-start) | collective-permute-done | bytes 262176 | tf_op jit(solution)/shard_map/ppermute | solution.py:47
  11.4 5.3 %pack.1 = (bf16[2,208,1024]{2,1,0:T(8,128)(2,1)}, bf16[2,704,512]{2,1,0:T(8,128)(2,1)}, bf16[336,1024]{1,0:T(8,128)(2,1)}, bf16[704,512]{1,0:T(8,128)(2,1)}) custom-call(bf16[128,1024]{1,0:T(8,128)(2,1)} %refs_0_.6, bf16[2,1024,256]{2,1,0:T(8,128)(2,1)} %refs_12_.1, bf16[256,1024]{1,0:T(8,128)(2,1)} %refs_2_.2, bf16[256,512]{1,0:T(8,128)(2,1)} %refs_3_.1, ...), custom_call_target="tpu_custom_call" | custom-call | flops 68719476736 | tf_op jit(solution)/shard_map/pack/pallas_call | solution.py:723
  18.4 2.1 %collective-permute-start.7 = (bf16[512,256]{1,0:T(8,128)(2,1)S(1)}, bf16[512,256]{1,0:T(8,128)(2,1)S(1)}, u32[]{:S(2)}, u32[]{:S(2)}) collective-permute-start(bf16[512,256]{1,0:T(8,128)(2,1)S(1)} %collective-permute-done.refs_14_), channel_id=1, source_target_pairs={{0,16},{16,0},{1,17},{17,1},{2,18},{18,2},{3,19},{19,3},{4,20},{20... | collective-permute-start | bytes 786440 | tf_op jit(solution)/shard_map/ppermute | solution.py:47
  20.5 1.9 %collective-permute-start.6 = (bf16[336,1024]{1,0:T(8,128)(2,1)}, bf16[336,1024]{1,0:T(8,128)(2,1)S(1)}, u32[]{:S(2)}, u32[]{:S(2)}) collective-permute-start(bf16[336,1024]{1,0:T(8,128)(2,1)} %get-tuple-element.60), channel_id=1, source_target_pairs={{0,2},{2,0},{1,3},{3,1},{4,6},{6,4},{5,7},{7,5},{8,10},{10,8},{9,1... | collective-permute-start | bytes 2064392 | tf_op jit(solution)/shard_map/ppermute | solution.py:47
  23.2 3.7 %project.1 = (bf16[512,128]{1,0:T(8,128)(2,1)}, bf16[512,1024]{1,0:T(8,128)(2,1)}, bf16[672,256]{1,0:T(8,128)(2,1)}, bf16[672,256]{1,0:T(8,128)(2,1)}) custom-call(bf16[512,256]{1,0:T(8,128)(2,1)} %embed.1.refs_0_, bf16[512,256]{1,0:T(8,128)(2,1)} %copy-done.19, bf16[512,256]{1,0:T(8,128)(2,1)} %copy-done.18, bf16[512,256]{1,0:T(8,128)(2,1)} %copy-done.21, ...), custom_call_target="tpu_custom_call" | custom-call | flops 68719476736 | tf_op jit(solution)/shard_map/project/pallas_call | solution.py:756
  26.9 1.6 %collective-permute-start.5 = (bf16[672,256]{1,0:T(8,128)(2,1)}, bf16[672,256]{1,0:T(8,128)(2,1)S(1)}, u32[]{:S(2)}, u32[]{:S(2)}) collective-permute-start(bf16[672,256]{1,0:T(8,128)(2,1)} %get-tuple-element.57.refs_3_.refs_6_), channel_id=1, source_target_pairs={{0,4},{4,8},{8,12},{12,0},{1,5},{5,9},{9,13},{13,1},{2,6},{6,10},{... | collective-permute-start | bytes 1032200 | tf_op jit(solution)/shard_map/ppermute | solution.py:47
  28.4 2.2 %collective-permute-start.8 = (bf16[672,256]{1,0:T(8,128)(2,1)}, bf16[672,256]{1,0:T(8,128)(2,1)S(1)}, u32[]{:S(2)}, u32[]{:S(2)}) collective-permute-start(bf16[672,256]{1,0:T(8,128)(2,1)} %get-tuple-element.63), channel_id=1, source_target_pairs={{0,12},{4,0},{8,4},{12,8},{1,13},{5,1},{9,5},{13,9},{2,14},{6,2},{... | collective-permute-start | bytes 1032200 | tf_op jit(solution)/shard_map/ppermute | solution.py:47
  30.7 2.9 %attend.3.refs_4_ = f32[2,512,256]{2,1,0:T(8,128)} custom-call(s32[1]{0:T(128)S(6)} %copy.22.refs_0_, f32[2]{0:T(128)} %refs_1_.9, bf16[512,128]{1,0:T(8,128)(2,1)} %get-tuple-element.58.refs_2_, bf16[672,256]{1,0:T(8,128)(2,1)} %get-tuple-element.57.refs_3_.refs_6_), custom_call_target="tpu_custom_call" | custom-call | flops 68719476736 | tf_op jit(solution)/shard_map/attend/pallas_call | solution.py:775
  33.5 6.4 %collective-permute-done.5.refs_3_.refs_4_.refs_7_.refs_1_ = bf16[672,256]{1,0:T(8,128)(2,1)S(1)} collective-permute-done((bf16[672,256]{1,0:T(8,128)(2,1)}, bf16[672,256]{1,0:T(8,128)(2,1)S(1)}, u32[]{:S(2)}, u32[]{:S(2)}) %collective-permute-start.5) | collective-permute-done | bytes 344096 | tf_op jit(solution)/shard_map/ppermute | solution.py:47
  40.6 3.2 %attend.4.refs_4_ = f32[2,512,256]{2,1,0:T(8,128)} custom-call(s32[1]{0:T(128)S(6)} %copy.22.refs_0_, f32[2]{0:T(128)} %refs_1_.9, bf16[512,128]{1,0:T(8,128)(2,1)} %get-tuple-element.58.refs_2_, bf16[672,256]{1,0:T(8,128)(2,1)} %copy-done.7, f32[2,512,256]{2,1,0:T(8,128)} %attend.3.refs_4_), custom_call_target="tpu_custom_call" | custom-call | flops 68719476736 | tf_op jit(solution)/shard_map/attend/pallas_call | solution.py:775
  44.9 1.1 %collective-permute-done.8.refs_3_.refs_5_.refs_8_.refs_2_ = bf16[672,256]{1,0:T(8,128)(2,1)S(1)} collective-permute-done((bf16[672,256]{1,0:T(8,128)(2,1)}, bf16[672,256]{1,0:T(8,128)(2,1)S(1)}, u32[]{:S(2)}, u32[]{:S(2)}) %collective-permute-start.8) | collective-permute-done | bytes 344096 | tf_op jit(solution)/shard_map/ppermute | solution.py:47
  46.8 3.2 %attend.5.refs_3_ = f32[2,512,256]{2,1,0:T(8,128)} custom-call(s32[1]{0:T(128)S(6)} %copy.22.refs_0_, f32[2]{0:T(128)} %refs_1_.9, bf16[512,128]{1,0:T(8,128)(2,1)} %get-tuple-element.58.refs_2_, bf16[672,256]{1,0:T(8,128)(2,1)} %copy-done.17, f32[2,512,256]{2,1,0:T(8,128)} %attend.4.refs_4_), custom_call_target="tpu_custom_call" | custom-call | flops 68719476736 | tf_op jit(solution)/shard_map/attend/pallas_call | solution.py:775
  51.6 4.2 %attend_last.1 = (bf16[192,128]{1,0:T(8,128)(2,1)}, bf16[192,128]{1,0:T(8,128)(2,1)}, bf16[192,128]{1,0:T(8,128)(2,1)}, bf16[192,128]{1,0:T(8,128)(2,1)}) custom-call(s32[1]{0:T(128)S(6)} %copy.22.refs_0_, f32[2]{0:T(128)} %refs_1_.9, bf16[512,128]{1,0:T(8,128)(2,1)} %get-tuple-element.58.refs_2_, f32[2,512,256]{2,1,0:T(8,128)} %attend.5.refs_3_, ...), custom_call_target="tpu_custom_call" | custom-call | flops 68719476736 | tf_op jit(solution)/shard_map/attend_last/pallas_call | solution.py:809
  55.9 2.4 %collective-permute-done.10.refs_10_ = bf16[336,1024]{1,0:T(8,128)(2,1)S(1)} collective-permute-done((bf16[336,1024]{1,0:T(8,128)(2,1)S(1)}, bf16[336,1024]{1,0:T(8,128)(2,1)S(1)}, u32[]{:S(2)}, u32[]{:S(2)}) %collective-permute-start.10) | collective-permute-done | bytes 688160 | tf_op jit(solution)/shard_map/ppermute | solution.py:47
  58.3 1.1 %collective-permute-done.11.refs_8_ = bf16[704,512]{1,0:T(8,128)(2,1)S(1)} collective-permute-done((bf16[704,512]{1,0:T(8,128)(2,1)}, bf16[704,512]{1,0:T(8,128)(2,1)S(1)}, u32[]{:S(2)}, u32[]{:S(2)}) %collective-permute-start.11) | collective-permute-done | bytes 720928 | tf_op jit(solution)/shard_map/ppermute | solution.py:47
  60.2 1.5 %collective-permute-start.16 = (bf16[192,128]{1,0:T(8,128)(2,1)S(1)}, bf16[192,128]{1,0:T(8,128)(2,1)S(1)}, u32[]{:S(2)}, u32[]{:S(2)}) collective-permute-start(bf16[192,128]{1,0:T(8,128)(2,1)S(1)} %copy-done.23), channel_id=1, source_target_pairs={{0,2},{1,3},{2,0},{3,1},{4,6},{5,7},{6,4},{7,5},{8,10},{9,11},{10,... | collective-permute-start | bytes 147464 | tf_op jit(solution)/shard_map/ppermute | solution.py:60
  61.8 1.6 %collective-permute-start.19 = (bf16[704,512]{1,0:T(8,128)(2,1)S(1)}, bf16[704,512]{1,0:T(8,128)(2,1)S(1)}, u32[]{:S(2)}, u32[]{:S(2)}) collective-permute-start(bf16[704,512]{1,0:T(8,128)(2,1)S(1)} %collective-permute-done.11.refs_8_), channel_id=1, source_target_pairs={{0,16},{16,0},{1,17},{17,1},{2,18},{18,2},{3,19},{19,3},{4,20},{20... | collective-permute-start | bytes 2162696 | tf_op jit(solution)/shard_map/ppermute | solution.py:47
  64.3 1.5 %collective-permute-done.17.refs_6_ = bf16[192,128]{1,0:T(8,128)(2,1)S(1)} collective-permute-done((bf16[192,128]{1,0:T(8,128)(2,1)S(1)}, bf16[192,128]{1,0:T(8,128)(2,1)S(1)}, u32[]{:S(2)}, u32[]{:S(2)}) %collective-permute-start.17) | collective-permute-done | bytes 49184 | tf_op jit(solution)/shard_map/ppermute | solution.py:60
  66.9 8.6 %conv.1 = (bf16[128,1024]{1,0:T(8,128)(2,1)}, bf16[144,1024]{1,0:T(8,128)(2,1)}) custom-call(bf16[512,1024]{1,0:T(8,128)(2,1)} %get-tuple-element.56.refs_0_, bf16[672,256]{1,0:T(8,128)(2,1)} %copy-done.7, bf16[672,256]{1,0:T(8,128)(2,1)} %copy-done.17, bf16[192,128]{1,0:T(8,128)(2,1)} %get-tuple-element.80.refs_3_, bf16[192,128]{1,0:T(8,128)(2,1)} %copy-done.25, ...), custom_call_target="tpu_custom_call" | custom-call | flops 68719476736 | tf_op jit(solution)/shard_map/conv/pallas_call | solution.py:839
  75.5 4.9 %collective-permute-done.19.refs_9_ = bf16[704,512]{1,0:T(8,128)(2,1)S(1)} collective-permute-done((bf16[704,512]{1,0:T(8,128)(2,1)S(1)}, bf16[704,512]{1,0:T(8,128)(2,1)S(1)}, u32[]{:S(2)}, u32[]{:S(2)}) %collective-permute-start.19) | collective-permute-done | bytes 720928 | tf_op jit(solution)/shard_map/ppermute | solution.py:47
  82.0 2.7 %collective-permute-done.20.refs_10_ = bf16[2,704,512]{2,1,0:T(8,128)(2,1)} collective-permute-done((bf16[2,704,512]{2,1,0:T(8,128)(2,1)S(1)}, bf16[2,704,512]{2,1,0:T(8,128)(2,1)}, u32[]{:S(2)}, u32[]{:S(2)}) %collective-permute-start.20) | collective-permute-done | bytes 1441824 | tf_op jit(solution)/shard_map/ppermute | solution.py:47
  84.6 7.7 %vocoder.1 = f32[320,128]{1,0:T(8,128)} custom-call(s32[1]{0:T(128)S(6)} %copy.22.refs_0_, bf16[144,1024]{1,0:T(8,128)(2,1)} %get-tuple-element.91.refs_1_, f32[7,512]{1,0:T(8,128)} %refs_2_.3, f32[1,1536]{1,0:T(1,128)} %bitcast.21, bf16[1536,1536]{1,0:T(8,128)(2,1)} %constant.19.clone.refs_4_, f32[4,384]{1,0:T(4,128)} %constant.20.clone.refs_5_, ...), custom_call_target="tpu_custom_call" | custom-call | flops 68719476736 | tf_op jit(solution)/shard_map/vocoder/pallas_call | solution.py:863
  (91 shorter events, 11.7 us)
Async XLA Ops:
  1.6 9.8 %collective-permute-start = (bf16[512,256]{1,0:T(8,128)(2,1)S(1)}, bf16[512,256]{1,0:T(8,128)(2,1)S(1)}, u32[]{:S(2)}, u32[]{:S(2)}) collective-permute-start(bf16[512,256]{1,0:T(8,128)(2,1)S(1)} %dynamic-slice_bitcast_fusion), channel_id=1, source_target_pairs={{0,2},{2,0},{1,3},{3,1},{4,6},{6,4},{5,7},{7,5},{8,10},{10,8},{9,1... | collective-permute-start | bytes 786440 | tf_op jit(solution)/shard_map/ppermute | solution.py:47
  8.1 8.6 %collective-permute-start.1 = (bf16[512,256]{1,0:T(8,128)(2,1)}, bf16[512,256]{1,0:T(8,128)(2,1)S(1)}, u32[]{:S(2)}, u32[]{:S(2)}) collective-permute-start(bf16[512,256]{1,0:T(8,128)(2,1)} %embed.1.refs_0_), channel_id=1, source_target_pairs={{0,2},{2,0},{1,3},{3,1},{4,6},{6,4},{5,7},{7,5},{8,10},{10,8},{9,1... | collective-permute-start | bytes 786440 | tf_op jit(solution)/shard_map/ppermute | solution.py:47
  8.1 8.7 %collective-permute-start.2 = (bf16[512,256]{1,0:T(8,128)(2,1)}, bf16[512,256]{1,0:T(8,128)(2,1)S(1)}, u32[]{:S(2)}, u32[]{:S(2)}) collective-permute-start(bf16[512,256]{1,0:T(8,128)(2,1)} %embed.1.refs_0_), channel_id=1, source_target_pairs={{0,1},{1,0},{2,3},{3,2},{4,5},{5,4},{6,7},{7,6},{8,9},{9,8},{10,11... | collective-permute-start | bytes 786440 | tf_op jit(solution)/shard_map/ppermute | solution.py:47
  8.1 8.7 %collective-permute-start.3 = (bf16[2,1024,256]{2,1,0:T(8,128)(2,1)S(1)}, bf16[2,1024,256]{2,1,0:T(8,128)(2,1)S(1)}, u32[]{:S(2)}, u32[]{:S(2)}) collective-permute-start(bf16[2,1024,256]{2,1,0:T(8,128)(2,1)S(1)} %copy-done.8), channel_id=1, source_target_pairs={{0,1},{1,0},{2,3},{3,2},{4,5},{5,4},{6,7},{7,6},{8,9},{9,8},{10,11... | collective-permute-start | bytes 3145736 | tf_op jit(solution)/shard_map/ppermute | solution.py:47
  16.8 5.7 %collective-permute-start.4 = (bf16[512,256]{1,0:T(8,128)(2,1)S(1)}, bf16[512,256]{1,0:T(8,128)(2,1)S(1)}, u32[]{:S(2)}, u32[]{:S(2)}) collective-permute-start(bf16[512,256]{1,0:T(8,128)(2,1)S(1)} %collective-permute-done.1.refs_2_), channel_id=1, source_target_pairs={{0,1},{1,0},{2,3},{3,2},{4,5},{5,4},{6,7},{7,6},{8,9},{9,8},{10,11... | collective-permute-start | bytes 786440 | tf_op jit(solution)/shard_map/ppermute | solution.py:47
  18.4 15.1 %collective-permute-start.7 = (bf16[512,256]{1,0:T(8,128)(2,1)S(1)}, bf16[512,256]{1,0:T(8,128)(2,1)S(1)}, u32[]{:S(2)}, u32[]{:S(2)}) collective-permute-start(bf16[512,256]{1,0:T(8,128)(2,1)S(1)} %collective-permute-done.refs_14_), channel_id=1, source_target_pairs={{0,16},{16,0},{1,17},{17,1},{2,18},{18,2},{3,19},{19,3},{4,20},{20... | collective-permute-start | bytes 786440 | tf_op jit(solution)/shard_map/ppermute | solution.py:47
  20.5 19.4 %collective-permute-start.6 = (bf16[336,1024]{1,0:T(8,128)(2,1)}, bf16[336,1024]{1,0:T(8,128)(2,1)S(1)}, u32[]{:S(2)}, u32[]{:S(2)}) collective-permute-start(bf16[336,1024]{1,0:T(8,128)(2,1)} %get-tuple-element.60), channel_id=1, source_target_pairs={{0,2},{2,0},{1,3},{3,1},{4,6},{6,4},{5,7},{7,5},{8,10},{10,8},{9,1... | collective-permute-start | bytes 2064392 | tf_op jit(solution)/shard_map/ppermute | solution.py:47
  26.9 13.1 %collective-permute-start.5 = (bf16[672,256]{1,0:T(8,128)(2,1)}, bf16[672,256]{1,0:T(8,128)(2,1)S(1)}, u32[]{:S(2)}, u32[]{:S(2)}) collective-permute-start(bf16[672,256]{1,0:T(8,128)(2,1)} %get-tuple-element.57.refs_3_.refs_6_), channel_id=1, source_target_pairs={{0,4},{4,8},{8,12},{12,0},{1,5},{5,9},{9,13},{13,1},{2,6},{6,10},{... | collective-permute-start | bytes 1032200 | tf_op jit(solution)/shard_map/ppermute | solution.py:47
  28.4 17.6 %collective-permute-start.8 = (bf16[672,256]{1,0:T(8,128)(2,1)}, bf16[672,256]{1,0:T(8,128)(2,1)S(1)}, u32[]{:S(2)}, u32[]{:S(2)}) collective-permute-start(bf16[672,256]{1,0:T(8,128)(2,1)} %get-tuple-element.63), channel_id=1, source_target_pairs={{0,12},{4,0},{8,4},{12,8},{1,13},{5,1},{9,5},{13,9},{2,14},{6,2},{... | collective-permute-start | bytes 1032200 | tf_op jit(solution)/shard_map/ppermute | solution.py:47
  33.5 17.4 %copy-start.6 = (bf16[512,256]{1,0:T(8,128)(2,1)}, bf16[512,256]{1,0:T(8,128)(2,1)S(1)}, u32[]{:S(2)}) copy-start(bf16[512,256]{1,0:T(8,128)(2,1)S(1)} %collective-permute-done.7.refs_15_) | copy-start | bytes 786436
  39.9 19.6 %copy-start.2 = (bf16[336,1024]{1,0:T(8,128)(2,1)}, bf16[336,1024]{1,0:T(8,128)(2,1)S(1)}, u32[]{:S(2)}) copy-start(bf16[336,1024]{1,0:T(8,128)(2,1)S(1)} %collective-permute-done.6.refs_9_) | copy-start | bytes 2064388
  39.9 11.0 %collective-permute-start.9 = (bf16[512,256]{1,0:T(8,128)(2,1)S(1)}, bf16[512,256]{1,0:T(8,128)(2,1)S(1)}, u32[]{:S(2)}, u32[]{:S(2)}) collective-permute-start(bf16[512,256]{1,0:T(8,128)(2,1)S(1)} %slice.3), channel_id=1, source_target_pairs={{0,4},{4,8},{8,12},{12,0},{1,5},{5,9},{9,13},{13,1},{2,6},{6,10},{... | collective-permute-start | bytes 786440 | tf_op jit(solution)/shard_map/ppermute | solution.py:47
  43.9 14.4 %collective-permute-start.10 = (bf16[336,1024]{1,0:T(8,128)(2,1)S(1)}, bf16[336,1024]{1,0:T(8,128)(2,1)S(1)}, u32[]{:S(2)}, u32[]{:S(2)}) collective-permute-start(bf16[336,1024]{1,0:T(8,128)(2,1)S(1)} %collective-permute-done.6.refs_9_), channel_id=1, source_target_pairs={{0,16},{16,0},{1,17},{17,1},{2,18},{18,2},{3,19},{19,3},{4,20},{20... | collective-permute-start | bytes 2064392 | tf_op jit(solution)/shard_map/ppermute | solution.py:47
  44.4 15.0 %collective-permute-start.11 = (bf16[704,512]{1,0:T(8,128)(2,1)}, bf16[704,512]{1,0:T(8,128)(2,1)S(1)}, u32[]{:S(2)}, u32[]{:S(2)}) collective-permute-start(bf16[704,512]{1,0:T(8,128)(2,1)} %get-tuple-element.75), channel_id=1, source_target_pairs={{0,2},{2,0},{1,3},{3,1},{4,6},{6,4},{5,7},{7,5},{8,10},{10,8},{9,1... | collective-permute-start | bytes 2162696 | tf_op jit(solution)/shard_map/ppermute | solution.py:47
  51.0 8.5 %collective-permute-start.12 = (bf16[2,512,256]{2,1,0:T(8,128)(2,1)S(1)}, bf16[2,512,256]{2,1,0:T(8,128)(2,1)S(1)}, u32[]{:S(2)}, u32[]{:S(2)}) collective-permute-start(bf16[2,512,256]{2,1,0:T(8,128)(2,1)S(1)} %pad_maximum_fusion.2), channel_id=1, source_target_pairs={{0,1},{1,0},{2,3},{3,2},{4,5},{5,4},{6,7},{7,6},{8,9},{9,8},{10,11... | collective-permute-start | bytes 1572872 | tf_op jit(solution)/shard_map/ppermute | solution.py:47
  51.1 8.4 %collective-permute-start.13 = (bf16[2,208,1024]{2,1,0:T(8,128)(2,1)S(1)}, bf16[2,208,1024]{2,1,0:T(8,128)(2,1)S(1)}, u32[]{:S(2)}, u32[]{:S(2)}) collective-permute-start(bf16[2,208,1024]{2,1,0:T(8,128)(2,1)S(1)} %copy-done.14), channel_id=1, source_target_pairs={{0,1},{1,0},{2,3},{3,2},{4,5},{5,4},{6,7},{7,6},{8,9},{9,8},{10,11... | collective-permute-start | bytes 2555912 | tf_op jit(solution)/shard_map/ppermute | solution.py:47
  51.6 7.9 %collective-permute-start.14 = (bf16[2,704,512]{2,1,0:T(8,128)(2,1)S(1)}, bf16[2,704,512]{2,1,0:T(8,128)(2,1)S(1)}, u32[]{:S(2)}, u32[]{:S(2)}) collective-permute-start(bf16[2,704,512]{2,1,0:T(8,128)(2,1)S(1)} %copy-done.10), channel_id=1, source_target_pairs={{0,1},{1,0},{2,3},{3,2},{4,5},{5,4},{6,7},{7,6},{8,9},{9,8},{10,11... | collective-permute-start | bytes 4325384 | tf_op jit(solution)/shard_map/ppermute | solution.py:47
  59.4 21.0 %copy-start = (bf16[704,512]{1,0:T(8,128)(2,1)}, bf16[704,512]{1,0:T(8,128)(2,1)S(1)}, u32[]{:S(2)}) copy-start(bf16[704,512]{1,0:T(8,128)(2,1)S(1)} %collective-permute-done.11.refs_8_) | copy-start | bytes 2162692
  59.6 6.2 %collective-permute-start.18 = (bf16[2,336,1024]{2,1,0:T(8,128)(2,1)S(1)}, bf16[2,336,1024]{2,1,0:T(8,128)(2,1)S(1)}, u32[]{:S(2)}, u32[]{:S(2)}) collective-permute-start(bf16[2,336,1024]{2,1,0:T(8,128)(2,1)S(1)} %pad_maximum_fusion.1), channel_id=1, source_target_pairs={{0,1},{1,0},{2,3},{3,2},{4,5},{5,4},{6,7},{7,6},{8,9},{9,8},{10,11... | collective-permute-start | bytes 4128776 | tf_op jit(solution)/shard_map/ppermute | solution.py:47
  59.7 3.7 %collective-permute-start.15 = (bf16[192,128]{1,0:T(8,128)(2,1)S(1)}, bf16[192,128]{1,0:T(8,128)(2,1)S(1)}, u32[]{:S(2)}, u32[]{:S(2)}) collective-permute-start(bf16[192,128]{1,0:T(8,128)(2,1)S(1)} %copy-done.24), channel_id=1, source_target_pairs={{0,1},{1,0},{2,3},{3,2},{4,5},{5,4},{6,7},{7,6},{8,9},{9,8},{10,11... | collective-permute-start | bytes 147464 | tf_op jit(solution)/shard_map/ppermute | solution.py:60
  60.2 4.1 %collective-permute-start.16 = (bf16[192,128]{1,0:T(8,128)(2,1)S(1)}, bf16[192,128]{1,0:T(8,128)(2,1)S(1)}, u32[]{:S(2)}, u32[]{:S(2)}) collective-permute-start(bf16[192,128]{1,0:T(8,128)(2,1)S(1)} %copy-done.23), channel_id=1, source_target_pairs={{0,2},{1,3},{2,0},{3,1},{4,6},{5,7},{6,4},{7,5},{8,10},{9,11},{10,... | collective-permute-start | bytes 147464 | tf_op jit(solution)/shard_map/ppermute | solution.py:60
  61.7 4.0 %collective-permute-start.17 = (bf16[192,128]{1,0:T(8,128)(2,1)S(1)}, bf16[192,128]{1,0:T(8,128)(2,1)S(1)}, u32[]{:S(2)}, u32[]{:S(2)}) collective-permute-start(bf16[192,128]{1,0:T(8,128)(2,1)S(1)} %copy-done.22), channel_id=1, source_target_pairs={{0,3},{1,2},{2,1},{3,0},{4,7},{5,6},{6,5},{7,4},{8,11},{9,10},{10,... | collective-permute-start | bytes 147464 | tf_op jit(solution)/shard_map/ppermute | solution.py:60
  61.8 18.6 %collective-permute-start.19 = (bf16[704,512]{1,0:T(8,128)(2,1)S(1)}, bf16[704,512]{1,0:T(8,128)(2,1)S(1)}, u32[]{:S(2)}, u32[]{:S(2)}) collective-permute-start(bf16[704,512]{1,0:T(8,128)(2,1)S(1)} %collective-permute-done.11.refs_8_), channel_id=1, source_target_pairs={{0,16},{16,0},{1,17},{17,1},{2,18},{18,2},{3,19},{19,3},{4,20},{20... | collective-permute-start | bytes 2162696 | tf_op jit(solution)/shard_map/ppermute | solution.py:47
  81.3 3.4 %collective-permute-start.20 = (bf16[2,704,512]{2,1,0:T(8,128)(2,1)S(1)}, bf16[2,704,512]{2,1,0:T(8,128)(2,1)}, u32[]{:S(2)}, u32[]{:S(2)}) collective-permute-start(bf16[2,704,512]{2,1,0:T(8,128)(2,1)S(1)} %pad_maximum_fusion), channel_id=1, source_target_pairs={{0,1},{1,0},{2,3},{3,2},{4,5},{5,4},{6,7},{7,6},{8,9},{9,8},{10,11... | collective-permute-start | bytes 4325384 | tf_op jit(solution)/shard_map/ppermute | solution.py:47
  (25 other events, 101.6 us)

commit v3 on v2

--- a/solution.py
+++ b/solution.py
@@ -13,8 +13,8 @@
 LANES = 128
 ROWS = 128
 COST = 2**36
+COSTS = (1, 1, 0, 0)
 EDGE = 32
-VMEM_BYTES = 56 * 2**20
 F32 = jnp.float32
 BF16 = jnp.bfloat16
 HBM = pl.BlockSpec(memory_space=pl.ANY)
@@ -94,8 +94,10 @@
         in_specs=in_specs,
         out_specs=out_specs,
         scratch_shapes=scratch,
-        compiler_params=pltpu.CompilerParams(vmem_limit_bytes=VMEM_BYTES),
-        cost_estimate=pl.CostEstimate(flops=COST, bytes_accessed=0, transcendentals=0),
+        compiler_params=pltpu.CompilerParams(
+            vmem_limit_bytes=(56 if name in ("embed", "vocoder") else 28) * 2**20
+        ),
+        cost_estimate=pl.CostEstimate(flops=int(cost * COST), bytes_accessed=0, transcendentals=0),
         name=name,
     )
 
@@ -292,8 +294,8 @@
 
 def pack_kernel(*refs):
     attn_out, conv_in, conv_out, voc_in, voc_up, voc_down, conv_kernel, head = refs[:8]
-    own_first, own_rest, mine_first, mine_rest = refs[8:12]
-    k_scr, head_scr, sems = refs[12:]
+    own_first, own_rest, own_head, mine_first, mine_rest = refs[8:13]
+    k_scr, head_scr, sems = refs[13:]
     group = lax.axis_index("groups") % 2
     taps, split = conv_kernel.shape
     kernel = conv_kernel[...]
@@ -315,23 +317,24 @@
     values = jnp.concatenate([values[:bins], blank, values[bins:], blank], axis=0)
     head_scr[...] = jnp.transpose(values).astype(BF16)
     chunks = (
-        ((attn_out, conv_out, k_scr), own_first, 0, mine_first),
-        ((voc_in, voc_down, voc_up, head_scr), own_rest, 0, mine_rest),
+        ((attn_out, conv_out, k_scr), own_first, mine_first),
+        ((voc_in, voc_down, voc_up), own_rest, mine_rest),
+        ((head_scr,), own_head, None),
     )
     copies = []
-    for sources, own, base, mine in chunks:
+    for sources, own, mine in chunks:
         for side in range(2):
             half = lax.rem(group + side, 2)
             start = 0
             for src in sources:
                 part = src.shape[0] // 2
-                cols = mine.shape[1]
+                cols = own.shape[2]
                 for c in range(src.shape[1] // cols):
                     piece = src.at[
                         pl.ds(pl.multiple_of(half * part, part), part), pl.ds(c * cols, cols)
                     ]
-                    copies.append((piece, own.at[side, pl.ds(base + start, part), :]))
-                    if side == 0:
+                    copies.append((piece, own.at[side, pl.ds(start, part), :]))
+                    if side == 0 and mine is not None:
                         copies.append((piece, mine.at[pl.ds(start, part), :]))
                     start += part
     start = own_first.shape[1]
@@ -351,48 +354,56 @@
         copy.wait()
 
 
-def fetcher(chunks, sems):
+def fetcher(chunks, sems=None):
     group = lax.axis_index("groups") % 2
     subs = lax.axis_size("sub")
-    copies = {}
-    used = [0]
-
-    def fetch(
-        kind, r, chunk, start, part, dst, base, stride=None, cols=None, lanes=None
-    ):
-        copies[kind, r] = []
+    moves, used = {}, [0]
+
+    def fetch(kind, r, chunk, start, part, dst, base, stride=None, cols=None, lanes=None):
         pieces = chunks[chunk][r]
         here = r < subs
+        moves[kind, r] = []
         for side in range(2):
             half = lax.rem(group + side, 2)
             if len(pieces) == 2:
-                src = pieces[side]
+                src, index = pieces[side], ()
             else:
-                src = pieces[0]
-                src = src.at[half if here and stride else side]
+                src, index = pieces[0], (half if here and stride else side,)
             to = pl.ds(pl.multiple_of(base + half * (stride or part), part), part)
             for c in range(dst.shape[1] // cols if cols else 1):
-                target = dst.at[to, pl.ds(c * cols, cols)] if cols else dst.at[to, :]
-                source = src.at[pl.ds(start + c * part, part), pl.ds(*lanes) if lanes else slice(None)]
-                copy = pltpu.make_async_copy(source, target, sems.at[used[0]])
-                used[0] += 1
-                copy.start()
-                copies[kind, r].append(copy)
+                from_rows = slice(start + c * part, start + (c + 1) * part)
+                from_cols = slice(lanes[0], lanes[0] + lanes[1]) if lanes else slice(None)
+                to_cols = slice(c * cols, (c + 1) * cols) if cols else slice(None)
+                source, target = index + (from_rows, from_cols), (to, to_cols)
+                if sems is None:
+                    moves[kind, r].append((src, source, dst, target))
+                else:
+                    at = pl.ds(start + c * part, part)
+                    copy = pltpu.make_async_copy(
+                        src.at[index + (at, slice(None))], dst.at[target], sems.at[used[0]]
+                    )
+                    used[0] += 1
+                    copy.start()
+                    moves[kind, r].append(copy)
 
     def ready(kind, r):
-        for copy in copies[kind, r]:
-            copy.wait()
+        for move in moves[kind, r]:
+            if sems is None:
+                src, source, dst, target = move
+                dst[target] = src[source]
+            else:
+                move.wait()
 
     return fetch, ready
 
 
-def weight_pairs(refs, chunk_count):
+def weight_pairs(refs, counts):
     chunks, at = [], 0
-    for _ in range(chunk_count):
+    for pieces in counts:
         pairs = []
         for dh in range(lax.axis_size("head")):
             for ds in range(lax.axis_size("sub")):
-                taken = 2 if dh and not ds else 1
+                taken = pieces if dh else 1
                 pairs.append(refs[at : at + taken])
                 at += taken
         chunks.append(pairs)
@@ -408,7 +419,7 @@
     count, halo, rim, taps = geo
     emb_ref, before_ref, after_ref = refs[:3]
     att_refs = refs[3 : 3 + count]
-    chunks, refs = weight_pairs(refs[3 + count :], 2)
+    chunks, refs = weight_pairs(refs[3 + count :], (2, 2))
     feat_ref, window_ref, emb_scr, w_out, w_conv, k_conv, w_mix, stream_scr, gate_scr, sems = refs
     win, model = emb_scr.shape
     slab = feat_ref.shape[0]
@@ -437,11 +448,11 @@
 
     def window_copies(act):
         for at, (here, src, dst) in enumerate(window):
-            copy = pltpu.make_async_copy(src, dst, sems.at[18 * count + at])
+            copy = pltpu.make_async_copy(src, dst, sems.at[at])
             pl.when(here)(lambda copy=copy: getattr(copy, act)())
 
     window_copies("start")
-    fetch, ready = fetcher(chunks, sems)
+    fetch, ready = fetcher(chunks)
     out_half = w_out.shape[0] // count // 2
     mix_half = w_mix.shape[1] // 2
     tap_half = k_conv.shape[1] // 2
@@ -517,7 +528,7 @@
 def voc_kernel_body(geo, *refs):
     count, rim, half_voc = geo
     used_ref, window_ref, voc_kernel_ref, bias_ref, table_ref, hann_ref = refs[:6]
-    chunks, refs = weight_pairs(refs[6:], 1)
+    chunks, refs = weight_pairs(refs[6:], (2, 1))
     wave_ref, w_vin, w_up, w_down, w_head, w_table, base_scr, wave_scr, out_scr, sems = refs
     slab = out_scr.shape[1]
     first = first_frame(slab)
@@ -540,12 +551,11 @@
     for r in range(count):
         fetch("down", r, 0, vin_half, down_half, w_down, owners[r] * 2 * down_half)
     for r in range(count):
-        at = up_half * (w_up.shape[1] // voc)
         fetch(
             "head",
             r,
+            1,
             0,
-            rest + at,
             head_half,
             w_head,
             owners[r] * 2 * head_half,
@@ -687,10 +697,7 @@
     def share(xs):
         return [rotate(x, "sub", 1) for x in xs]
 
-    def share_both(kind):
-        return share([jnp.stack(pair) for pair in zip(near[kind], far[kind])])
-
-    near, far, both, own, own_sub, mine = {}, {}, {}, {}, {}, {}
+    near, far, near_sub, far_sub, own, own_sub, mine = {}, {}, {}, {}, {}, {}, {}
     mine["top"] = lax.dynamic_slice(
         conv_in, (group, 0, 0), (1, deep // 2, conv_in.shape[2])
     ).reshape(deep // 2, conv_in.shape[2])
@@ -704,7 +711,7 @@
         [VMEM] * 4,
         VMEM,
         [],
-        9,
+        1,
         "embed",
     )(tokens, masked[None, :], tables, mask_vec)
     crossed = cross(embedded)
@@ -719,28 +726,34 @@
     first_rows = (attn_out.shape[0] + conv_out.shape[0] + tap_rows) // 2
     low_rows = deep // 2 * conv_in.shape[2] // model
     conv_rows = (voc_in.shape[0] + voc_down.shape[0]) // 2
-    head_rows = (voc_up.shape[0] * voc_up.shape[1] + voc_head.shape[0] * 2 * padded) // voc // 2
+    conv_rows += voc_up.shape[0] * voc_up.shape[1] // voc // 2
+    head_rows = voc_head.shape[0] * 2 * padded // voc // 2
     packed = call(
         pack_kernel,
         [
             jax.ShapeDtypeStruct((2, first_rows, model), BF16),
-            jax.ShapeDtypeStruct((2, conv_rows + head_rows, voc), BF16),
+            jax.ShapeDtypeStruct((2, conv_rows, voc), BF16),
+            jax.ShapeDtypeStruct((2, head_rows, voc), BF16),
             jax.ShapeDtypeStruct((first_rows + low_rows, model), BF16),
-            jax.ShapeDtypeStruct((conv_rows + head_rows, voc), BF16),
+            jax.ShapeDtypeStruct((conv_rows, voc), BF16),
         ],
         [HBM] * 6 + [VMEM] * 2,
-        [VMEM] * 4,
+        [VMEM] * 5,
         [
             pltpu.VMEM((tap_rows, model), BF16),
             pltpu.VMEM((voc_head.shape[0], 2 * padded), BF16),
             pltpu.SemaphoreType.DMA((48,)),
         ],
-        15,
+        1,
         "pack",
     )(attn_out, conv_in, conv_out, voc_in, voc_up, voc_down, conv_kernel, voc_head.T)
 
-    crossed, beside, own_sub["b"], packed = together(crossed, beside, own_sub["b"], packed)
-    own["a"], own["c"], mine["a"], mine["c"] = packed
+    own["a"], own["c"], own["h"], mine["a"], mine["c"] = packed
+    near["a"] = cross(mine["a"])
+
+    crossed, beside, own_sub["b"], [own["a"], own["c"], own["h"], mine["c"]] = together(
+        crossed, beside, own_sub["b"], [own["a"], own["c"], own["h"], mine["c"]]
+    )
 
     def members(own_piece, beside_piece, others_pieces):
         pieces = [own_piece] + beside_piece
@@ -749,8 +762,8 @@
         return pieces
 
     pieces = members(embedded, beside, crossed)
-    far["top"] = spread(near["top"])
-    near["a"] = cross(mine["a"])
+    for kind in ("a", "c"):
+        own_sub[kind] = share([own[kind]])
     chunk = 2 * width
     message = (frame_count + (model // chunk + 1) * halo, chunk)
     q_own, emb, upward, downward = call(
@@ -764,28 +777,33 @@
         [VMEM] * (count + 1),
         (VMEM,) * 4,
         [pltpu.VMEM((model, 3 * width), BF16)],
-        10,
+        1,
         "project",
     )(*pieces, attn_in)
 
     below, above = rotate(upward, "seq", 1), rotate(downward, "seq", -1)
     heads = head_temp.shape[0]
 
-    def attend(hops, blocks, sums):
+    def attend(hops, blocks, sums, cost):
         return call(
             lambda *refs: attend_part_kernel(head_size, hops, *refs),
             jax.ShapeDtypeStruct((heads, frame_count, chunk), F32),
             [SMEM, SMEM] + [VMEM] * (1 + len(blocks) + len(sums)),
             VMEM,
             [pltpu.VMEM((len(blocks), frame_count, chunk), BF16)],
-            10,
+            cost,
             "attend",
         )(used_frames, head_temp, q_own, *blocks, *sums)
 
-    sums = attend([0], [upward], [])
-    [below, sums, mine["c"]], near["a"], far["top"] = together(
-        [below, sums, mine["c"]], near["a"], far["top"]
-    )
+    [q_own], near["top"], own_sub["a"], own_sub["c"] = together(
+        [q_own], near["top"], own_sub["a"], own_sub["c"]
+    )
+    far["top"] = spread(near["top"])
+    sums = attend([0], [upward], [], COSTS[0])
+    [sums, mine["c"]], near["a"], far["top"] = together([sums, mine["c"]], near["a"], far["top"])
+    far["a"], near["c"] = spread(near["a"]), cross(mine["c"])
+    near_sub["a"] = share(near["a"])
+    [below, sums] = together([below, sums])[0]
     blocks, hops = [upward, below, above], [0, -1, 1]
     ahead, behind = below[:frame_count], above[:frame_count]
     for hop in range(2, seq_size // 2 + 1):
@@ -796,16 +814,13 @@
             behind = rotate(behind, "seq", -1)
             blocks.append(behind)
             hops.append(hop)
-    far["a"], near["c"] = spread(near["a"]), cross(mine["c"])
-    sums = attend([-1], [below], [sums])
-
-    sums = attend([1], [above], [sums])
-    last, [sums, own["a"], own["c"]], near["top"], far["top"] = together(
-        blocks[3:], [sums, own["a"], own["c"]], near["top"], far["top"]
+    sums = attend([-1], [below], [sums], COSTS[1])
+    sums = attend([1], [above], [sums], COSTS[2])
+    last, [sums], near["top"], far["top"], near_sub["a"] = together(
+        blocks[3:], [sums], near["top"], far["top"], near_sub["a"]
     )
     blocks[3:] = last
-    own_sub["a"], own_sub["c"] = share([own["a"]]), share([own["c"]])
-    both["top"] = share_both("top")
+    near_sub["top"], far_sub["top"] = share(near["top"]), share(far["top"])
     windows = call(
         lambda *refs: attend_last_kernel(head_size, halo, hops, 3, count, slab, *refs),
         (jax.ShapeDtypeStruct((win, cols), BF16),) * count,
@@ -815,22 +830,26 @@
             pltpu.VMEM((len(blocks), frame_count, chunk), BF16),
             pltpu.VMEM((frame_count + 2 * halo, width), BF16),
         ],
-        10,
+        COSTS[3],
         "attend_last",
     )(used_frames, head_temp, q_own, sums, below, above, *blocks)
 
-    windows, far["a"], near["c"], both["top"], own_sub["a"], own_sub["c"] = together(
-        windows, far["a"], near["c"], both["top"], own_sub["a"], own_sub["c"]
+    windows, near_sub["top"], far_sub["top"], far["a"], near["c"] = together(
+        windows, near_sub["top"], far_sub["top"], far["a"], near["c"]
     )
     attended = send_members(windows)
-    both["a"] = share_both("a")
-    far["c"] = spread(near["c"])
+    far_sub["a"], far["c"] = share(far["a"]), spread(near["c"])
+    attended, far_sub["a"], near["c"], [own["h"]] = together(
+        attended, far_sub["a"], near["c"], [own["h"]]
+    )
+    near["h"], near_sub["c"] = cross(own["h"]), share(near["c"])
+    own_sub["h"] = share([own["h"]])
     own["top"], own_sub["top"] = own["b"], own_sub["b"]
 
     def weights(kind):
         found = [own[kind], *own_sub[kind]]
         for dh in range(len(others)):
-            found += [t[kind][dh] for t in (near, far, both)]
+            found += [t[kind][dh] for t in (near, far, near_sub, far_sub) if kind in t]
         return found
 
     conv_weights = [w for kind in ("a", "top") for w in weights(kind)]
@@ -842,7 +861,7 @@
             jax.ShapeDtypeStruct((slab, model), BF16),
             jax.ShapeDtypeStruct((mid, model), BF16),
         ),
-        [HBM] * 3 + [VMEM] * count + [HBM] * len(conv_weights),
+        [HBM] * 3 + [VMEM] * (count + len(conv_weights)),
         (VMEM, VMEM),
         [
             pltpu.VMEM((win, model), BF16),
@@ -852,14 +871,16 @@
             pltpu.VMEM((count,) + conv_out.shape, BF16),
             pltpu.VMEM((win, model), F32),
             pltpu.VMEM((conv_in.shape[2] // LANES, win, LANES), F32),
-            pltpu.SemaphoreType.DMA((10 * count + 3 + 2 * model // (2 * width) + 8 * count,)),
+            pltpu.SemaphoreType.DMA((3 + 2 * model // (2 * width),)),
         ],
-        18,
+        0,
         "conv",
     )(emb, below, above, *attended, *conv_weights)
-    [window], far["c"] = together([window], far["c"])
-    both["c"] = share_both("c")
-    voc_weights = weights("c")
+    [window], far["c"], near_sub["c"], near["h"], own_sub["h"] = together(
+        [window], far["c"], near_sub["c"], near["h"], own_sub["h"]
+    )
+    far_sub["c"], near_sub["h"] = share(far["c"]), share(near["h"])
+    voc_weights = weights("c") + weights("h")
     wave = call(
         lambda *refs: voc_kernel_body((count, rim, half_voc), *refs),
         jax.ShapeDtypeStruct((slab * HOP // LANES, LANES), F32),
@@ -876,7 +897,7 @@
             pltpu.VMEM((span // LANES, slab, LANES), F32),
             pltpu.SemaphoreType.DMA((4 * count + 4 * count * (voc_up.shape[1] // voc) + 1,)),
         ],
-        18,
+        1,
         "vocoder",
     )(
         used_frames,

time: 93 us -> 83.5 us (0.90)
  Pallas kernels: 42.2 us -> 27.7 us
  starting transfers between devices: 17.1 us -> 21.3 us
  waiting for transfers between devices: 24.8 us -> 27.3 us
  local copies, waits for them, and re-layouts: 6.41 us -> 5.29 us
    pallas_call x3, Pallas kernels: 9.29 us -> 4.09 us  [attend(): call(lambda *refs: attend_part_kernel(head_size, hops, *refs), jax.ShapeD...]
    ppermute x18 -> x24, starting transfers between devices: 15 us -> 19 us  [rotate(): return lax.ppermute(x, axis, [(i, (i + by) % size) for i in range(size)])]
    pallas_call x1, Pallas kernels: 5.31 us -> 2.85 us  [local(): call(pack_kernel, [jax.ShapeDtypeStruct((2, first_rows, model), BF16), ja...]
    pallas_call x1, Pallas kernels: 8.56 us -> 6.11 us  [local(): call(lambda *refs: conv_kernel_body((count, halo, rim, taps), *refs), (ja...]
    ppermute x18 -> x24, waiting for transfers between devices: 22.4 us -> 24.8 us  [rotate(): return lax.ppermute(x, axis, [(i, (i + by) % size) for i in range(size)])]
    pallas_call x1, Pallas kernels: 3.66 us -> 1.31 us  [local(): call(lambda *refs: project_kernel(count, head_size, *refs), (jax.ShapeDty...]
    pallas_call x1, Pallas kernels: 4.18 us -> 2.2 us  [local(): call(lambda *refs: attend_last_kernel(head_size, halo, hops, 3, count, sl...]
    unnamed x58 -> x50, local copies, waits for them, and re-layouts: 5.34 us -> 4.22 us
  transfers between devices with their start and end apart: 21 -> 27, of which waited for: 10 -> 11; matrix products, arithmetic and copies ran while one was open for 1% -> 1% of each run, Pallas kernels for 37% -> 24%
where the time goes in v3:
time: 83.5 us; the launch traced here: 83.3 us
  Pallas kernels  27.7 us (33%)
  waiting for transfers between devices  27.3 us (33%)
  starting transfers between devices  21.3 us (26%)
  local copies, waits for them, and re-layouts  5.29 us (6%)
  between operations  1.74 us (2%)
    ppermute x24, waiting for transfers between devices, rotate(): return lax.ppermute(x, axis, [(i, (i + by) % size) for i in range(size)])  24.8 us
    ppermute x24, starting transfers between devices, rotate(): return lax.ppermute(x, axis, [(i, (i + by) % size) for i in range(size)])  19 us
    pallas_call x1, Pallas kernels, local(): call(lambda *refs: voc_kernel_body((count, rim, half_voc), *refs), jax.Sh...  7.72 us
    pallas_call x1, Pallas kernels, local(): call(lambda *refs: conv_kernel_body((count, halo, rim, taps), *refs), (ja...  6.11 us
    unnamed x50, local copies, waits for them, and re-layouts  4.22 us
    pallas_call x3, Pallas kernels, attend(): call(lambda *refs: attend_part_kernel(head_size, hops, *refs), jax.ShapeD...  4.09 us
    pallas_call x1, Pallas kernels, local(): call(embed_kernel, jax.ShapeDtypeStruct((frame_count, piece_cols), BF16),...  3.47 us
    pallas_call x1, Pallas kernels, local(): call(pack_kernel, [jax.ShapeDtypeStruct((2, first_rows, model), BF16), ja...  2.85 us
  transfers between devices with their start and end apart: 27, of which 11 were waited for; matrix products, arithmetic and copies ran while one was open for 1% of the time, Pallas kernels for 24%

profile of v3, /device:TPU:0, one launch (start us, length us, event | category | flops | bytes accessed | tf_op | source)
XLA Modules:
  0.0 83.3 jit_solution(17063915559360367763)
XLA Ops:
  1.6 3.0 %collective-permute-start = (bf16[512,256]{1,0:T(8,128)(2,1)S(1)}, bf16[512,256]{1,0:T(8,128)(2,1)S(1)}, u32[]{:S(2)}, u32[]{:S(2)}) collective-permute-start(bf16[512,256]{1,0:T(8,128)(2,1)S(1)} %dynamic-slice_bitcast_fusion), channel_id=1, source_target_pairs={{0,2},{2,0},{1,3},{3,1},{4,6},{6,4},{5,7},{7,5},{8,10},{10,8},{9,1... | collective-permute-start | bytes 786440 | tf_op jit(solution)/shard_map/ppermute | solution.py:47
  4.7 3.5 %embed.1.refs_0_ = bf16[512,256]{1,0:T(8,128)(2,1)} custom-call(s32[3,512]{1,0:T(4,128)} %tokens_ref.1, s32[1,512]{1,0:T(1,128)} %bitcast.11, bf16[3,1024,256]{2,1,0:T(8,128)(2,1)} %tables_ref.1, bf16[256]{0:T(256)(128)(2,1)} %mask_ref.1), custom_call_target="tpu_custom_call" | custom-call | flops 68719476736 | tf_op jit(solution)/shard_map/embed/pallas_call | solution.py:708
  8.7 2.6 %collective-permute-done.refs_15_ = bf16[512,256]{1,0:T(8,128)(2,1)S(1)} collective-permute-done((bf16[512,256]{1,0:T(8,128)(2,1)S(1)}, bf16[512,256]{1,0:T(8,128)(2,1)S(1)}, u32[]{:S(2)}, u32[]{:S(2)}) %collective-permute-start) | collective-permute-done | bytes 262176 | tf_op jit(solution)/shard_map/ppermute | solution.py:47
  11.4 2.8 %pack.1 = (bf16[2,208,1024]{2,1,0:T(8,128)(2,1)S(1)}, bf16[2,512,512]{2,1,0:T(8,128)(2,1)S(1)}, bf16[2,192,512]{2,1,0:T(8,128)(2,1)S(1)}, bf16[336,1024]{1,0:T(8,128)(2,1)S(1)}, bf16[512,512]{1,0:T(8,128)(2,1)S(1)}) custom-call(bf16[128,1024]{1,0:T(8,128)(2,1)S(1)} %copy-done.12, bf16[2,1024,256]{2,1,0:T(8,128)(2,1)S(1)} %copy-done, ...), custom_call_target="tpu_custom_call" | custom-call | flops 68719476736 | tf_op jit(solution)/shard_map/pack/pallas_call | solution.py:731
  14.3 2.3 %collective-permute-done.1.refs_2_ = bf16[512,256]{1,0:T(8,128)(2,1)S(1)} collective-permute-done((bf16[512,256]{1,0:T(8,128)(2,1)}, bf16[512,256]{1,0:T(8,128)(2,1)S(1)}, u32[]{:S(2)}, u32[]{:S(2)}) %collective-permute-start.1) | collective-permute-done | bytes 262176 | tf_op jit(solution)/shard_map/ppermute | solution.py:47
  18.2 1.8 %collective-permute-start.8 = (bf16[336,1024]{1,0:T(8,128)(2,1)S(1)}, bf16[336,1024]{1,0:T(8,128)(2,1)S(1)}, u32[]{:S(2)}, u32[]{:S(2)}) collective-permute-start(bf16[336,1024]{1,0:T(8,128)(2,1)S(1)} %get-tuple-element.78), channel_id=1, source_target_pairs={{0,2},{2,0},{1,3},{3,1},{4,6},{6,4},{5,7},{7,5},{8,10},{10,8},{9,1... | collective-permute-start | bytes 2064392 | tf_op jit(solution)/shard_map/ppermute | solution.py:47
  21.8 1.6 %collective-permute-start.5 = (bf16[672,256]{1,0:T(8,128)(2,1)S(1)}, bf16[672,256]{1,0:T(8,128)(2,1)S(1)}, u32[]{:S(2)}, u32[]{:S(2)}) collective-permute-start(bf16[672,256]{1,0:T(8,128)(2,1)S(1)} %get-tuple-element.71.refs_3_.refs_6_), channel_id=1, source_target_pairs={{0,4},{4,8},{8,12},{12,0},{1,5},{5,9},{9,13},{13,1},{2,6},{6,10},{... | collective-permute-start | bytes 1032200 | tf_op jit(solution)/shard_map/ppermute | solution.py:47
  23.5 2.2 %collective-permute-start.10 = (bf16[672,256]{1,0:T(8,128)(2,1)S(1)}, bf16[672,256]{1,0:T(8,128)(2,1)S(1)}, u32[]{:S(2)}, u32[]{:S(2)}) collective-permute-start(bf16[672,256]{1,0:T(8,128)(2,1)S(1)} %get-tuple-element.82), channel_id=1, source_target_pairs={{0,12},{4,0},{8,4},{12,8},{1,13},{5,1},{9,5},{13,9},{2,14},{6,2},{... | collective-permute-start | bytes 1032200 | tf_op jit(solution)/shard_map/ppermute | solution.py:47
  25.7 1.6 %collective-permute-start.9 = (bf16[512,256]{1,0:T(8,128)(2,1)S(1)}, bf16[512,256]{1,0:T(8,128)(2,1)S(1)}, u32[]{:S(2)}, u32[]{:S(2)}) collective-permute-start(bf16[512,256]{1,0:T(8,128)(2,1)S(1)} %collective-permute-done.refs_15_), channel_id=1, source_target_pairs={{0,16},{16,0},{1,17},{17,1},{2,18},{18,2},{3,19},{19,3},{4,20},{20... | collective-permute-start | bytes 786440 | tf_op jit(solution)/shard_map/ppermute | solution.py:47
  28.7 7.4 %collective-permute-done.8.refs_9_ = bf16[336,1024]{1,0:T(8,128)(2,1)S(1)} collective-permute-done((bf16[336,1024]{1,0:T(8,128)(2,1)S(1)}, bf16[336,1024]{1,0:T(8,128)(2,1)S(1)}, u32[]{:S(2)}, u32[]{:S(2)}) %collective-permute-start.8) | collective-permute-done | bytes 688160 | tf_op jit(solution)/shard_map/ppermute | solution.py:47
  36.1 1.8 %collective-permute-start.15 = (bf16[336,1024]{1,0:T(8,128)(2,1)S(1)}, bf16[336,1024]{1,0:T(8,128)(2,1)S(1)}, u32[]{:S(2)}, u32[]{:S(2)}) collective-permute-start(bf16[336,1024]{1,0:T(8,128)(2,1)S(1)} %collective-permute-done.8.refs_9_), channel_id=1, source_target_pairs={{0,16},{16,0},{1,17},{17,1},{2,18},{18,2},{3,19},{19,3},{4,20},{20... | collective-permute-start | bytes 2064392 | tf_op jit(solution)/shard_map/ppermute | solution.py:47
  37.9 1.6 %collective-permute-start.11 = (bf16[512,256]{1,0:T(8,128)(2,1)S(1)}, bf16[512,256]{1,0:T(8,128)(2,1)S(1)}, u32[]{:S(2)}, u32[]{:S(2)}) collective-permute-start(bf16[512,256]{1,0:T(8,128)(2,1)S(1)} %slice.3), channel_id=1, source_target_pairs={{0,4},{4,8},{8,12},{12,0},{1,5},{5,9},{9,13},{13,1},{2,6},{6,10},{... | collective-permute-start | bytes 786440 | tf_op jit(solution)/shard_map/ppermute | solution.py:47
  39.5 1.5 %collective-permute-start.16 = (bf16[512,512]{1,0:T(8,128)(2,1)S(1)}, bf16[512,512]{1,0:T(8,128)(2,1)S(1)}, u32[]{:S(2)}, u32[]{:S(2)}) collective-permute-start(bf16[512,512]{1,0:T(8,128)(2,1)S(1)} %get-tuple-element.94), channel_id=1, source_target_pairs={{0,2},{2,0},{1,3},{3,1},{4,6},{6,4},{5,7},{7,5},{8,10},{10,8},{9,1... | collective-permute-start | bytes 1572872 | tf_op jit(solution)/shard_map/ppermute | solution.py:47
  41.0 1.4 %attend.4.refs_4_ = f32[2,512,256]{2,1,0:T(8,128)S(1)} custom-call(s32[1]{0:T(128)S(6)} %copy.22.refs_0_, f32[2]{0:T(128)S(1)} %copy-done.3, bf16[512,128]{1,0:T(8,128)(2,1)S(1)} %get-tuple-element.76.refs_2_, bf16[672,256]{1,0:T(8,128)(2,1)S(1)} %collective-permute-done.5.refs_3_.refs_4_.refs_7_.refs_1_, f32[2,512,256]{2,1,0:T(8,128)S(1)} %attend.3.refs_4_), custom_call_target="tpu_custom_call" | custom-call | flops 68719476736 | tf_op jit(solution)/shard_map/attend/pallas_call | solution.py:788
  42.4 1.4 %attend.5.refs_3_ = f32[2,512,256]{2,1,0:T(8,128)S(1)} custom-call(s32[1]{0:T(128)S(6)} %copy.22.refs_0_, f32[2]{0:T(128)S(1)} %copy-done.3, bf16[512,128]{1,0:T(8,128)(2,1)S(1)} %get-tuple-element.76.refs_2_, bf16[672,256]{1,0:T(8,128)(2,1)S(1)} %collective-permute-done.10.refs_3_.refs_5_.refs_8_.refs_2_, f32[2,512,256]{2,1,0:T(8,128)S(1)} %attend.4.refs_4_), custom_call_target="tpu_custom_call" | custom-call | tf_op jit(solution)/shard_map/attend/pallas_call | solution.py:788
  43.8 4.5 %collective-permute-done.11.refs_9_ = bf16[512,256]{1,0:T(8,128)(2,1)S(1)} collective-permute-done((bf16[512,256]{1,0:T(8,128)(2,1)S(1)}, bf16[512,256]{1,0:T(8,128)(2,1)S(1)}, u32[]{:S(2)}, u32[]{:S(2)}) %collective-permute-start.11) | collective-permute-done | bytes 262176 | tf_op jit(solution)/shard_map/ppermute | solution.py:47
  48.8 2.2 %attend_last.1 = (bf16[192,128]{1,0:T(8,128)(2,1)S(1)}, bf16[192,128]{1,0:T(8,128)(2,1)S(1)}, bf16[192,128]{1,0:T(8,128)(2,1)S(1)}, bf16[192,128]{1,0:T(8,128)(2,1)S(1)}) custom-call(s32[1]{0:T(128)S(6)} %copy.22.refs_0_, f32[2]{0:T(128)S(1)} %copy-done.3, bf16[512,128]{1,0:T(8,128)(2,1)S(1)} %get-tuple-element.76.refs_2_, ...), custom_call_target="tpu_custom_call" | custom-call | tf_op jit(solution)/shard_map/attend_last/pallas_call | solution.py:824
  51.0 2.3 %collective-permute-done.16.refs_8_ = bf16[512,512]{1,0:T(8,128)(2,1)S(1)} collective-permute-done((bf16[512,512]{1,0:T(8,128)(2,1)S(1)}, bf16[512,512]{1,0:T(8,128)(2,1)S(1)}, u32[]{:S(2)}, u32[]{:S(2)}) %collective-permute-start.16) | collective-permute-done | bytes 524320 | tf_op jit(solution)/shard_map/ppermute | solution.py:47
  54.5 1.7 %collective-permute-start.18 = (bf16[192,128]{1,0:T(8,128)(2,1)S(1)}, bf16[192,128]{1,0:T(8,128)(2,1)S(1)}, u32[]{:S(2)}, u32[]{:S(2)}) collective-permute-start(bf16[192,128]{1,0:T(8,128)(2,1)S(1)} %get-tuple-element.97), channel_id=1, source_target_pairs={{0,2},{1,3},{2,0},{3,1},{4,6},{5,7},{6,4},{7,5},{8,10},{9,11},{10,... | collective-permute-start | bytes 147464 | tf_op jit(solution)/shard_map/ppermute | solution.py:60
  56.2 1.5 %collective-permute-start.21 = (bf16[512,512]{1,0:T(8,128)(2,1)S(1)}, bf16[512,512]{1,0:T(8,128)(2,1)}, u32[]{:S(2)}, u32[]{:S(2)}) collective-permute-start(bf16[512,512]{1,0:T(8,128)(2,1)S(1)} %collective-permute-done.16.refs_8_), channel_id=1, source_target_pairs={{0,16},{16,0},{1,17},{17,1},{2,18},{18,2},{3,19},{19,3},{4,20},{20... | collective-permute-start | bytes 1572872 | tf_op jit(solution)/shard_map/ppermute | solution.py:47
  58.6 1.6 %collective-permute-done.19.refs_6_ = bf16[192,128]{1,0:T(8,128)(2,1)S(1)} collective-permute-done((bf16[192,128]{1,0:T(8,128)(2,1)S(1)}, bf16[192,128]{1,0:T(8,128)(2,1)S(1)}, u32[]{:S(2)}, u32[]{:S(2)}) %collective-permute-start.19) | collective-permute-done | bytes 49184 | tf_op jit(solution)/shard_map/ppermute | solution.py:60
  60.9 6.1 %conv.1 = (bf16[128,1024]{1,0:T(8,128)(2,1)}, bf16[144,1024]{1,0:T(8,128)(2,1)S(1)}) custom-call(bf16[512,1024]{1,0:T(8,128)(2,1)S(1)} %get-tuple-element.70.refs_0_, bf16[672,256]{1,0:T(8,128)(2,1)S(1)} %collective-permute-done.5.refs_3_.refs_4_.refs_7_.refs_1_, bf16[672,256]{1,0:T(8,128)(2,1)S(1)} %collective-permute-done.10.refs_3_.refs_5_.refs_8_.refs_2_, ...), custom_call_target="tpu_custom_call" | custom-call | tf_op jit(solution)/shard_map/conv/pallas_call | solution.py:858
  67.8 2.8 %collective-permute-done.21.refs_9_ = bf16[512,512]{1,0:T(8,128)(2,1)} collective-permute-done((bf16[512,512]{1,0:T(8,128)(2,1)S(1)}, bf16[512,512]{1,0:T(8,128)(2,1)}, u32[]{:S(2)}, u32[]{:S(2)}) %collective-permute-start.21) | collective-permute-done | bytes 524320 | tf_op jit(solution)/shard_map/ppermute | solution.py:47
  75.4 7.7 %vocoder.1 = f32[320,128]{1,0:T(8,128)} custom-call(s32[1]{0:T(128)S(6)} %copy.22.refs_0_, bf16[144,1024]{1,0:T(8,128)(2,1)} %copy-done.11, f32[7,512]{1,0:T(8,128)} %refs_2_.3, f32[1,1536]{1,0:T(1,128)} %bitcast.10, bf16[1536,1536]{1,0:T(8,128)(2,1)} %constant.19.clone.refs_4_, f32[4,384]{1,0:T(4,128)} %constant.20.clone.refs_5_, ...), custom_call_target="tpu_custom_call" | custom-call | flops 68719476736 | tf_op jit(solution)/shard_map/vocoder/pallas_call | solution.py:884
  (92 shorter events, 14.6 us)
Async XLA Ops:
  1.6 9.7 %collective-permute-start = (bf16[512,256]{1,0:T(8,128)(2,1)S(1)}, bf16[512,256]{1,0:T(8,128)(2,1)S(1)}, u32[]{:S(2)}, u32[]{:S(2)}) collective-permute-start(bf16[512,256]{1,0:T(8,128)(2,1)S(1)} %dynamic-slice_bitcast_fusion), channel_id=1, source_target_pairs={{0,2},{2,0},{1,3},{3,1},{4,6},{6,4},{5,7},{7,5},{8,10},{10,8},{9,1... | collective-permute-start | bytes 786440 | tf_op jit(solution)/shard_map/ppermute | solution.py:47
  8.2 8.4 %collective-permute-start.1 = (bf16[512,256]{1,0:T(8,128)(2,1)}, bf16[512,256]{1,0:T(8,128)(2,1)S(1)}, u32[]{:S(2)}, u32[]{:S(2)}) collective-permute-start(bf16[512,256]{1,0:T(8,128)(2,1)} %embed.1.refs_0_), channel_id=1, source_target_pairs={{0,2},{2,0},{1,3},{3,1},{4,6},{6,4},{5,7},{7,5},{8,10},{10,8},{9,1... | collective-permute-start | bytes 786440 | tf_op jit(solution)/shard_map/ppermute | solution.py:47
  8.2 8.3 %collective-permute-start.2 = (bf16[512,256]{1,0:T(8,128)(2,1)}, bf16[512,256]{1,0:T(8,128)(2,1)S(1)}, u32[]{:S(2)}, u32[]{:S(2)}) collective-permute-start(bf16[512,256]{1,0:T(8,128)(2,1)} %embed.1.refs_0_), channel_id=1, source_target_pairs={{0,1},{1,0},{2,3},{3,2},{4,5},{5,4},{6,7},{7,6},{8,9},{9,8},{10,11... | collective-permute-start | bytes 786440 | tf_op jit(solution)/shard_map/ppermute | solution.py:47
  8.2 8.3 %collective-permute-start.3 = (bf16[2,1024,256]{2,1,0:T(8,128)(2,1)S(1)}, bf16[2,1024,256]{2,1,0:T(8,128)(2,1)S(1)}, u32[]{:S(2)}, u32[]{:S(2)}) collective-permute-start(bf16[2,1024,256]{2,1,0:T(8,128)(2,1)S(1)} %copy-done), channel_id=1, source_target_pairs={{0,1},{1,0},{2,3},{3,2},{4,5},{5,4},{6,7},{7,6},{8,9},{9,8},{10,11... | collective-permute-start | bytes 3145736 | tf_op jit(solution)/shard_map/ppermute | solution.py:47
  18.2 17.9 %collective-permute-start.8 = (bf16[336,1024]{1,0:T(8,128)(2,1)S(1)}, bf16[336,1024]{1,0:T(8,128)(2,1)S(1)}, u32[]{:S(2)}, u32[]{:S(2)}) collective-permute-start(bf16[336,1024]{1,0:T(8,128)(2,1)S(1)} %get-tuple-element.78), channel_id=1, source_target_pairs={{0,2},{2,0},{1,3},{3,1},{4,6},{6,4},{5,7},{7,5},{8,10},{10,8},{9,1... | collective-permute-start | bytes 2064392 | tf_op jit(solution)/shard_map/ppermute | solution.py:47
  20.0 5.7 %collective-permute-start.7 = (bf16[2,512,512]{2,1,0:T(8,128)(2,1)S(1)}, bf16[2,512,512]{2,1,0:T(8,128)(2,1)S(1)}, u32[]{:S(2)}, u32[]{:S(2)}) collective-permute-start(bf16[2,512,512]{2,1,0:T(8,128)(2,1)S(1)} %get-tuple-element.75.refs_6_), channel_id=1, source_target_pairs={{0,1},{1,0},{2,3},{3,2},{4,5},{5,4},{6,7},{7,6},{8,9},{9,8},{10,11... | collective-permute-start | bytes 3145736 | tf_op jit(solution)/shard_map/ppermute | solution.py:47
  20.2 5.5 %collective-permute-start.6 = (bf16[2,208,1024]{2,1,0:T(8,128)(2,1)S(1)}, bf16[2,208,1024]{2,1,0:T(8,128)(2,1)S(1)}, u32[]{:S(2)}, u32[]{:S(2)}) collective-permute-start(bf16[2,208,1024]{2,1,0:T(8,128)(2,1)S(1)} %get-tuple-element.74.refs_7_), channel_id=1, source_target_pairs={{0,1},{1,0},{2,3},{3,2},{4,5},{5,4},{6,7},{7,6},{8,9},{9,8},{10,11... | collective-permute-start | bytes 2555912 | tf_op jit(solution)/shard_map/ppermute | solution.py:47
  21.8 16.0 %collective-permute-start.5 = (bf16[672,256]{1,0:T(8,128)(2,1)S(1)}, bf16[672,256]{1,0:T(8,128)(2,1)S(1)}, u32[]{:S(2)}, u32[]{:S(2)}) collective-permute-start(bf16[672,256]{1,0:T(8,128)(2,1)S(1)} %get-tuple-element.71.refs_3_.refs_6_), channel_id=1, source_target_pairs={{0,4},{4,8},{8,12},{12,0},{1,5},{5,9},{9,13},{13,1},{2,6},{6,10},{... | collective-permute-start | bytes 1032200 | tf_op jit(solution)/shard_map/ppermute | solution.py:47
  23.5 18.9 %collective-permute-start.10 = (bf16[672,256]{1,0:T(8,128)(2,1)S(1)}, bf16[672,256]{1,0:T(8,128)(2,1)S(1)}, u32[]{:S(2)}, u32[]{:S(2)}) collective-permute-start(bf16[672,256]{1,0:T(8,128)(2,1)S(1)} %get-tuple-element.82), channel_id=1, source_target_pairs={{0,12},{4,0},{8,4},{12,8},{1,13},{5,1},{9,5},{13,9},{2,14},{6,2},{... | collective-permute-start | bytes 1032200 | tf_op jit(solution)/shard_map/ppermute | solution.py:47
  25.7 10.4 %collective-permute-start.9 = (bf16[512,256]{1,0:T(8,128)(2,1)S(1)}, bf16[512,256]{1,0:T(8,128)(2,1)S(1)}, u32[]{:S(2)}, u32[]{:S(2)}) collective-permute-start(bf16[512,256]{1,0:T(8,128)(2,1)S(1)} %collective-permute-done.refs_15_), channel_id=1, source_target_pairs={{0,16},{16,0},{1,17},{17,1},{2,18},{18,2},{3,19},{19,3},{4,20},{20... | collective-permute-start | bytes 786440 | tf_op jit(solution)/shard_map/ppermute | solution.py:47
  36.1 12.2 %collective-permute-start.12 = (bf16[336,1024]{1,0:T(8,128)(2,1)S(1)}, bf16[336,1024]{1,0:T(8,128)(2,1)S(1)}, u32[]{:S(2)}, u32[]{:S(2)}) collective-permute-start(bf16[336,1024]{1,0:T(8,128)(2,1)S(1)} %collective-permute-done.8.refs_9_), channel_id=1, source_target_pairs={{0,1},{1,0},{2,3},{3,2},{4,5},{5,4},{6,7},{7,6},{8,9},{9,8},{10,11... | collective-permute-start | bytes 2064392 | tf_op jit(solution)/shard_map/ppermute | solution.py:47
  36.1 17.9 %collective-permute-start.15 = (bf16[336,1024]{1,0:T(8,128)(2,1)S(1)}, bf16[336,1024]{1,0:T(8,128)(2,1)S(1)}, u32[]{:S(2)}, u32[]{:S(2)}) collective-permute-start(bf16[336,1024]{1,0:T(8,128)(2,1)S(1)} %collective-permute-done.8.refs_9_), channel_id=1, source_target_pairs={{0,16},{16,0},{1,17},{17,1},{2,18},{18,2},{3,19},{19,3},{4,20},{20... | collective-permute-start | bytes 2064392 | tf_op jit(solution)/shard_map/ppermute | solution.py:47
  37.9 10.4 %collective-permute-start.11 = (bf16[512,256]{1,0:T(8,128)(2,1)S(1)}, bf16[512,256]{1,0:T(8,128)(2,1)S(1)}, u32[]{:S(2)}, u32[]{:S(2)}) collective-permute-start(bf16[512,256]{1,0:T(8,128)(2,1)S(1)} %slice.3), channel_id=1, source_target_pairs={{0,4},{4,8},{8,12},{12,0},{1,5},{5,9},{9,13},{13,1},{2,6},{6,10},{... | collective-permute-start | bytes 786440 | tf_op jit(solution)/shard_map/ppermute | solution.py:47
  39.5 13.8 %collective-permute-start.16 = (bf16[512,512]{1,0:T(8,128)(2,1)S(1)}, bf16[512,512]{1,0:T(8,128)(2,1)S(1)}, u32[]{:S(2)}, u32[]{:S(2)}) collective-permute-start(bf16[512,512]{1,0:T(8,128)(2,1)S(1)} %get-tuple-element.94), channel_id=1, source_target_pairs={{0,2},{2,0},{1,3},{3,1},{4,6},{6,4},{5,7},{7,5},{8,10},{10,8},{9,1... | collective-permute-start | bytes 1572872 | tf_op jit(solution)/shard_map/ppermute | solution.py:47
  48.2 5.7 %collective-permute-start.13 = (bf16[512,256]{1,0:T(8,128)(2,1)S(1)}, bf16[512,256]{1,0:T(8,128)(2,1)S(1)}, u32[]{:S(2)}, u32[]{:S(2)}) collective-permute-start(bf16[512,256]{1,0:T(8,128)(2,1)S(1)} %collective-permute-done.refs_15_), channel_id=1, source_target_pairs={{0,1},{1,0},{2,3},{3,2},{4,5},{5,4},{6,7},{7,6},{8,9},{9,8},{10,11... | collective-permute-start | bytes 786440 | tf_op jit(solution)/shard_map/ppermute | solution.py:47
  48.3 5.7 %collective-permute-start.14 = (bf16[512,256]{1,0:T(8,128)(2,1)S(1)}, bf16[512,256]{1,0:T(8,128)(2,1)S(1)}, u32[]{:S(2)}, u32[]{:S(2)}) collective-permute-start(bf16[512,256]{1,0:T(8,128)(2,1)S(1)} %collective-permute-done.9.refs_16_), channel_id=1, source_target_pairs={{0,1},{1,0},{2,3},{3,2},{4,5},{5,4},{6,7},{7,6},{8,9},{9,8},{10,11... | collective-permute-start | bytes 786440 | tf_op jit(solution)/shard_map/ppermute | solution.py:47
  54.0 6.2 %collective-permute-start.20 = (bf16[336,1024]{1,0:T(8,128)(2,1)S(1)}, bf16[336,1024]{1,0:T(8,128)(2,1)S(1)}, u32[]{:S(2)}, u32[]{:S(2)}) collective-permute-start(bf16[336,1024]{1,0:T(8,128)(2,1)S(1)} %collective-permute-done.15.refs_10_), channel_id=1, source_target_pairs={{0,1},{1,0},{2,3},{3,2},{4,5},{5,4},{6,7},{7,6},{8,9},{9,8},{10,11... | collective-permute-start | bytes 2064392 | tf_op jit(solution)/shard_map/ppermute | solution.py:47
  54.0 3.7 %collective-permute-start.17 = (bf16[192,128]{1,0:T(8,128)(2,1)S(1)}, bf16[192,128]{1,0:T(8,128)(2,1)S(1)}, u32[]{:S(2)}, u32[]{:S(2)}) collective-permute-start(bf16[192,128]{1,0:T(8,128)(2,1)S(1)} %get-tuple-element.96), channel_id=1, source_target_pairs={{0,1},{1,0},{2,3},{3,2},{4,5},{5,4},{6,7},{7,6},{8,9},{9,8},{10,11... | collective-permute-start | bytes 147464 | tf_op jit(solution)/shard_map/ppermute | solution.py:60
  54.5 4.1 %collective-permute-start.18 = (bf16[192,128]{1,0:T(8,128)(2,1)S(1)}, bf16[192,128]{1,0:T(8,128)(2,1)S(1)}, u32[]{:S(2)}, u32[]{:S(2)}) collective-permute-start(bf16[192,128]{1,0:T(8,128)(2,1)S(1)} %get-tuple-element.97), channel_id=1, source_target_pairs={{0,2},{1,3},{2,0},{3,1},{4,6},{5,7},{6,4},{7,5},{8,10},{9,11},{10,... | collective-permute-start | bytes 147464 | tf_op jit(solution)/shard_map/ppermute | solution.py:60
  56.2 4.0 %collective-permute-start.19 = (bf16[192,128]{1,0:T(8,128)(2,1)S(1)}, bf16[192,128]{1,0:T(8,128)(2,1)S(1)}, u32[]{:S(2)}, u32[]{:S(2)}) collective-permute-start(bf16[192,128]{1,0:T(8,128)(2,1)S(1)} %get-tuple-element.98), channel_id=1, source_target_pairs={{0,3},{1,2},{2,1},{3,0},{4,7},{5,6},{6,5},{7,4},{8,11},{9,10},{10,... | collective-permute-start | bytes 147464 | tf_op jit(solution)/shard_map/ppermute | solution.py:60
  56.2 14.4 %collective-permute-start.21 = (bf16[512,512]{1,0:T(8,128)(2,1)S(1)}, bf16[512,512]{1,0:T(8,128)(2,1)}, u32[]{:S(2)}, u32[]{:S(2)}) collective-permute-start(bf16[512,512]{1,0:T(8,128)(2,1)S(1)} %collective-permute-done.16.refs_8_), channel_id=1, source_target_pairs={{0,16},{16,0},{1,17},{17,1},{2,18},{18,2},{3,19},{19,3},{4,20},{20... | collective-permute-start | bytes 1572872 | tf_op jit(solution)/shard_map/ppermute | solution.py:47
  60.2 11.5 %collective-permute-start.22 = (bf16[512,512]{1,0:T(8,128)(2,1)S(1)}, bf16[512,512]{1,0:T(8,128)(2,1)S(1)}, u32[]{:S(2)}, u32[]{:S(2)}) collective-permute-start(bf16[512,512]{1,0:T(8,128)(2,1)S(1)} %collective-permute-done.16.refs_8_), channel_id=1, source_target_pairs={{0,1},{1,0},{2,3},{3,2},{4,5},{5,4},{6,7},{7,6},{8,9},{9,8},{10,11... | collective-permute-start | bytes 1572872 | tf_op jit(solution)/shard_map/ppermute | solution.py:47
  60.4 11.3 %collective-permute-start.23 = (bf16[2,192,512]{2,1,0:T(8,128)(2,1)S(1)}, bf16[2,192,512]{2,1,0:T(8,128)(2,1)S(1)}, u32[]{:S(2)}, u32[]{:S(2)}) collective-permute-start(bf16[2,192,512]{2,1,0:T(8,128)(2,1)S(1)} %get-tuple-element.115.refs_12_), channel_id=1, source_target_pairs={{0,2},{2,0},{1,3},{3,1},{4,6},{6,4},{5,7},{7,5},{8,10},{10,8},{9,1... | collective-permute-start | bytes 1179656 | tf_op jit(solution)/shard_map/ppermute | solution.py:47
  60.9 10.8 %collective-permute-start.24 = (bf16[2,192,512]{2,1,0:T(8,128)(2,1)S(1)}, bf16[2,192,512]{2,1,0:T(8,128)(2,1)S(1)}, u32[]{:S(2)}, u32[]{:S(2)}) collective-permute-start(bf16[2,192,512]{2,1,0:T(8,128)(2,1)S(1)} %get-tuple-element.115.refs_12_), channel_id=1, source_target_pairs={{0,1},{1,0},{2,3},{3,2},{4,5},{5,4},{6,7},{7,6},{8,9},{9,8},{10,11... | collective-permute-start | bytes 1179656 | tf_op jit(solution)/shard_map/ppermute | solution.py:47
  (27 other events, 194.6 us)

commit v4 on v3

--- a/solution.py
+++ b/solution.py
@@ -529,8 +529,8 @@
     count, rim, half_voc = geo
     used_ref, window_ref, voc_kernel_ref, bias_ref, table_ref, hann_ref = refs[:6]
     chunks, refs = weight_pairs(refs[6:], (2, 1))
-    wave_ref, w_vin, w_up, w_down, w_head, w_table, base_scr, wave_scr, out_scr, sems = refs
-    slab = out_scr.shape[1]
+    wave_ref, w_vin, w_up, w_down, w_head, w_table, base_scr, wave_scr, out_scr, row_scr, sems = refs
+    slab = wave_ref.shape[0] * LANES // HOP
     first = first_frame(slab)
     total_frames = lax.axis_size("seq") * count * slab
     used = used_ref[0]
@@ -618,7 +618,7 @@
     audio = audio / energy
     tiles = range(span // LANES)
     for c in tiles:
-        out_scr[c] = audio[:, c * LANES : (c + 1) * LANES]
+        out_scr[c, :slab, :] = audio[:, c * LANES : (c + 1) * LANES]
     even, odd = (
         jnp.concatenate([out_scr[c, pl.ds(at, slab // 2, stride=2), :] for c in tiles], axis=1)
         for at in range(2)
@@ -626,7 +626,8 @@
     samples = jnp.concatenate([even[:, :HOP], odd[:, :HOP]], axis=1)
     count = 2 * HOP // LANES
     for c in range(count):
-        wave_ref[pl.ds(c, slab // 2, stride=count), :] = samples[:, c * LANES : (c + 1) * LANES]
+        row_scr[pl.ds(c, slab // 2, stride=count), :] = samples[:, c * LANES : (c + 1) * LANES]
+    wave_ref[...] = row_scr[: wave_ref.shape[0], :]
 
 
 def synthesis(bins, padded, span):
@@ -894,7 +895,8 @@
             pltpu.VMEM(table.shape, BF16),
             pltpu.VMEM((voc // LANES, mid, LANES), F32),
             pltpu.VMEM((parts, mid - 2 * (half_voc + 1), span), F32),
-            pltpu.VMEM((span // LANES, slab, LANES), F32),
+            pltpu.VMEM((span // LANES, slab + 8, LANES), F32),
+            pltpu.VMEM((slab * HOP // LANES + 8, LANES), F32),
             pltpu.SemaphoreType.DMA((4 * count + 4 * count * (voc_up.shape[1] // voc) + 1,)),
         ],
         1,

time: 83.5 us -> 83.5 us (level)
  no operation moved by 1% of the time
where the time goes in v4:
time: 83.5 us; the launch traced here: 83.3 us
  Pallas kernels  27.8 us (33%)
  waiting for transfers between devices  27.3 us (33%)
  starting transfers between devices  21.3 us (26%)
  local copies, waits for them, and re-layouts  5.29 us (6%)
  between operations  1.74 us (2%)
    ppermute x24, waiting for transfers between devices, rotate(): return lax.ppermute(x, axis, [(i, (i + by) % size) for i in range(size)])  24.8 us
    ppermute x24, starting transfers between devices, rotate(): return lax.ppermute(x, axis, [(i, (i + by) % size) for i in range(size)])  19 us
    pallas_call x1, Pallas kernels, local(): call(lambda *refs: voc_kernel_body((count, rim, half_voc), *refs), jax.Sh...  7.73 us
    pallas_call x1, Pallas kernels, local(): call(lambda *refs: conv_kernel_body((count, halo, rim, taps), *refs), (ja...  6.11 us
    unnamed x50, local copies, waits for them, and re-layouts  4.22 us
    pallas_call x3, Pallas kernels, attend(): call(lambda *refs: attend_part_kernel(head_size, hops, *refs), jax.ShapeD...  4.09 us
    pallas_call x1, Pallas kernels, local(): call(embed_kernel, jax.ShapeDtypeStruct((frame_count, piece_cols), BF16),...  3.47 us
    pallas_call x1, Pallas kernels, local(): call(pack_kernel, [jax.ShapeDtypeStruct((2, first_rows, model), BF16), ja...  2.85 us
  transfers between devices with their start and end apart: 27, of which 11 were waited for; matrix products, arithmetic and copies ran while one was open for 1% of the time, Pallas kernels for 24%

profile of v4, /device:TPU:0, one launch (start us, length us, event | category | flops | bytes accessed | tf_op | source)
XLA Modules:
  0.0 83.3 jit_solution(2319846026384262479)
XLA Ops:
  1.6 3.0 %collective-permute-start = (bf16[512,256]{1,0:T(8,128)(2,1)S(1)}, bf16[512,256]{1,0:T(8,128)(2,1)S(1)}, u32[]{:S(2)}, u32[]{:S(2)}) collective-permute-start(bf16[512,256]{1,0:T(8,128)(2,1)S(1)} %dynamic-slice_bitcast_fusion), channel_id=1, source_target_pairs={{0,2},{2,0},{1,3},{3,1},{4,6},{6,4},{5,7},{7,5},{8,10},{10,8},{9,1... | collective-permute-start | bytes 786440 | tf_op jit(solution)/shard_map/ppermute | solution.py:47
  4.7 3.5 %embed.1.refs_0_ = bf16[512,256]{1,0:T(8,128)(2,1)} custom-call(s32[3,512]{1,0:T(4,128)} %tokens_ref.1, s32[1,512]{1,0:T(1,128)} %bitcast.11, bf16[3,1024,256]{2,1,0:T(8,128)(2,1)} %tables_ref.1, bf16[256]{0:T(256)(128)(2,1)} %mask_ref.1), custom_call_target="tpu_custom_call" | custom-call | flops 68719476736 | tf_op jit(solution)/shard_map/embed/pallas_call | solution.py:709
  8.7 2.6 %collective-permute-done.refs_15_ = bf16[512,256]{1,0:T(8,128)(2,1)S(1)} collective-permute-done((bf16[512,256]{1,0:T(8,128)(2,1)S(1)}, bf16[512,256]{1,0:T(8,128)(2,1)S(1)}, u32[]{:S(2)}, u32[]{:S(2)}) %collective-permute-start) | collective-permute-done | bytes 262176 | tf_op jit(solution)/shard_map/ppermute | solution.py:47
  11.4 2.8 %pack.1 = (bf16[2,208,1024]{2,1,0:T(8,128)(2,1)S(1)}, bf16[2,512,512]{2,1,0:T(8,128)(2,1)S(1)}, bf16[2,192,512]{2,1,0:T(8,128)(2,1)S(1)}, bf16[336,1024]{1,0:T(8,128)(2,1)S(1)}, bf16[512,512]{1,0:T(8,128)(2,1)S(1)}) custom-call(bf16[128,1024]{1,0:T(8,128)(2,1)S(1)} %copy-done.12, bf16[2,1024,256]{2,1,0:T(8,128)(2,1)S(1)} %copy-done, ...), custom_call_target="tpu_custom_call" | custom-call | flops 68719476736 | tf_op jit(solution)/shard_map/pack/pallas_call | solution.py:732
  14.3 2.3 %collective-permute-done.1.refs_2_ = bf16[512,256]{1,0:T(8,128)(2,1)S(1)} collective-permute-done((bf16[512,256]{1,0:T(8,128)(2,1)}, bf16[512,256]{1,0:T(8,128)(2,1)S(1)}, u32[]{:S(2)}, u32[]{:S(2)}) %collective-permute-start.1) | collective-permute-done | bytes 262176 | tf_op jit(solution)/shard_map/ppermute | solution.py:47
  18.2 1.8 %collective-permute-start.8 = (bf16[336,1024]{1,0:T(8,128)(2,1)S(1)}, bf16[336,1024]{1,0:T(8,128)(2,1)S(1)}, u32[]{:S(2)}, u32[]{:S(2)}) collective-permute-start(bf16[336,1024]{1,0:T(8,128)(2,1)S(1)} %get-tuple-element.78), channel_id=1, source_target_pairs={{0,2},{2,0},{1,3},{3,1},{4,6},{6,4},{5,7},{7,5},{8,10},{10,8},{9,1... | collective-permute-start | bytes 2064392 | tf_op jit(solution)/shard_map/ppermute | solution.py:47
  21.8 1.6 %collective-permute-start.5 = (bf16[672,256]{1,0:T(8,128)(2,1)S(1)}, bf16[672,256]{1,0:T(8,128)(2,1)S(1)}, u32[]{:S(2)}, u32[]{:S(2)}) collective-permute-start(bf16[672,256]{1,0:T(8,128)(2,1)S(1)} %get-tuple-element.71.refs_3_.refs_6_), channel_id=1, source_target_pairs={{0,4},{4,8},{8,12},{12,0},{1,5},{5,9},{9,13},{13,1},{2,6},{6,10},{... | collective-permute-start | bytes 1032200 | tf_op jit(solution)/shard_map/ppermute | solution.py:47
  23.5 2.2 %collective-permute-start.10 = (bf16[672,256]{1,0:T(8,128)(2,1)S(1)}, bf16[672,256]{1,0:T(8,128)(2,1)S(1)}, u32[]{:S(2)}, u32[]{:S(2)}) collective-permute-start(bf16[672,256]{1,0:T(8,128)(2,1)S(1)} %get-tuple-element.82), channel_id=1, source_target_pairs={{0,12},{4,0},{8,4},{12,8},{1,13},{5,1},{9,5},{13,9},{2,14},{6,2},{... | collective-permute-start | bytes 1032200 | tf_op jit(solution)/shard_map/ppermute | solution.py:47
  25.7 1.6 %collective-permute-start.9 = (bf16[512,256]{1,0:T(8,128)(2,1)S(1)}, bf16[512,256]{1,0:T(8,128)(2,1)S(1)}, u32[]{:S(2)}, u32[]{:S(2)}) collective-permute-start(bf16[512,256]{1,0:T(8,128)(2,1)S(1)} %collective-permute-done.refs_15_), channel_id=1, source_target_pairs={{0,16},{16,0},{1,17},{17,1},{2,18},{18,2},{3,19},{19,3},{4,20},{20... | collective-permute-start | bytes 786440 | tf_op jit(solution)/shard_map/ppermute | solution.py:47
  28.7 7.4 %collective-permute-done.8.refs_9_ = bf16[336,1024]{1,0:T(8,128)(2,1)S(1)} collective-permute-done((bf16[336,1024]{1,0:T(8,128)(2,1)S(1)}, bf16[336,1024]{1,0:T(8,128)(2,1)S(1)}, u32[]{:S(2)}, u32[]{:S(2)}) %collective-permute-start.8) | collective-permute-done | bytes 688160 | tf_op jit(solution)/shard_map/ppermute | solution.py:47
  36.1 1.8 %collective-permute-start.15 = (bf16[336,1024]{1,0:T(8,128)(2,1)S(1)}, bf16[336,1024]{1,0:T(8,128)(2,1)S(1)}, u32[]{:S(2)}, u32[]{:S(2)}) collective-permute-start(bf16[336,1024]{1,0:T(8,128)(2,1)S(1)} %collective-permute-done.8.refs_9_), channel_id=1, source_target_pairs={{0,16},{16,0},{1,17},{17,1},{2,18},{18,2},{3,19},{19,3},{4,20},{20... | collective-permute-start | bytes 2064392 | tf_op jit(solution)/shard_map/ppermute | solution.py:47
  37.9 1.6 %collective-permute-start.11 = (bf16[512,256]{1,0:T(8,128)(2,1)S(1)}, bf16[512,256]{1,0:T(8,128)(2,1)S(1)}, u32[]{:S(2)}, u32[]{:S(2)}) collective-permute-start(bf16[512,256]{1,0:T(8,128)(2,1)S(1)} %slice.3), channel_id=1, source_target_pairs={{0,4},{4,8},{8,12},{12,0},{1,5},{5,9},{9,13},{13,1},{2,6},{6,10},{... | collective-permute-start | bytes 786440 | tf_op jit(solution)/shard_map/ppermute | solution.py:47
  39.5 1.5 %collective-permute-start.16 = (bf16[512,512]{1,0:T(8,128)(2,1)S(1)}, bf16[512,512]{1,0:T(8,128)(2,1)S(1)}, u32[]{:S(2)}, u32[]{:S(2)}) collective-permute-start(bf16[512,512]{1,0:T(8,128)(2,1)S(1)} %get-tuple-element.94), channel_id=1, source_target_pairs={{0,2},{2,0},{1,3},{3,1},{4,6},{6,4},{5,7},{7,5},{8,10},{10,8},{9,1... | collective-permute-start | bytes 1572872 | tf_op jit(solution)/shard_map/ppermute | solution.py:47
  41.0 1.4 %attend.4.refs_4_ = f32[2,512,256]{2,1,0:T(8,128)S(1)} custom-call(s32[1]{0:T(128)S(6)} %copy.22.refs_0_, f32[2]{0:T(128)S(1)} %copy-done.3, bf16[512,128]{1,0:T(8,128)(2,1)S(1)} %get-tuple-element.76.refs_2_, bf16[672,256]{1,0:T(8,128)(2,1)S(1)} %collective-permute-done.5.refs_3_.refs_4_.refs_7_.refs_1_, f32[2,512,256]{2,1,0:T(8,128)S(1)} %attend.3.refs_4_), custom_call_target="tpu_custom_call" | custom-call | flops 68719476736 | tf_op jit(solution)/shard_map/attend/pallas_call | solution.py:789
  42.4 1.4 %attend.5.refs_3_ = f32[2,512,256]{2,1,0:T(8,128)S(1)} custom-call(s32[1]{0:T(128)S(6)} %copy.22.refs_0_, f32[2]{0:T(128)S(1)} %copy-done.3, bf16[512,128]{1,0:T(8,128)(2,1)S(1)} %get-tuple-element.76.refs_2_, bf16[672,256]{1,0:T(8,128)(2,1)S(1)} %collective-permute-done.10.refs_3_.refs_5_.refs_8_.refs_2_, f32[2,512,256]{2,1,0:T(8,128)S(1)} %attend.4.refs_4_), custom_call_target="tpu_custom_call" | custom-call | tf_op jit(solution)/shard_map/attend/pallas_call | solution.py:789
  43.8 4.5 %collective-permute-done.11.refs_9_ = bf16[512,256]{1,0:T(8,128)(2,1)S(1)} collective-permute-done((bf16[512,256]{1,0:T(8,128)(2,1)S(1)}, bf16[512,256]{1,0:T(8,128)(2,1)S(1)}, u32[]{:S(2)}, u32[]{:S(2)}) %collective-permute-start.11) | collective-permute-done | bytes 262176 | tf_op jit(solution)/shard_map/ppermute | solution.py:47
  48.8 2.2 %attend_last.1 = (bf16[192,128]{1,0:T(8,128)(2,1)S(1)}, bf16[192,128]{1,0:T(8,128)(2,1)S(1)}, bf16[192,128]{1,0:T(8,128)(2,1)S(1)}, bf16[192,128]{1,0:T(8,128)(2,1)S(1)}) custom-call(s32[1]{0:T(128)S(6)} %copy.22.refs_0_, f32[2]{0:T(128)S(1)} %copy-done.3, bf16[512,128]{1,0:T(8,128)(2,1)S(1)} %get-tuple-element.76.refs_2_, ...), custom_call_target="tpu_custom_call" | custom-call | tf_op jit(solution)/shard_map/attend_last/pallas_call | solution.py:825
  51.0 2.3 %collective-permute-done.16.refs_8_ = bf16[512,512]{1,0:T(8,128)(2,1)S(1)} collective-permute-done((bf16[512,512]{1,0:T(8,128)(2,1)S(1)}, bf16[512,512]{1,0:T(8,128)(2,1)S(1)}, u32[]{:S(2)}, u32[]{:S(2)}) %collective-permute-start.16) | collective-permute-done | bytes 524320 | tf_op jit(solution)/shard_map/ppermute | solution.py:47
  54.5 1.7 %collective-permute-start.18 = (bf16[192,128]{1,0:T(8,128)(2,1)S(1)}, bf16[192,128]{1,0:T(8,128)(2,1)S(1)}, u32[]{:S(2)}, u32[]{:S(2)}) collective-permute-start(bf16[192,128]{1,0:T(8,128)(2,1)S(1)} %get-tuple-element.97), channel_id=1, source_target_pairs={{0,2},{1,3},{2,0},{3,1},{4,6},{5,7},{6,4},{7,5},{8,10},{9,11},{10,... | collective-permute-start | bytes 147464 | tf_op jit(solution)/shard_map/ppermute | solution.py:60
  56.2 1.5 %collective-permute-start.21 = (bf16[512,512]{1,0:T(8,128)(2,1)S(1)}, bf16[512,512]{1,0:T(8,128)(2,1)}, u32[]{:S(2)}, u32[]{:S(2)}) collective-permute-start(bf16[512,512]{1,0:T(8,128)(2,1)S(1)} %collective-permute-done.16.refs_8_), channel_id=1, source_target_pairs={{0,16},{16,0},{1,17},{17,1},{2,18},{18,2},{3,19},{19,3},{4,20},{20... | collective-permute-start | bytes 1572872 | tf_op jit(solution)/shard_map/ppermute | solution.py:47
  58.6 1.6 %collective-permute-done.19.refs_6_ = bf16[192,128]{1,0:T(8,128)(2,1)S(1)} collective-permute-done((bf16[192,128]{1,0:T(8,128)(2,1)S(1)}, bf16[192,128]{1,0:T(8,128)(2,1)S(1)}, u32[]{:S(2)}, u32[]{:S(2)}) %collective-permute-start.19) | collective-permute-done | bytes 49184 | tf_op jit(solution)/shard_map/ppermute | solution.py:60
  60.9 6.1 %conv.1 = (bf16[128,1024]{1,0:T(8,128)(2,1)}, bf16[144,1024]{1,0:T(8,128)(2,1)S(1)}) custom-call(bf16[512,1024]{1,0:T(8,128)(2,1)S(1)} %get-tuple-element.70.refs_0_, bf16[672,256]{1,0:T(8,128)(2,1)S(1)} %collective-permute-done.5.refs_3_.refs_4_.refs_7_.refs_1_, bf16[672,256]{1,0:T(8,128)(2,1)S(1)} %collective-permute-done.10.refs_3_.refs_5_.refs_8_.refs_2_, ...), custom_call_target="tpu_custom_call" | custom-call | tf_op jit(solution)/shard_map/conv/pallas_call | solution.py:859
  67.8 2.8 %collective-permute-done.21.refs_9_ = bf16[512,512]{1,0:T(8,128)(2,1)} collective-permute-done((bf16[512,512]{1,0:T(8,128)(2,1)S(1)}, bf16[512,512]{1,0:T(8,128)(2,1)}, u32[]{:S(2)}, u32[]{:S(2)}) %collective-permute-start.21) | collective-permute-done | bytes 524320 | tf_op jit(solution)/shard_map/ppermute | solution.py:47
  75.4 7.7 %vocoder.1 = f32[320,128]{1,0:T(8,128)} custom-call(s32[1]{0:T(128)S(6)} %copy.22.refs_0_, bf16[144,1024]{1,0:T(8,128)(2,1)} %copy-done.11, f32[7,512]{1,0:T(8,128)} %refs_2_.3, f32[1,1536]{1,0:T(1,128)} %bitcast.10, bf16[1536,1536]{1,0:T(8,128)(2,1)} %constant.19.clone.refs_4_, f32[4,384]{1,0:T(4,128)} %constant.20.clone.refs_5_, ...), custom_call_target="tpu_custom_call" | custom-call | flops 68719476736 | tf_op jit(solution)/shard_map/vocoder/pallas_call | solution.py:885
  (92 shorter events, 14.6 us)
Async XLA Ops:
  1.6 9.7 %collective-permute-start = (bf16[512,256]{1,0:T(8,128)(2,1)S(1)}, bf16[512,256]{1,0:T(8,128)(2,1)S(1)}, u32[]{:S(2)}, u32[]{:S(2)}) collective-permute-start(bf16[512,256]{1,0:T(8,128)(2,1)S(1)} %dynamic-slice_bitcast_fusion), channel_id=1, source_target_pairs={{0,2},{2,0},{1,3},{3,1},{4,6},{6,4},{5,7},{7,5},{8,10},{10,8},{9,1... | collective-permute-start | bytes 786440 | tf_op jit(solution)/shard_map/ppermute | solution.py:47
  8.2 8.4 %collective-permute-start.1 = (bf16[512,256]{1,0:T(8,128)(2,1)}, bf16[512,256]{1,0:T(8,128)(2,1)S(1)}, u32[]{:S(2)}, u32[]{:S(2)}) collective-permute-start(bf16[512,256]{1,0:T(8,128)(2,1)} %embed.1.refs_0_), channel_id=1, source_target_pairs={{0,2},{2,0},{1,3},{3,1},{4,6},{6,4},{5,7},{7,5},{8,10},{10,8},{9,1... | collective-permute-start | bytes 786440 | tf_op jit(solution)/shard_map/ppermute | solution.py:47
  8.2 8.3 %collective-permute-start.2 = (bf16[512,256]{1,0:T(8,128)(2,1)}, bf16[512,256]{1,0:T(8,128)(2,1)S(1)}, u32[]{:S(2)}, u32[]{:S(2)}) collective-permute-start(bf16[512,256]{1,0:T(8,128)(2,1)} %embed.1.refs_0_), channel_id=1, source_target_pairs={{0,1},{1,0},{2,3},{3,2},{4,5},{5,4},{6,7},{7,6},{8,9},{9,8},{10,11... | collective-permute-start | bytes 786440 | tf_op jit(solution)/shard_map/ppermute | solution.py:47
  8.2 8.3 %collective-permute-start.3 = (bf16[2,1024,256]{2,1,0:T(8,128)(2,1)S(1)}, bf16[2,1024,256]{2,1,0:T(8,128)(2,1)S(1)}, u32[]{:S(2)}, u32[]{:S(2)}) collective-permute-start(bf16[2,1024,256]{2,1,0:T(8,128)(2,1)S(1)} %copy-done), channel_id=1, source_target_pairs={{0,1},{1,0},{2,3},{3,2},{4,5},{5,4},{6,7},{7,6},{8,9},{9,8},{10,11... | collective-permute-start | bytes 3145736 | tf_op jit(solution)/shard_map/ppermute | solution.py:47
  18.2 17.9 %collective-permute-start.8 = (bf16[336,1024]{1,0:T(8,128)(2,1)S(1)}, bf16[336,1024]{1,0:T(8,128)(2,1)S(1)}, u32[]{:S(2)}, u32[]{:S(2)}) collective-permute-start(bf16[336,1024]{1,0:T(8,128)(2,1)S(1)} %get-tuple-element.78), channel_id=1, source_target_pairs={{0,2},{2,0},{1,3},{3,1},{4,6},{6,4},{5,7},{7,5},{8,10},{10,8},{9,1... | collective-permute-start | bytes 2064392 | tf_op jit(solution)/shard_map/ppermute | solution.py:47
  20.0 5.7 %collective-permute-start.7 = (bf16[2,512,512]{2,1,0:T(8,128)(2,1)S(1)}, bf16[2,512,512]{2,1,0:T(8,128)(2,1)S(1)}, u32[]{:S(2)}, u32[]{:S(2)}) collective-permute-start(bf16[2,512,512]{2,1,0:T(8,128)(2,1)S(1)} %get-tuple-element.75.refs_6_), channel_id=1, source_target_pairs={{0,1},{1,0},{2,3},{3,2},{4,5},{5,4},{6,7},{7,6},{8,9},{9,8},{10,11... | collective-permute-start | bytes 3145736 | tf_op jit(solution)/shard_map/ppermute | solution.py:47
  20.2 5.5 %collective-permute-start.6 = (bf16[2,208,1024]{2,1,0:T(8,128)(2,1)S(1)}, bf16[2,208,1024]{2,1,0:T(8,128)(2,1)S(1)}, u32[]{:S(2)}, u32[]{:S(2)}) collective-permute-start(bf16[2,208,1024]{2,1,0:T(8,128)(2,1)S(1)} %get-tuple-element.74.refs_7_), channel_id=1, source_target_pairs={{0,1},{1,0},{2,3},{3,2},{4,5},{5,4},{6,7},{7,6},{8,9},{9,8},{10,11... | collective-permute-start | bytes 2555912 | tf_op jit(solution)/shard_map/ppermute | solution.py:47
  21.8 16.0 %collective-permute-start.5 = (bf16[672,256]{1,0:T(8,128)(2,1)S(1)}, bf16[672,256]{1,0:T(8,128)(2,1)S(1)}, u32[]{:S(2)}, u32[]{:S(2)}) collective-permute-start(bf16[672,256]{1,0:T(8,128)(2,1)S(1)} %get-tuple-element.71.refs_3_.refs_6_), channel_id=1, source_target_pairs={{0,4},{4,8},{8,12},{12,0},{1,5},{5,9},{9,13},{13,1},{2,6},{6,10},{... | collective-permute-start | bytes 1032200 | tf_op jit(solution)/shard_map/ppermute | solution.py:47
  23.5 18.9 %collective-permute-start.10 = (bf16[672,256]{1,0:T(8,128)(2,1)S(1)}, bf16[672,256]{1,0:T(8,128)(2,1)S(1)}, u32[]{:S(2)}, u32[]{:S(2)}) collective-permute-start(bf16[672,256]{1,0:T(8,128)(2,1)S(1)} %get-tuple-element.82), channel_id=1, source_target_pairs={{0,12},{4,0},{8,4},{12,8},{1,13},{5,1},{9,5},{13,9},{2,14},{6,2},{... | collective-permute-start | bytes 1032200 | tf_op jit(solution)/shard_map/ppermute | solution.py:47
  25.7 10.4 %collective-permute-start.9 = (bf16[512,256]{1,0:T(8,128)(2,1)S(1)}, bf16[512,256]{1,0:T(8,128)(2,1)S(1)}, u32[]{:S(2)}, u32[]{:S(2)}) collective-permute-start(bf16[512,256]{1,0:T(8,128)(2,1)S(1)} %collective-permute-done.refs_15_), channel_id=1, source_target_pairs={{0,16},{16,0},{1,17},{17,1},{2,18},{18,2},{3,19},{19,3},{4,20},{20... | collective-permute-start | bytes 786440 | tf_op jit(solution)/shard_map/ppermute | solution.py:47
  36.1 12.2 %collective-permute-start.12 = (bf16[336,1024]{1,0:T(8,128)(2,1)S(1)}, bf16[336,1024]{1,0:T(8,128)(2,1)S(1)}, u32[]{:S(2)}, u32[]{:S(2)}) collective-permute-start(bf16[336,1024]{1,0:T(8,128)(2,1)S(1)} %collective-permute-done.8.refs_9_), channel_id=1, source_target_pairs={{0,1},{1,0},{2,3},{3,2},{4,5},{5,4},{6,7},{7,6},{8,9},{9,8},{10,11... | collective-permute-start | bytes 2064392 | tf_op jit(solution)/shard_map/ppermute | solution.py:47
  36.1 17.9 %collective-permute-start.15 = (bf16[336,1024]{1,0:T(8,128)(2,1)S(1)}, bf16[336,1024]{1,0:T(8,128)(2,1)S(1)}, u32[]{:S(2)}, u32[]{:S(2)}) collective-permute-start(bf16[336,1024]{1,0:T(8,128)(2,1)S(1)} %collective-permute-done.8.refs_9_), channel_id=1, source_target_pairs={{0,16},{16,0},{1,17},{17,1},{2,18},{18,2},{3,19},{19,3},{4,20},{20... | collective-permute-start | bytes 2064392 | tf_op jit(solution)/shard_map/ppermute | solution.py:47
  37.9 10.4 %collective-permute-start.11 = (bf16[512,256]{1,0:T(8,128)(2,1)S(1)}, bf16[512,256]{1,0:T(8,128)(2,1)S(1)}, u32[]{:S(2)}, u32[]{:S(2)}) collective-permute-start(bf16[512,256]{1,0:T(8,128)(2,1)S(1)} %slice.3), channel_id=1, source_target_pairs={{0,4},{4,8},{8,12},{12,0},{1,5},{5,9},{9,13},{13,1},{2,6},{6,10},{... | collective-permute-start | bytes 786440 | tf_op jit(solution)/shard_map/ppermute | solution.py:47
  39.5 13.8 %collective-permute-start.16 = (bf16[512,512]{1,0:T(8,128)(2,1)S(1)}, bf16[512,512]{1,0:T(8,128)(2,1)S(1)}, u32[]{:S(2)}, u32[]{:S(2)}) collective-permute-start(bf16[512,512]{1,0:T(8,128)(2,1)S(1)} %get-tuple-element.94), channel_id=1, source_target_pairs={{0,2},{2,0},{1,3},{3,1},{4,6},{6,4},{5,7},{7,5},{8,10},{10,8},{9,1... | collective-permute-start | bytes 1572872 | tf_op jit(solution)/shard_map/ppermute | solution.py:47
  48.2 5.7 %collective-permute-start.13 = (bf16[512,256]{1,0:T(8,128)(2,1)S(1)}, bf16[512,256]{1,0:T(8,128)(2,1)S(1)}, u32[]{:S(2)}, u32[]{:S(2)}) collective-permute-start(bf16[512,256]{1,0:T(8,128)(2,1)S(1)} %collective-permute-done.refs_15_), channel_id=1, source_target_pairs={{0,1},{1,0},{2,3},{3,2},{4,5},{5,4},{6,7},{7,6},{8,9},{9,8},{10,11... | collective-permute-start | bytes 786440 | tf_op jit(solution)/shard_map/ppermute | solution.py:47
  48.3 5.7 %collective-permute-start.14 = (bf16[512,256]{1,0:T(8,128)(2,1)S(1)}, bf16[512,256]{1,0:T(8,128)(2,1)S(1)}, u32[]{:S(2)}, u32[]{:S(2)}) collective-permute-start(bf16[512,256]{1,0:T(8,128)(2,1)S(1)} %collective-permute-done.9.refs_16_), channel_id=1, source_target_pairs={{0,1},{1,0},{2,3},{3,2},{4,5},{5,4},{6,7},{7,6},{8,9},{9,8},{10,11... | collective-permute-start | bytes 786440 | tf_op jit(solution)/shard_map/ppermute | solution.py:47
  54.0 6.2 %collective-permute-start.20 = (bf16[336,1024]{1,0:T(8,128)(2,1)S(1)}, bf16[336,1024]{1,0:T(8,128)(2,1)S(1)}, u32[]{:S(2)}, u32[]{:S(2)}) collective-permute-start(bf16[336,1024]{1,0:T(8,128)(2,1)S(1)} %collective-permute-done.15.refs_10_), channel_id=1, source_target_pairs={{0,1},{1,0},{2,3},{3,2},{4,5},{5,4},{6,7},{7,6},{8,9},{9,8},{10,11... | collective-permute-start | bytes 2064392 | tf_op jit(solution)/shard_map/ppermute | solution.py:47
  54.0 3.7 %collective-permute-start.17 = (bf16[192,128]{1,0:T(8,128)(2,1)S(1)}, bf16[192,128]{1,0:T(8,128)(2,1)S(1)}, u32[]{:S(2)}, u32[]{:S(2)}) collective-permute-start(bf16[192,128]{1,0:T(8,128)(2,1)S(1)} %get-tuple-element.96), channel_id=1, source_target_pairs={{0,1},{1,0},{2,3},{3,2},{4,5},{5,4},{6,7},{7,6},{8,9},{9,8},{10,11... | collective-permute-start | bytes 147464 | tf_op jit(solution)/shard_map/ppermute | solution.py:60
  54.5 4.1 %collective-permute-start.18 = (bf16[192,128]{1,0:T(8,128)(2,1)S(1)}, bf16[192,128]{1,0:T(8,128)(2,1)S(1)}, u32[]{:S(2)}, u32[]{:S(2)}) collective-permute-start(bf16[192,128]{1,0:T(8,128)(2,1)S(1)} %get-tuple-element.97), channel_id=1, source_target_pairs={{0,2},{1,3},{2,0},{3,1},{4,6},{5,7},{6,4},{7,5},{8,10},{9,11},{10,... | collective-permute-start | bytes 147464 | tf_op jit(solution)/shard_map/ppermute | solution.py:60
  56.2 4.0 %collective-permute-start.19 = (bf16[192,128]{1,0:T(8,128)(2,1)S(1)}, bf16[192,128]{1,0:T(8,128)(2,1)S(1)}, u32[]{:S(2)}, u32[]{:S(2)}) collective-permute-start(bf16[192,128]{1,0:T(8,128)(2,1)S(1)} %get-tuple-element.98), channel_id=1, source_target_pairs={{0,3},{1,2},{2,1},{3,0},{4,7},{5,6},{6,5},{7,4},{8,11},{9,10},{10,... | collective-permute-start | bytes 147464 | tf_op jit(solution)/shard_map/ppermute | solution.py:60
  56.2 14.4 %collective-permute-start.21 = (bf16[512,512]{1,0:T(8,128)(2,1)S(1)}, bf16[512,512]{1,0:T(8,128)(2,1)}, u32[]{:S(2)}, u32[]{:S(2)}) collective-permute-start(bf16[512,512]{1,0:T(8,128)(2,1)S(1)} %collective-permute-done.16.refs_8_), channel_id=1, source_target_pairs={{0,16},{16,0},{1,17},{17,1},{2,18},{18,2},{3,19},{19,3},{4,20},{20... | collective-permute-start | bytes 1572872 | tf_op jit(solution)/shard_map/ppermute | solution.py:47
  60.2 11.5 %collective-permute-start.22 = (bf16[512,512]{1,0:T(8,128)(2,1)S(1)}, bf16[512,512]{1,0:T(8,128)(2,1)S(1)}, u32[]{:S(2)}, u32[]{:S(2)}) collective-permute-start(bf16[512,512]{1,0:T(8,128)(2,1)S(1)} %collective-permute-done.16.refs_8_), channel_id=1, source_target_pairs={{0,1},{1,0},{2,3},{3,2},{4,5},{5,4},{6,7},{7,6},{8,9},{9,8},{10,11... | collective-permute-start | bytes 1572872 | tf_op jit(solution)/shard_map/ppermute | solution.py:47
  60.4 11.3 %collective-permute-start.23 = (bf16[2,192,512]{2,1,0:T(8,128)(2,1)S(1)}, bf16[2,192,512]{2,1,0:T(8,128)(2,1)S(1)}, u32[]{:S(2)}, u32[]{:S(2)}) collective-permute-start(bf16[2,192,512]{2,1,0:T(8,128)(2,1)S(1)} %get-tuple-element.115.refs_12_), channel_id=1, source_target_pairs={{0,2},{2,0},{1,3},{3,1},{4,6},{6,4},{5,7},{7,5},{8,10},{10,8},{9,1... | collective-permute-start | bytes 1179656 | tf_op jit(solution)/shard_map/ppermute | solution.py:47
  60.9 10.8 %collective-permute-start.24 = (bf16[2,192,512]{2,1,0:T(8,128)(2,1)S(1)}, bf16[2,192,512]{2,1,0:T(8,128)(2,1)S(1)}, u32[]{:S(2)}, u32[]{:S(2)}) collective-permute-start(bf16[2,192,512]{2,1,0:T(8,128)(2,1)S(1)} %get-tuple-element.115.refs_12_), channel_id=1, source_target_pairs={{0,1},{1,0},{2,3},{3,2},{4,5},{5,4},{6,7},{7,6},{8,9},{9,8},{10,11... | collective-permute-start | bytes 1179656 | tf_op jit(solution)/shard_map/ppermute | solution.py:47
  (27 other events, 194.6 us)
